TPU v7x, 256 devices: a whole 4x4x8 slice. The times are simulated.
256 devices in a mesh: row: 4 (over z_hi), col: 64 (over y, x, z_lo, core).
Axes of the slice: x: 4, y: 4, z: 8 (z_hi: 4, z_lo: 2; z = z_hi * 2 + z_lo), core: 2. Of those that a mesh axis runs over, the one named last changes fastest.
Arguments:
- grm_tiles: bfloat16 [1024, 1024, 1024], P(('row', 'col')), as said below
- tile_row: int32 [1024], P(('row', 'col')), may hold values from 0 to 7, as said below
- tile_col: int32 [1024], P(('row', 'col')), may hold values from -1 to 127, as said below
- panel: bfloat16 [131072, 128], P('col'), may hold values from -6 to 6
Outputs:
- y_rows: float32 [8192, 128], P(('row', 'col'))
- y_cols: float32 [131072, 128], P('col')
Inputs may be any that keep to these rules, and one draw needn't show every extreme that they name: The slots of the device with index r on row and c on col hold slab row tiles r * 2 to r * 2 + 1 and column tiles c * 2 to c * 2 + 1; every pair of these with column tile <= 120 + row tile stands in exactly one of that device's slots, in an order drawn from the seed; in the other slots tile_col is -1 and tile_row still names a row tile of the device. `tile_col`: as for tile_row. `grm_tiles`: entries of a diagonal tile above its diagonal are not used.
All inputs are finite; a program needn't handle non-finite values.
Results may differ from a plain program's by a relative error of at most 0.0003.
Values may be sent and summed in bfloat16 or wider, within the bound.
No kernel may reach another device: no remote copies, remote signals or barrier semaphores. Data moves between devices by JAX's collectives and lax.ppermute only.
A program may use at most 64 MiB of HBM per device.

v0:
```python
import jax
import jax.numpy as jnp
from jax import lax
from jax.sharding import PartitionSpec as P

RT_DEV = 2
CTD = 2


def from_root(block, axis, owner):
    block = jnp.where(lax.axis_index(axis) == owner, block, jnp.zeros_like(block))
    return lax.psum(block, axis)


def plain_product(tile, source):
    return jnp.dot(tile, source, preferred_element_type=jnp.float32)


def diagonal_product(tile, source):
    size = tile.shape[0]
    row_ids = lax.broadcasted_iota(jnp.int32, (size, size), 0)
    col_ids = lax.broadcasted_iota(jnp.int32, (size, size), 1)
    zeros_tile = jnp.zeros_like(tile)
    lower_part = jnp.where(row_ids >= col_ids, tile, zeros_tile)
    strict_part = jnp.where(row_ids > col_ids, tile, zeros_tile)
    first = jnp.dot(lower_part, source, preferred_element_type=jnp.float32)
    second = lax.dot_general(
        strict_part, source, (((0,), (0,)), ((), ())), preferred_element_type=jnp.float32
    )
    return first + second


def row_products(grm_tiles, tile_row, tile_col, panel, base_row, base_col, offset):
    width = grm_tiles.shape[1]
    depth = panel.shape[1]
    total = jnp.zeros((RT_DEV * width, depth), jnp.float32)
    for slot in range(grm_tiles.shape[0]):
        row_tile = tile_row[slot]
        col_tile = tile_col[slot]
        present = col_tile >= 0
        local_col = jnp.maximum(col_tile - base_col, 0)
        local_row = row_tile - base_row
        source = lax.dynamic_slice_in_dim(panel, local_col * width, width, 0)
        product = lax.cond(
            col_tile == offset + row_tile, diagonal_product, plain_product, grm_tiles[slot], source
        )
        product = jnp.where(present, product, jnp.zeros_like(product))
        current = lax.dynamic_slice_in_dim(total, local_row * width, width, 0)
        total = lax.dynamic_update_slice_in_dim(total, current + product, local_row * width, 0)
    return total


def column_products(grm_tiles, tile_row, tile_col, slab, base_row, base_col, offset):
    width = grm_tiles.shape[1]
    depth = slab.shape[1]
    total = jnp.zeros((CTD * width, depth), jnp.float32)
    for slot in range(grm_tiles.shape[0]):
        row_tile = tile_row[slot]
        col_tile = tile_col[slot]
        keep = jnp.logical_and(col_tile >= 0, col_tile < offset + row_tile)
        local_col = jnp.maximum(col_tile - base_col, 0)
        local_row = row_tile - base_row
        source = lax.dynamic_slice_in_dim(slab, local_row * width, width, 0)
        mirror = lax.dot_general(
            grm_tiles[slot], source, (((0,), (0,)), ((), ())), preferred_element_type=jnp.float32
        )
        mirror = jnp.where(keep, mirror, jnp.zeros_like(mirror))
        current = lax.dynamic_slice_in_dim(total, local_col * width, width, 0)
        total = lax.dynamic_update_slice_in_dim(total, current + mirror, local_col * width, 0)
    return total


def rows_reduce(partial_value, col_index, col_count):
    total = lax.psum(partial_value, "col")
    share = partial_value.shape[0] // col_count
    return lax.dynamic_slice_in_dim(total, col_index * share, share, 0)


def on_device(grm_tiles, tile_row, tile_col, panel):
    row_index = lax.axis_index("row")
    col_index = lax.axis_index("col")
    col_count = lax.axis_size("col")
    row_count = lax.axis_size("row")
    offset = CTD * col_count - RT_DEV * row_count
    base_row = row_index * RT_DEV
    base_col = col_index * CTD
    first_slab = offset + base_row
    owner = first_slab // CTD
    slab = from_root(panel, "col", owner)
    row_part = row_products(grm_tiles, tile_row, tile_col, panel, base_row, base_col, offset)
    col_part = column_products(grm_tiles, tile_row, tile_col, slab, base_row, base_col, offset)
    y_rows = rows_reduce(row_part, col_index, col_count)
    y_cols = lax.psum(col_part, "row")
    return (y_rows, y_cols)


def solution(mesh):
    in_specs = (P(("row", "col"), None, None), P(("row", "col")), P(("row", "col")), P("col", None))
    out_specs = (P(("row", "col"), None), P("col", None))
    return jax.shard_map(
        on_device, mesh=mesh, in_specs=in_specs, out_specs=out_specs, check_vma=False
    )
```

profile of v0, /device:TPU:6, one launch (start us, length us, event | category | flops | bytes accessed | tf_op | source)
XLA Modules:
  0.0 1194.2 jit_solution(10176638371403068245)
XLA Ops:
  8.1 1.5 fusion.100
  11.0 1.5 fusion.99
  16.3 5.7 slice_bitcast_fusion
  23.3 2.4 conditional.4
  23.3 2.4 fusion
  26.5 3.2 conditional.5
  26.5 3.2 fusion.20
  29.8 1.1 select_dynamic-update-slice_fusion
  30.9 1.2 add_dynamic-update-slice_fusion.2
  38.5 3.2 conditional.6
  38.5 3.2 fusion.40
  41.8 2.6 conditional.7
  41.8 2.6 fusion.60
  44.3 1.1 add_dynamic-update-slice_fusion.1
  45.5 1.2 add_dynamic-update-slice_fusion
  50.3 485.7 %all-reduce.6.cloned.1.call-done = bf16[2048,128]{1,0:T(8,128)(2,1)} async-done(((bf16[2048,128]{1,0:T(8,128)(2,1)}), bf16[2048,128]{1,0:T(8,128)(2,1)}) %all-reduce.6.cloned.1.call-update) | async-done | bytes 524304 | tf_op jit(solution)/shard_map/psum | solution.py:12
  536.0 2.2 fusion.81
  538.3 2.1 fusion.84
  540.3 2.1 fusion.87
  542.4 2.1 fusion.90
  544.5 1.0 copy-done
  545.5 544.7 %all-reduce.4.cloned.1.call-done = f32[2048,128]{0,1:T(8,128)} async-done(((f32[2048,128]{0,1:T(8,128)}), f32[2048,128]{0,1:T(8,128)}) %all-reduce.4.cloned.1.call-update) | async-done | bytes 1048592 | tf_op jit(solution)/shard_map/psum | solution.py:74
  1091.8 93.3 %all-reduce.8.cloned.1.call-done = f32[2048,128]{0,1:T(8,128)} async-done(((f32[2048,128]{0,1:T(8,128)}), f32[2048,128]{0,1:T(8,128)}) %all-reduce.8.cloned.1.call-update) | async-done | bytes 1048592 | tf_op jit(solution)/shard_map/psum | solution.py:93
  1185.1 2.5 copy.11
  (20 shorter events, 4.5 us)
Async XLA Ops:
  7.2 528.8 %all-reduce.6.cloned.1.call-start = ((), (), s32[]{:S(2)}) async-start(), calls=%async_computation.1 | async-start | bytes 1048576 | tf_op jit(solution)/shard_map/psum | solution.py:12
  8.1 1082.1 %all-reduce.4.cloned.1.call-start = ((), (), s32[]{:S(2)}) async-start(), calls=%async_computation | async-start | bytes 2097152 | tf_op jit(solution)/shard_map/psum | solution.py:74
  16.3 7.0 copy-start.5
  25.7 0.8 copy-start.8
  46.6 1.0 copy-start.1
  47.6 1137.5 %all-reduce.8.cloned.1.call-start = ((), (), s32[]{:S(2)}) async-start(), calls=%async_computation.2 | async-start | bytes 2097152 | tf_op jit(solution)/shard_map/psum | solution.py:93
  535.9 2.3 copy-start.9
  544.5 1.0 copy-start
Sparse Core Ops, SparseCore 0:
  10.6 525.2 all-reduce.5
  539.3 550.8 all-reduce.3
  1092.9 92.1 all-reduce.7
where the time goes:
time: 1200 us; the launch traced here: 1190 us
  waiting for transfers between devices  1120 us (93%)
  between operations  29.3 us (2%)
  matrix products  19.9 us (2%)
  local copies, waits for them, and re-layouts  15.7 us (1%)
    psum x1, waiting for transfers between devices, rows_reduce(): total = lax.psum(partial_value, 'col')  545 us
    psum x1, waiting for transfers between devices, from_root(): return lax.psum(block, axis)  486 us
    psum x1, waiting for transfers between devices, on_device(): y_cols = lax.psum(col_part, 'row')  93.3 us
  transfers between devices with their start and end apart: 3, of which 3 were waited for; matrix products, arithmetic and copies ran while one was open for 3% of the time, Pallas kernels for 0%

commit v1 on v0

v1 whole, which is shorter than its diff:
```python
import functools

import jax
import jax.numpy as jnp
from jax import lax
from jax.experimental import pallas as pl
from jax.experimental.pallas import tpu as pltpu
from jax.sharding import PartitionSpec as P

RT_DEV = 2
CTD = 2
STEPS = 2
MIB = 1024 * 1024
PAD = 16
SITES = 16
PLANES = 4
LINE = 4
BF16_MOST = 3.3895313892515355e38


def site_at(place):
    return place % LINE * LINE + place // LINE


def place_of(info, index, depth, width):
    slot = index // STEPS
    part = index % STEPS
    local_row = info[0, slot]
    local_col = info[1, slot]
    first = pl.multiple_of(local_row * width + part * depth, depth)
    rows = pl.ds(first, depth)
    cols = pl.ds(pl.multiple_of(local_col * width, width), width)
    piece = pl.ds(pl.multiple_of(part * depth, depth), depth)
    return slot, part, rows, cols, piece


def fetch_of(info, tiles_ref, held, sems):
    slots, width, _ = held.shape
    depth = width // STEPS

    def fetch(index):
        slot, part, rows, cols, piece = place_of(info, index, depth, width)
        return pltpu.make_async_copy(
            tiles_ref.at[slot, piece], held.at[slot, piece], sems.at[index]
        )

    return fetch


def row_kernel(info, tiles_ref, panel_ref, keep_ref, send_ref, total, held, sems):
    slots, width, _ = held.shape
    depth = width // STEPS
    fetch = fetch_of(info, tiles_ref, held, sems)
    for index in range(slots * STEPS):
        fetch(index).start()
    total[...] = jnp.zeros_like(total)

    @pl.loop(0, slots * STEPS)
    def _(index):
        slot, part, rows, cols, piece = place_of(info, index, depth, width)
        kind = info[2, slot]
        fetch(index).wait()

        @pl.when(kind == 1)
        def _():
            total[rows, :] += jnp.dot(
                held[slot, piece, :], panel_ref[cols, :], preferred_element_type=jnp.float32
            )

        @pl.when(kind == 2)
        def _():
            row_ids = lax.broadcasted_iota(jnp.int32, (depth, width), 0) + part * depth
            col_ids = lax.broadcasted_iota(jnp.int32, (depth, width), 1)
            tile = held[slot, piece, :].astype(jnp.float32)
            lower = jnp.where(row_ids >= col_ids, tile, 0.0).astype(jnp.bfloat16)
            strict = jnp.where(row_ids > col_ids, tile, 0.0).astype(jnp.bfloat16)
            total[rows, :] += jnp.dot(lower, panel_ref[cols, :], preferred_element_type=jnp.float32)
            own = pl.ds(pl.multiple_of(info[1, slot] * width + part * depth, depth), depth)
            whole = pl.ds(pl.multiple_of(info[0, slot] * width, width), width)
            total[whole, :] += lax.dot_general(
                panel_ref[own, :], strict, (((0,), (0,)), ((), ())),
                preferred_element_type=jnp.float32,
            ).T

    core = info[4, 0]
    depth_z = info[4, 1]
    share = total.shape[0] // (SITES * PLANES)
    for ref, which in ((keep_ref, core), (send_ref, 1 - core)):
        for step, chip in enumerate((depth_z, 1 - depth_z)):
            for place in range(SITES):
                site = site_at(place)
                source = pl.multiple_of((site * PLANES + chip * 2 + which) * share, share)
                target = (step * SITES + place) * share
                ref[target : target + share, :] = total[pl.ds(source, share), :]


def add_kernel(keep_ref, got_ref, mine_ref, send_ref):
    size = mine_ref.shape[0]
    mine_ref[...] = keep_ref[:size, :] + got_ref[:size, :]
    encode(keep_ref[size:, :] + got_ref[size:, :], send_ref)


def sum_of(refs):
    total = refs[0][...].astype(jnp.float32)
    for ref in refs[1:]:
        total += ref[...].astype(jnp.float32)
    return total.astype(refs[0].dtype)


def strip_kernel(home, bits, panel_ref, got1_ref, got2_ref, got3_ref, after_ref, *out_refs):
    del after_ref
    rows = got1_ref.shape[0]
    own = panel_ref[home * rows : (home + 1) * rows, :].astype(jnp.float32)
    own = jnp.where(bits[4] == 1, own, 0.0)
    rest = got1_ref[...].astype(jnp.float32) + got2_ref[...].astype(jnp.float32)
    strip = (own + rest + got3_ref[...].astype(jnp.float32)).astype(jnp.bfloat16)
    size = rows // LINE
    for index, out_ref in enumerate(out_refs):
        out_ref[...] = strip[index * size : (index + 1) * size]


def sum_kernel(*refs):
    refs[-1][...] = sum_of(refs[:-1])


def pack_kernel(mine_ref, got_ref, piece_ref, got1_ref, got2_ref, got3_ref, out_ref):
    sites = out_ref.shape[0]
    size = piece_ref.shape[0]
    share = mine_ref.shape[0] // sites
    piece = sum_of((piece_ref, got1_ref, got2_ref, got3_ref))
    sums = mine_ref[...] + decode(got_ref)
    high = jnp.clip(sums, -BF16_MOST, BF16_MOST).astype(jnp.bfloat16)
    low = (sums - high.astype(jnp.float32)).astype(jnp.bfloat16)
    for site in range(sites):
        out_ref[site, :size, :] = piece
        out_ref[site, size : size + share, :] = high[site * share : (site + 1) * share]
        out_ref[site, size + share :, :] = low[site * share : (site + 1) * share]


def block_rows(size):
    return min(128, size)


def encode(value, out_ref):
    size = value.shape[0]
    block = block_rows(size)
    lanes = value.shape[1]
    powers = []
    for start in range(0, size, block):
        part = value[start : start + block]
        most = jnp.max(jnp.abs(part), axis=0, keepdims=True)
        power = 15.0 - jnp.maximum(jnp.ceil(jnp.log2(most)), -126.0)
        half = jnp.floor(power * 0.5)
        scaled = part * jnp.exp2(half) * jnp.exp2(power - half)
        whole = jnp.clip(jnp.round(scaled), -32767.0, 32767.0)
        out_ref[start : start + block, :] = whole.astype(jnp.int32).astype(jnp.int16)
        powers.append(power)
    powers.append(jnp.zeros((PAD - len(powers), lanes), jnp.float32))
    tail = jnp.concatenate(powers, axis=0)
    out_ref[size:, :] = tail.astype(jnp.int32).astype(jnp.int16)


def decode(ref):
    size = ref.shape[0] - PAD
    block = block_rows(size)
    tail = ref[size:, :].astype(jnp.int32).astype(jnp.float32)
    parts = []
    for index in range(size // block):
        power = tail[index : index + 1]
        half = jnp.floor(power * 0.5)
        part = ref[index * block : (index + 1) * block, :].astype(jnp.int32).astype(jnp.float32)
        parts.append(part * jnp.exp2(-half) * jnp.exp2(half - power))
    return jnp.concatenate(parts, axis=0)


def col_kernel(
    info, tiles_ref, slab_ref, rows_ref, keep_ref, send0_ref, send1_ref, total, result, held, sems
):
    slots, width, _ = held.shape
    depth = width // STEPS
    size, share = slab_ref.shape[1], rows_ref.shape[0]
    size = size - 2 * share
    count = depth // size
    fetch = fetch_of(info, tiles_ref, held, sems)
    for index in range(slots * STEPS):
        fetch(index).start()
    total[...] = jnp.zeros_like(total)
    sums = jnp.zeros(rows_ref.shape, jnp.float32)
    for site in range(slab_ref.shape[0]):
        sums += slab_ref[site, size : size + share, :].astype(jnp.float32)
        sums += slab_ref[site, size + share :, :].astype(jnp.float32)
    rows_ref[...] = sums

    @pl.loop(0, slots * STEPS)
    def _(index):
        slot, part, rows, cols, piece = place_of(info, index, depth, width)
        fetch(index).wait()

        @pl.when(info[2, slot] == 1)
        def _():
            first = (info[0, slot] * STEPS + part) * count
            source = slab_ref[pl.ds(first, count), :size, :].reshape(depth, slab_ref.shape[2])
            total[:, cols] += lax.dot_general(
                source, held[slot, piece, :], (((0,), (0,)), ((), ())),
                preferred_element_type=jnp.float32,
            )

    result[...] = total[...].T
    half = width // 2
    for index, send_ref in enumerate((send0_ref, send1_ref)):
        bit = info[3, index]
        mine = pl.multiple_of(index * width + bit * half, half)
        other = pl.multiple_of(index * width + (1 - bit) * half, half)
        keep_ref[index] = result[pl.ds(mine, half), :]
        encode(result[pl.ds(other, half), :], send_ref)


def first_kernel(index, keep_ref, got_ref, out_ref):
    encode(keep_ref[index] + decode(got_ref), out_ref)


def second_kernel(own_ref, got_ref, out_ref):
    encode(decode(own_ref) + decode(got_ref), out_ref)


def place_kernel(index, bits, own_ref, got_ref, *refs):
    out_ref, held, sem = refs[-3:]
    size = own_ref.shape[0] - PAD
    mine = pl.multiple_of(bits[index] * size, size)
    other = pl.multiple_of((1 - bits[index]) * size, size)
    held[pl.ds(mine, size), :] = decode(own_ref)
    held[pl.ds(other, size), :] = decode(got_ref)
    copy = pltpu.make_async_copy(held, out_ref.at[pl.ds(index * 2 * size, 2 * size)], sem)
    copy.start()
    copy.wait()


VMEM = pl.BlockSpec(memory_space=pltpu.VMEM)
SMEM = pl.BlockSpec(memory_space=pltpu.SMEM)
HBM = pl.BlockSpec(memory_space=pltpu.HBM)
ANY = pl.BlockSpec(memory_space=pl.ANY)


def limit(size):
    return pltpu.CompilerParams(vmem_limit_bytes=size * MIB)


def small_call(kernel, outs, *args, scalars=0, after=None):
    specs = [SMEM] * scalars + [VMEM] * (len(args) - scalars)
    if after is not None:
        specs, args = specs + [ANY], args + (after,)
    return pl.pallas_call(
        kernel, in_specs=specs, out_specs=[VMEM] * len(outs), out_shape=outs, compiler_params=limit(6)
    )(*args)


def place_half(index, bits, own, got, result):
    size, lanes = own.shape[0] - PAD, own.shape[1]
    args = (bits, own, got) + (() if result is None else (result,))
    return pl.pallas_call(
        functools.partial(place_kernel, index),
        in_specs=[SMEM, VMEM, VMEM] + [HBM] * (len(args) - 3),
        out_specs=HBM,
        out_shape=floats(4 * size, lanes),
        scratch_shapes=[pltpu.VMEM((2 * size, lanes), jnp.float32), pltpu.SemaphoreType.DMA],
        input_output_aliases={} if result is None else {3: 0},
        compiler_params=limit(6),
    )(*args)


def tile_cost(shape, lanes):
    slots, width, _ = shape
    return pl.CostEstimate(
        flops=2 * slots * width * width * lanes,
        bytes_accessed=2 * slots * width * width + 2 * MIB,
        transcendentals=0,
    )


def floats(*shape):
    return jax.ShapeDtypeStruct(shape, jnp.float32)


def coded(size, lanes):
    return jax.ShapeDtypeStruct((size + PAD, lanes), jnp.int16)


def tile_scratch(grm_tiles):
    return [
        pltpu.VMEM(grm_tiles.shape, grm_tiles.dtype),
        pltpu.SemaphoreType.DMA((grm_tiles.shape[0] * STEPS,)),
    ]


def row_products(info, grm_tiles, panel):
    slots, width, _ = grm_tiles.shape
    lanes = panel.shape[1]
    rows = RT_DEV * width
    return pl.pallas_call(
        row_kernel,
        in_specs=[SMEM, HBM, VMEM],
        out_specs=[VMEM, VMEM],
        out_shape=[floats(rows // 2, lanes), floats(rows // 2, lanes)],
        scratch_shapes=[pltpu.VMEM((rows, lanes), jnp.float32)] + tile_scratch(grm_tiles),
        compiler_params=limit(24),
        cost_estimate=tile_cost(grm_tiles.shape, lanes),
    )(info, grm_tiles, panel)


def col_products(info, grm_tiles, packed, share):
    slots, width, _ = grm_tiles.shape
    lanes = packed.shape[2]
    half = width // 2
    return pl.pallas_call(
        col_kernel,
        in_specs=[SMEM, HBM, VMEM],
        out_specs=[VMEM] * 4,
        out_shape=[floats(share, lanes), floats(2, half, lanes), coded(half, lanes), coded(half, lanes)],
        scratch_shapes=[
            pltpu.VMEM((lanes, CTD * width), jnp.float32),
            pltpu.VMEM((CTD * width, lanes), jnp.float32),
        ]
        + tile_scratch(grm_tiles),
        compiler_params=limit(24),
        cost_estimate=tile_cost(grm_tiles.shape, lanes),
    )(info, grm_tiles, packed)


def swap(value, axis, flip):
    return lax.ppermute(value, axis, [(k, k ^ flip) for k in range(lax.axis_size(axis))])


def sum_over_row(bits, keep, sends):
    size, lanes = keep.shape[1:]
    outs = [coded(size, lanes)]
    flips = [(1, 3, 1), (3, 1, 3)]
    gots = [swap(send, "row", flip[0]) for send, flip in zip(sends, flips)]
    owns = [
        small_call(functools.partial(first_kernel, index), outs, keep, got)[0]
        for index, got in enumerate(gots)
    ]
    gots = [swap(own, "row", flip[1]) for own, flip in zip(owns, flips)]
    owns = [small_call(second_kernel, outs, own, got)[0] for own, got in zip(owns, gots)]
    gots = [swap(own, "row", flip[2]) for own, flip in zip(owns, flips)]
    result = None
    for index in range(2):
        result = place_half(index, bits, owns[index], gots[index], result)
    return result


def permute(value, pairs):
    return lax.ppermute(value, ("row", "col"), pairs)


def send_pieces(bits, panel, owners, after):
    lanes = panel.shape[1]
    rows = panel.shape[0] // LINE
    planes = [owner % PLANES for owner in owners]
    home_y, home_x = divmod(owners[0] // PLANES, LINE)

    def device(row, y, x, plane):
        return ((row * LINE + y) * LINE + x) * PLANES + plane

    got = [
        permute(
            panel[x * rows : (x + 1) * rows],
            [(device(r, home_y, home_x, p), device(r, home_y, x, p)) for r, p in enumerate(planes)],
        )
        for x in range(LINE)
        if x != home_x
    ]
    shape = jax.ShapeDtypeStruct((rows // LINE, lanes), panel.dtype)
    pieces = small_call(
        functools.partial(strip_kernel, home_x), [shape] * LINE, bits, panel, *got,
        scalars=1, after=after,
    )
    got = [
        permute(
            pieces[y],
            [
                (device(r, home_y, x, p), device(r, y, x, p))
                for r, p in enumerate(planes)
                for x in range(LINE)
            ],
        )
        for y in range(LINE)
        if y != home_y
    ]
    piece = small_call(sum_kernel, [shape], pieces[home_y], *got)[0]
    got = [
        permute(
            piece,
            [
                (device(r, y, x, p), device(r, y, x, (p + step) % PLANES))
                for r, p in enumerate(planes)
                for y in range(LINE)
                for x in range(LINE)
            ],
        )
        for step in range(1, PLANES)
    ]
    return [piece, *got]


def on_device(grm_tiles, tile_row, tile_col, panel):
    row_index = lax.axis_index("row")
    col_index = lax.axis_index("col")
    col_count = lax.axis_size("col")
    row_count = lax.axis_size("row")
    lanes = panel.shape[1]
    offset = CTD * col_count - RT_DEV * row_count
    base_row = row_index * RT_DEV
    base_col = col_index * CTD
    owners = [(offset + row * RT_DEV) // CTD for row in range(row_count)]

    local_row = tile_row - base_row
    local_col = jnp.maximum(tile_col - base_col, 0)
    kind = jnp.where(tile_col < 0, 0, jnp.where(tile_col == offset + tile_row, 2, 1))
    high = row_index // 2
    low = (row_index + high) % 2
    core = col_index % 2
    chip = col_index // 2 % 2
    root = (col_index == (offset + base_row) // CTD).astype(jnp.int32)
    bits = jnp.stack([low, high, core, chip, root]).astype(jnp.int32)
    info = jnp.stack(
        [local_row, local_col, kind, jnp.pad(bits[:2], (0, 2)), jnp.pad(bits[2:4], (0, 2))]
    ).astype(jnp.int32)

    across = [[site_at(place) * PLANES + plane for place in range(SITES)] for plane in range(PLANES)]
    tiles = pltpu.with_memory_space_constraint(grm_tiles, pltpu.HBM)
    keep, send = row_products(info, tiles, panel)
    half = keep.shape[0] // 2
    share = half // SITES
    mine, send_z = small_call(
        add_kernel, [floats(half, lanes), coded(half, lanes)], keep, swap(send, "col", 1)
    )
    pieces = send_pieces(bits, panel, owners, keep)
    size = pieces[0].shape[0]
    packed = small_call(
        pack_kernel,
        [jax.ShapeDtypeStruct((SITES, size + 2 * share, lanes), jnp.bfloat16)],
        mine, swap(send_z, "col", 2), *pieces,
    )[0]
    packed = lax.all_to_all(packed, "col", 0, 0, axis_index_groups=across)
    y_rows, keep, *sends = col_products(info, tiles, packed, share)
    y_cols = sum_over_row(bits, keep, sends)
    return (y_rows, y_cols)


def solution(mesh):
    in_specs = (P(("row", "col"), None, None), P(("row", "col")), P(("row", "col")), P("col", None))
    out_specs = (P(("row", "col"), None), P("col", None))
    return jax.shard_map(
        on_device, mesh=mesh, in_specs=in_specs, out_specs=out_specs, check_vma=False
    )
```

time: 1200 us -> 89.1 us (0.07)
  waiting for transfers between devices: 1120 us -> 17.2 us
  starting transfers between devices: 0.12 us -> 30.4 us
  between operations: 29.3 us -> 0.89 us
  blocking collectives: 0 us -> 21.3 us
  matrix products: 19.9 us -> 0 us
  Pallas kernels: 0 us -> 15.8 us
  local copies, waits for them, and re-layouts: 15.7 us -> 1.18 us
    psum x3 -> x0, waiting for transfers between devices: 1120 us -> none  [the longest x1 545 us: rows_reduce(): total = lax.psum(partial_value, 'col')]
    ppermute x0 -> x17, starting transfers between devices: none -> 30.4 us  [the longest x8 21.9 us: swap(): lax.ppermute(value, axis, [(k, k ^ flip) for k in range(lax.axis_size(axi...]
    all_to_all x0 -> x1, blocking collectives: none -> 21.3 us  [on_device(): packed = lax.all_to_all(packed, 'col', 0, 0, axis_index_groups=across)]
    ppermute x0 -> x17, waiting for transfers between devices: none -> 17.2 us  [the longest x8 9.27 us: swap(): lax.ppermute(value, axis, [(k, k ^ flip) for k in range(lax.axis_size(axi...]
    pallas_call x0 -> x12, Pallas kernels: none -> 15.8 us  [the longest x1 5.8 us: col_products(): pl.pallas_call(col_kernel, in_specs=[SMEM, HBM, VMEM], out_specs=[VMEM] *...]
  transfers between devices with their start and end apart: 3 -> 17, of which waited for: 3 -> 9; matrix products, arithmetic and copies ran while one was open for 3% -> 0% of each run, Pallas kernels for 0% -> 3%
where the time goes in v1:
time: 89.1 us; the launch traced here: 87.6 us
  starting transfers between devices  30.4 us (34%)
  blocking collectives  21.3 us (24%)
  waiting for transfers between devices  17.2 us (19%)
  Pallas kernels  15.8 us (18%)
  local copies, waits for them, and re-layouts  1.18 us (1%)
    ppermute x8, starting transfers between devices, swap(): lax.ppermute(value, axis, [(k, k ^ flip) for k in range(lax.axis_size(axi...  21.9 us
    all_to_all x1, blocking collectives, on_device(): packed = lax.all_to_all(packed, 'col', 0, 0, axis_index_groups=across)  21.3 us
    ppermute x8, waiting for transfers between devices, swap(): lax.ppermute(value, axis, [(k, k ^ flip) for k in range(lax.axis_size(axi...  9.27 us
    ppermute x9, starting transfers between devices, permute(): return lax.ppermute(value, ('row', 'col'), pairs)  8.5 us
    ppermute x9, waiting for transfers between devices, permute(): return lax.ppermute(value, ('row', 'col'), pairs)  7.94 us
    pallas_call x1, Pallas kernels, col_products(): pl.pallas_call(col_kernel, in_specs=[SMEM, HBM, VMEM], out_specs=[VMEM] *...  5.8 us
    pallas_call x1, Pallas kernels, row_products(): pl.pallas_call(row_kernel, in_specs=[SMEM, HBM, VMEM], out_specs=[VMEM, V...  5.65 us
    pallas_call x2, Pallas kernels, place_half(): pl.pallas_call(functools.partial(place_kernel, index), in_specs=[SMEM, VM...  2.83 us
  transfers between devices with their start and end apart: 17, of which 9 were waited for; matrix products, arithmetic and copies ran while one was open for 0% of the time, Pallas kernels for 3%

profile of v1, /device:TPU:6, one launch (start us, length us, event | category | flops | bytes accessed | tf_op | source)
XLA Modules:
  0.0 87.6 jit_solution(7518352858468306793)
XLA Ops:
  0.8 0.7 fusion
  1.6 1.0 %copy-done = bf16[2048,128]{1,0:T(8,128)(2,1)S(1)} copy-done((bf16[2048,128]{1,0:T(8,128)(2,1)S(1)}, bf16[2048,128]{1,0:T(8,128)(2,1)}, u32[]{:S(2)}) %copy-start) | copy-done | bytes 524312
  2.6 5.7 %shard_map.59 = (f32[1024,128]{1,0:T(8,128)S(1)}, f32[1024,128]{1,0:T(8,128)S(1)}) custom-call(s32[5,4]{1,0:T(8,128)S(1)} %stack.54.info, bf16[4,1024,1024]{2,1,0:T(8,128)(2,1)} %tiles_ref.3, bf16[2048,128]{1,0:T(8,128)(2,1)S(1)} %copy-done), custom_call_target="tpu_custom_call" | custom-call | flops 1073741824 | bytes 10485760 | tf_op jit(solution)/shard_map/pallas_call | solution.py:299
  8.4 0.7 collective-permute-start.4
  9.1 0.7 collective-permute-start.3
  9.7 0.7 collective-permute-start.2
  10.6 2.0 %collective-permute-start.1 = (s16[528,128]{1,0:T(8,128)(2,1)S(1)}, s16[528,128]{1,0:T(8,128)(2,1)S(1)}, u32[]{:S(2)}, u32[]{:S(2)}) collective-permute-start(s16[528,128]{1,0:T(8,128)(2,1)S(1)} %get-tuple-element.17), channel_id=1, source_target_pairs={{0,2},{1,3},{2,0},{3,1},{4,6},{5,7},{6,4},{7,5},{8,10},{9,11},{10,... | collective-permute-start | bytes 405512 | tf_op jit(solution)/shard_map/ppermute | solution.py:330
  13.3 1.3 %collective-permute-start.5 = (bf16[128,128]{1,0:T(8,128)(2,1)S(1)}, bf16[128,128]{1,0:T(8,128)(2,1)S(1)}, u32[]{:S(2)}, u32[]{:S(2)}) collective-permute-start(bf16[128,128]{1,0:T(8,128)(2,1)S(1)} %get-tuple-element.19), channel_id=1, source_target_pairs={{48,0},{52,4},{56,8},{60,12},{113,65},{117,69},{121,73},{125,77},{... | collective-permute-start | bytes 98312 | tf_op jit(solution)/shard_map/ppermute | solution.py:352
  16.0 7.1 %collective-permute-done.5.refs_1_ = bf16[128,128]{1,0:T(8,128)(2,1)S(1)} collective-permute-done((bf16[128,128]{1,0:T(8,128)(2,1)S(1)}, bf16[128,128]{1,0:T(8,128)(2,1)S(1)}, u32[]{:S(2)}, u32[]{:S(2)}) %collective-permute-start.5) | collective-permute-done | bytes 32800 | tf_op jit(solution)/shard_map/ppermute | solution.py:352
  23.1 1.3 %collective-permute-start.10 = (bf16[128,128]{1,0:T(8,128)(2,1)S(1)}, bf16[128,128]{1,0:T(8,128)(2,1)S(1)}, u32[]{:S(2)}, u32[]{:S(2)}) collective-permute-start(bf16[128,128]{1,0:T(8,128)(2,1)S(1)} %shard_map.62.piece_ref), channel_id=1, source_target_pairs={{0,3},{4,7},{8,11},{12,15},{16,19},{20,23},{24,27},{28,31},{32,35}... | collective-permute-start | bytes 98312 | tf_op jit(solution)/shard_map/ppermute | solution.py:352
  24.4 1.3 %collective-permute-start.9 = (bf16[128,128]{1,0:T(8,128)(2,1)S(1)}, bf16[128,128]{1,0:T(8,128)(2,1)S(1)}, u32[]{:S(2)}, u32[]{:S(2)}) collective-permute-start(bf16[128,128]{1,0:T(8,128)(2,1)S(1)} %shard_map.62.piece_ref), channel_id=1, source_target_pairs={{0,2},{4,6},{8,10},{12,14},{16,18},{20,22},{24,26},{28,30},{32,34}... | collective-permute-start | bytes 98312 | tf_op jit(solution)/shard_map/ppermute | solution.py:352
  25.7 1.3 %collective-permute-start.8 = (bf16[128,128]{1,0:T(8,128)(2,1)S(1)}, bf16[128,128]{1,0:T(8,128)(2,1)S(1)}, u32[]{:S(2)}, u32[]{:S(2)}) collective-permute-start(bf16[128,128]{1,0:T(8,128)(2,1)S(1)} %shard_map.62.piece_ref), channel_id=1, source_target_pairs={{0,1},{4,5},{8,9},{12,13},{16,17},{20,21},{24,25},{28,29},{32,33},... | collective-permute-start | bytes 98312 | tf_op jit(solution)/shard_map/ppermute | solution.py:352
  28.0 21.3 %all_to_all.5.slab_ref = bf16[16,192,128]{2,1,0:T(8,128)(2,1)S(1)} all-to-all(bf16[16,192,128]{2,1,0:T(8,128)(2,1)S(1)} %shard_map.63), channel_id=1, replica_groups={{0,16,32,48,4,20,36,52,8,24,40,56,12,28,44,60},{1,17,33,49,5,21,37,53,9..., dimensions={0} | all-to-all | bytes 1572864 | tf_op jit(solution)/shard_map/all_to_all | solution.py:444
  49.3 5.8 %shard_map.64 = (f32[32,128]{1,0:T(8,128)}, f32[2,512,128]{2,1,0:T(8,128)S(1)}, s16[528,128]{1,0:T(8,128)(2,1)S(1)}, s16[528,128]{1,0:T(8,128)(2,1)S(1)}) custom-call(s32[5,4]{1,0:T(8,128)S(1)} %stack.54.info, bf16[4,1024,1024]{2,1,0:T(8,128)(2,1)} %tiles_ref.3, bf16[16,192,128]{2,1,0:T(8,128)(2,1)S(1)} %all_to_all.5.slab_ref), custom_call_target="tpu_custom_call" | custom-call | flops 1073741824 | bytes 10485760 | tf_op jit(solution)/shard_map/pallas_call | solution.py:314
  55.2 6.7 %collective-permute-start.11 = (s16[528,128]{1,0:T(8,128)(2,1)S(1)}, s16[528,128]{1,0:T(8,128)(2,1)S(1)}, u32[]{:S(2)}, u32[]{:S(2)}) collective-permute-start(s16[528,128]{1,0:T(8,128)(2,1)S(1)} %get-tuple-element.24), channel_id=1, source_target_pairs={{0,192},{64,128},{128,64},{192,0},{1,193},{65,129},{129,65},{193,1... | collective-permute-start | bytes 405512 | tf_op jit(solution)/shard_map/ppermute | solution.py:330
  62.3 3.8 %collective-permute-start.15 = (s16[528,128]{1,0:T(8,128)(2,1)S(1)}, s16[528,128]{1,0:T(8,128)(2,1)S(1)}, u32[]{:S(2)}, u32[]{:S(2)}) collective-permute-start(s16[528,128]{1,0:T(8,128)(2,1)S(1)} %shard_map.67.own_ref), channel_id=1, source_target_pairs={{0,192},{64,128},{128,64},{192,0},{1,193},{65,129},{129,65},{193,1... | collective-permute-start | bytes 405512 | tf_op jit(solution)/shard_map/ppermute | solution.py:330
  66.1 3.1 %collective-permute-done.11.got_ref = s16[528,128]{1,0:T(8,128)(2,1)S(1)} collective-permute-done((s16[528,128]{1,0:T(8,128)(2,1)S(1)}, s16[528,128]{1,0:T(8,128)(2,1)S(1)}, u32[]{:S(2)}, u32[]{:S(2)}) %collective-permute-start.11) | collective-permute-done | bytes 135200 | tf_op jit(solution)/shard_map/ppermute | solution.py:330
  69.7 2.4 %collective-permute-done.15.got_ref = s16[528,128]{1,0:T(8,128)(2,1)S(1)} collective-permute-done((s16[528,128]{1,0:T(8,128)(2,1)S(1)}, s16[528,128]{1,0:T(8,128)(2,1)S(1)}, u32[]{:S(2)}, u32[]{:S(2)}) %collective-permute-start.15) | collective-permute-done | bytes 135200 | tf_op jit(solution)/shard_map/ppermute | solution.py:330
  72.2 3.4 %collective-permute-start.16 = (s16[528,128]{1,0:T(8,128)(2,1)S(1)}, s16[528,128]{1,0:T(8,128)(2,1)S(1)}, u32[]{:S(2)}, u32[]{:S(2)}) collective-permute-start(s16[528,128]{1,0:T(8,128)(2,1)S(1)} %shard_map.68.own_ref), channel_id=1, source_target_pairs={{0,64},{64,0},{128,192},{192,128},{1,65},{65,1},{129,193},{193,129... | collective-permute-start | bytes 405512 | tf_op jit(solution)/shard_map/ppermute | solution.py:330
  76.0 5.5 %collective-permute-start.13 = (s16[528,128]{1,0:T(8,128)(2,1)S(1)}, s16[528,128]{1,0:T(8,128)(2,1)S(1)}, u32[]{:S(2)}, u32[]{:S(2)}) collective-permute-start(s16[528,128]{1,0:T(8,128)(2,1)S(1)} %shard_map.66.own_ref), channel_id=1, source_target_pairs={{0,192},{64,128},{128,64},{192,0},{1,193},{65,129},{129,65},{193,1... | collective-permute-start | bytes 405512 | tf_op jit(solution)/shard_map/ppermute | solution.py:330
  81.5 1.0 %collective-permute-done.16.got_ref = s16[528,128]{1,0:T(8,128)(2,1)S(1)} collective-permute-done((s16[528,128]{1,0:T(8,128)(2,1)S(1)}, s16[528,128]{1,0:T(8,128)(2,1)S(1)}, u32[]{:S(2)}, u32[]{:S(2)}) %collective-permute-start.16) | collective-permute-done | bytes 135200 | tf_op jit(solution)/shard_map/ppermute | solution.py:330
  82.5 1.4 %shard_map.69.refs_0_ = f32[2048,128]{1,0:T(8,128)} custom-call(s32[5]{0:T(128)S(1)} %stack.57.bits, s16[528,128]{1,0:T(8,128)(2,1)S(1)} %shard_map.68.own_ref, s16[528,128]{1,0:T(8,128)(2,1)S(1)} %collective-permute-done.16.got_ref), custom_call_target="tpu_custom_call" | custom-call | tf_op jit(solution)/shard_map/pallas_call | solution.py:260
  84.0 2.2 %collective-permute-done.13.got_ref = s16[528,128]{1,0:T(8,128)(2,1)S(1)} collective-permute-done((s16[528,128]{1,0:T(8,128)(2,1)S(1)}, s16[528,128]{1,0:T(8,128)(2,1)S(1)}, u32[]{:S(2)}, u32[]{:S(2)}) %collective-permute-start.13) | collective-permute-done | bytes 135200 | tf_op jit(solution)/shard_map/ppermute | solution.py:330
  86.2 1.4 %shard_map.70 = f32[2048,128]{1,0:T(8,128)} custom-call(s32[5]{0:T(128)S(1)} %stack.57.bits, s16[528,128]{1,0:T(8,128)(2,1)S(1)} %shard_map.66.own_ref, s16[528,128]{1,0:T(8,128)(2,1)S(1)} %collective-permute-done.13.got_ref, f32[2048,128]{1,0:T(8,128)} %shard_map.69.refs_0_), custom_call_target="tpu_custom_call", output_to_operand_aliasing={{}: (3, {})} | custom-call | tf_op jit(solution)/shard_map/pallas_call | solution.py:260
  (34 shorter events, 5.0 us)
Async XLA Ops:
  1.5 1.0 %copy-start = (bf16[2048,128]{1,0:T(8,128)(2,1)S(1)}, bf16[2048,128]{1,0:T(8,128)(2,1)}, u32[]{:S(2)}) copy-start(bf16[2048,128]{1,0:T(8,128)(2,1)} %panel_ref.3) | copy-start | bytes 1572868
  2.6 10.1 %copy-start.1 = (bf16[2048,128]{1,0:T(8,128)(2,1)S(1)}, bf16[2048,128]{1,0:T(8,128)(2,1)}, u32[]{:S(2)}) copy-start(bf16[2048,128]{1,0:T(8,128)(2,1)} %panel_ref.3) | copy-start | bytes 1572868
  8.3 2.2 %collective-permute-start = (f32[1024,128]{1,0:T(8,128)S(1)}, f32[1024,128]{1,0:T(8,128)S(1)}, u32[]{:S(2)}, u32[]{:S(2)}) collective-permute-start(f32[1024,128]{1,0:T(8,128)S(1)} %get-tuple-element.15), channel_id=1, source_target_pairs={{0,1},{1,0},{2,3},{3,2},{4,5},{5,4},{6,7},{7,6},{8,9},{9,8},{10,11... | collective-permute-start | bytes 1572872 | tf_op jit(solution)/shard_map/ppermute | solution.py:330
  8.4 4.3 %collective-permute-start.4 = (bf16[512,128]{1,0:T(8,128)(2,1)S(1)}, bf16[512,128]{1,0:T(8,128)(2,1)S(1)}, u32[]{:S(2)}, u32[]{:S(2)}) collective-permute-start(bf16[512,128]{1,0:T(8,128)(2,1)S(1)} %get-tuple-element.26), channel_id=1, source_target_pairs={{60,56},{125,121},{190,186},{255,251}} | collective-permute-start | bytes 393224 | tf_op jit(solution)/shard_map/ppermute | solution.py:352
  9.1 3.6 %collective-permute-start.3 = (bf16[512,128]{1,0:T(8,128)(2,1)S(1)}, bf16[512,128]{1,0:T(8,128)(2,1)S(1)}, u32[]{:S(2)}, u32[]{:S(2)}) collective-permute-start(bf16[512,128]{1,0:T(8,128)(2,1)S(1)} %get-tuple-element.27), channel_id=1, source_target_pairs={{60,52},{125,117},{190,182},{255,247}} | collective-permute-start | bytes 393224 | tf_op jit(solution)/shard_map/ppermute | solution.py:352
  9.7 2.9 %collective-permute-start.2 = (bf16[512,128]{1,0:T(8,128)(2,1)S(1)}, bf16[512,128]{1,0:T(8,128)(2,1)S(1)}, u32[]{:S(2)}, u32[]{:S(2)}) collective-permute-start(bf16[512,128]{1,0:T(8,128)(2,1)S(1)} %get-tuple-element.28), channel_id=1, source_target_pairs={{60,48},{125,113},{190,178},{255,243}} | collective-permute-start | bytes 393224 | tf_op jit(solution)/shard_map/ppermute | solution.py:352
  10.6 17.2 %collective-permute-start.1 = (s16[528,128]{1,0:T(8,128)(2,1)S(1)}, s16[528,128]{1,0:T(8,128)(2,1)S(1)}, u32[]{:S(2)}, u32[]{:S(2)}) collective-permute-start(s16[528,128]{1,0:T(8,128)(2,1)S(1)} %get-tuple-element.17), channel_id=1, source_target_pairs={{0,2},{1,3},{2,0},{3,1},{4,6},{5,7},{6,4},{7,5},{8,10},{9,11},{10,... | collective-permute-start | bytes 405512 | tf_op jit(solution)/shard_map/ppermute | solution.py:330
  13.3 9.7 %collective-permute-start.5 = (bf16[128,128]{1,0:T(8,128)(2,1)S(1)}, bf16[128,128]{1,0:T(8,128)(2,1)S(1)}, u32[]{:S(2)}, u32[]{:S(2)}) collective-permute-start(bf16[128,128]{1,0:T(8,128)(2,1)S(1)} %get-tuple-element.19), channel_id=1, source_target_pairs={{48,0},{52,4},{56,8},{60,12},{113,65},{117,69},{121,73},{125,77},{... | collective-permute-start | bytes 98312 | tf_op jit(solution)/shard_map/ppermute | solution.py:352
  14.6 8.4 %collective-permute-start.6 = (bf16[128,128]{1,0:T(8,128)(2,1)S(1)}, bf16[128,128]{1,0:T(8,128)(2,1)S(1)}, u32[]{:S(2)}, u32[]{:S(2)}) collective-permute-start(bf16[128,128]{1,0:T(8,128)(2,1)S(1)} %get-tuple-element.20), channel_id=1, source_target_pairs={{48,16},{52,20},{56,24},{60,28},{113,81},{117,85},{121,89},{125,93... | collective-permute-start | bytes 98312 | tf_op jit(solution)/shard_map/ppermute | solution.py:352
  15.3 7.8 %collective-permute-start.7 = (bf16[128,128]{1,0:T(8,128)(2,1)S(1)}, bf16[128,128]{1,0:T(8,128)(2,1)S(1)}, u32[]{:S(2)}, u32[]{:S(2)}) collective-permute-start(bf16[128,128]{1,0:T(8,128)(2,1)S(1)} %get-tuple-element.21), channel_id=1, source_target_pairs={{48,32},{52,36},{56,40},{60,44},{113,97},{117,101},{121,105},{125,... | collective-permute-start | bytes 98312 | tf_op jit(solution)/shard_map/ppermute | solution.py:352
  23.1 3.9 %collective-permute-start.10 = (bf16[128,128]{1,0:T(8,128)(2,1)S(1)}, bf16[128,128]{1,0:T(8,128)(2,1)S(1)}, u32[]{:S(2)}, u32[]{:S(2)}) collective-permute-start(bf16[128,128]{1,0:T(8,128)(2,1)S(1)} %shard_map.62.piece_ref), channel_id=1, source_target_pairs={{0,3},{4,7},{8,11},{12,15},{16,19},{20,23},{24,27},{28,31},{32,35}... | collective-permute-start | bytes 98312 | tf_op jit(solution)/shard_map/ppermute | solution.py:352
  24.4 2.9 %collective-permute-start.9 = (bf16[128,128]{1,0:T(8,128)(2,1)S(1)}, bf16[128,128]{1,0:T(8,128)(2,1)S(1)}, u32[]{:S(2)}, u32[]{:S(2)}) collective-permute-start(bf16[128,128]{1,0:T(8,128)(2,1)S(1)} %shard_map.62.piece_ref), channel_id=1, source_target_pairs={{0,2},{4,6},{8,10},{12,14},{16,18},{20,22},{24,26},{28,30},{32,34}... | collective-permute-start | bytes 98312 | tf_op jit(solution)/shard_map/ppermute | solution.py:352
  25.7 2.1 %collective-permute-start.8 = (bf16[128,128]{1,0:T(8,128)(2,1)S(1)}, bf16[128,128]{1,0:T(8,128)(2,1)S(1)}, u32[]{:S(2)}, u32[]{:S(2)}) collective-permute-start(bf16[128,128]{1,0:T(8,128)(2,1)S(1)} %shard_map.62.piece_ref), channel_id=1, source_target_pairs={{0,1},{4,5},{8,9},{12,13},{16,17},{20,21},{24,25},{28,29},{32,33},... | collective-permute-start | bytes 98312 | tf_op jit(solution)/shard_map/ppermute | solution.py:352
  55.1 7.1 %collective-permute-start.14 = (s16[528,128]{1,0:T(8,128)(2,1)S(1)}, s16[528,128]{1,0:T(8,128)(2,1)S(1)}, u32[]{:S(2)}, u32[]{:S(2)}) collective-permute-start(s16[528,128]{1,0:T(8,128)(2,1)S(1)} %get-tuple-element.25), channel_id=1, source_target_pairs={{0,64},{64,0},{128,192},{192,128},{1,65},{65,1},{129,193},{193,129... | collective-permute-start | bytes 405512 | tf_op jit(solution)/shard_map/ppermute | solution.py:330
  55.2 14.0 %collective-permute-start.11 = (s16[528,128]{1,0:T(8,128)(2,1)S(1)}, s16[528,128]{1,0:T(8,128)(2,1)S(1)}, u32[]{:S(2)}, u32[]{:S(2)}) collective-permute-start(s16[528,128]{1,0:T(8,128)(2,1)S(1)} %get-tuple-element.24), channel_id=1, source_target_pairs={{0,192},{64,128},{128,64},{192,0},{1,193},{65,129},{129,65},{193,1... | collective-permute-start | bytes 405512 | tf_op jit(solution)/shard_map/ppermute | solution.py:330
  62.3 9.8 %collective-permute-start.15 = (s16[528,128]{1,0:T(8,128)(2,1)S(1)}, s16[528,128]{1,0:T(8,128)(2,1)S(1)}, u32[]{:S(2)}, u32[]{:S(2)}) collective-permute-start(s16[528,128]{1,0:T(8,128)(2,1)S(1)} %shard_map.67.own_ref), channel_id=1, source_target_pairs={{0,192},{64,128},{128,64},{192,0},{1,193},{65,129},{129,65},{193,1... | collective-permute-start | bytes 405512 | tf_op jit(solution)/shard_map/ppermute | solution.py:330
  69.3 6.5 %collective-permute-start.12 = (s16[528,128]{1,0:T(8,128)(2,1)S(1)}, s16[528,128]{1,0:T(8,128)(2,1)S(1)}, u32[]{:S(2)}, u32[]{:S(2)}) collective-permute-start(s16[528,128]{1,0:T(8,128)(2,1)S(1)} %shard_map.65.own_ref), channel_id=1, source_target_pairs={{0,64},{64,0},{128,192},{192,128},{1,65},{65,1},{129,193},{193,129... | collective-permute-start | bytes 405512 | tf_op jit(solution)/shard_map/ppermute | solution.py:330
  72.2 10.3 %collective-permute-start.16 = (s16[528,128]{1,0:T(8,128)(2,1)S(1)}, s16[528,128]{1,0:T(8,128)(2,1)S(1)}, u32[]{:S(2)}, u32[]{:S(2)}) collective-permute-start(s16[528,128]{1,0:T(8,128)(2,1)S(1)} %shard_map.68.own_ref), channel_id=1, source_target_pairs={{0,64},{64,0},{128,192},{192,128},{1,65},{65,1},{129,193},{193,129... | collective-permute-start | bytes 405512 | tf_op jit(solution)/shard_map/ppermute | solution.py:330
  76.0 10.2 %collective-permute-start.13 = (s16[528,128]{1,0:T(8,128)(2,1)S(1)}, s16[528,128]{1,0:T(8,128)(2,1)S(1)}, u32[]{:S(2)}, u32[]{:S(2)}) collective-permute-start(s16[528,128]{1,0:T(8,128)(2,1)S(1)} %shard_map.66.own_ref), channel_id=1, source_target_pairs={{0,192},{64,128},{128,64},{192,0},{1,193},{65,129},{129,65},{193,1... | collective-permute-start | bytes 405512 | tf_op jit(solution)/shard_map/ppermute | solution.py:330

commit v2 on v1

--- a/solution.py
+++ b/solution.py
@@ -14,12 +14,7 @@
 PAD = 16
 SITES = 16
 PLANES = 4
-LINE = 4
 BF16_MOST = 3.3895313892515355e38
-
-
-def site_at(place):
-    return place % LINE * LINE + place // LINE
 
 
 def place_of(info, index, depth, width):
@@ -87,10 +82,9 @@
     share = total.shape[0] // (SITES * PLANES)
     for ref, which in ((keep_ref, core), (send_ref, 1 - core)):
         for step, chip in enumerate((depth_z, 1 - depth_z)):
-            for place in range(SITES):
-                site = site_at(place)
+            for site in range(SITES):
                 source = pl.multiple_of((site * PLANES + chip * 2 + which) * share, share)
-                target = (step * SITES + place) * share
+                target = (step * SITES + site) * share
                 ref[target : target + share, :] = total[pl.ds(source, share), :]
 
 
@@ -100,41 +94,24 @@
     encode(keep_ref[size:, :] + got_ref[size:, :], send_ref)
 
 
-def sum_of(refs):
-    total = refs[0][...].astype(jnp.float32)
-    for ref in refs[1:]:
-        total += ref[...].astype(jnp.float32)
-    return total.astype(refs[0].dtype)
-
-
-def strip_kernel(home, bits, panel_ref, got1_ref, got2_ref, got3_ref, after_ref, *out_refs):
+def pack_kernel(bits, piece_ref, got1_ref, got2_ref, got3_ref, out_ref):
+    own = jnp.where(bits[4] == 1, piece_ref[...].astype(jnp.float32), 0.0)
+    rest = got1_ref[...].astype(jnp.float32) + got2_ref[...].astype(jnp.float32)
+    piece = (own + rest + got3_ref[...].astype(jnp.float32)).astype(jnp.bfloat16)
+    for site in range(out_ref.shape[0]):
+        out_ref[site] = piece
+
+
+def rows_kernel(mine_ref, got_ref, after_ref, out_ref):
     del after_ref
-    rows = got1_ref.shape[0]
-    own = panel_ref[home * rows : (home + 1) * rows, :].astype(jnp.float32)
-    own = jnp.where(bits[4] == 1, own, 0.0)
-    rest = got1_ref[...].astype(jnp.float32) + got2_ref[...].astype(jnp.float32)
-    strip = (own + rest + got3_ref[...].astype(jnp.float32)).astype(jnp.bfloat16)
-    size = rows // LINE
-    for index, out_ref in enumerate(out_refs):
-        out_ref[...] = strip[index * size : (index + 1) * size]
-
-
-def sum_kernel(*refs):
-    refs[-1][...] = sum_of(refs[:-1])
-
-
-def pack_kernel(mine_ref, got_ref, piece_ref, got1_ref, got2_ref, got3_ref, out_ref):
-    sites = out_ref.shape[0]
-    size = piece_ref.shape[0]
-    share = mine_ref.shape[0] // sites
-    piece = sum_of((piece_ref, got1_ref, got2_ref, got3_ref))
-    sums = mine_ref[...] + decode(got_ref)
-    high = jnp.clip(sums, -BF16_MOST, BF16_MOST).astype(jnp.bfloat16)
-    low = (sums - high.astype(jnp.float32)).astype(jnp.bfloat16)
-    for site in range(sites):
-        out_ref[site, :size, :] = piece
-        out_ref[site, size : size + share, :] = high[site * share : (site + 1) * share]
-        out_ref[site, size + share :, :] = low[site * share : (site + 1) * share]
+    out_ref[...] = mine_ref[...] + decode(got_ref)
+
+
+def total_kernel(terms_ref, out_ref):
+    total = terms_ref[0]
+    for site in range(1, terms_ref.shape[0]):
+        total += terms_ref[site]
+    out_ref[...] = total
 
 
 def block_rows(size):
@@ -174,22 +151,16 @@
 
 
 def col_kernel(
-    info, tiles_ref, slab_ref, rows_ref, keep_ref, send0_ref, send1_ref, total, result, held, sems
+    info, tiles_ref, slab_ref, after_ref, keep_ref, send0_ref, send1_ref, total, result, held, sems
 ):
+    del after_ref
     slots, width, _ = held.shape
     depth = width // STEPS
-    size, share = slab_ref.shape[1], rows_ref.shape[0]
-    size = size - 2 * share
-    count = depth // size
+    count = depth // slab_ref.shape[1]
     fetch = fetch_of(info, tiles_ref, held, sems)
     for index in range(slots * STEPS):
         fetch(index).start()
     total[...] = jnp.zeros_like(total)
-    sums = jnp.zeros(rows_ref.shape, jnp.float32)
-    for site in range(slab_ref.shape[0]):
-        sums += slab_ref[site, size : size + share, :].astype(jnp.float32)
-        sums += slab_ref[site, size + share :, :].astype(jnp.float32)
-    rows_ref[...] = sums
 
     @pl.loop(0, slots * STEPS)
     def _(index):
@@ -199,7 +170,7 @@
         @pl.when(info[2, slot] == 1)
         def _():
             first = (info[0, slot] * STEPS + part) * count
-            source = slab_ref[pl.ds(first, count), :size, :].reshape(depth, slab_ref.shape[2])
+            source = slab_ref[pl.ds(first, count), :, :].reshape(depth, slab_ref.shape[2])
             total[:, cols] += lax.dot_general(
                 source, held[slot, piece, :], (((0,), (0,)), ((), ())),
                 preferred_element_type=jnp.float32,
@@ -238,19 +209,19 @@
 VMEM = pl.BlockSpec(memory_space=pltpu.VMEM)
 SMEM = pl.BlockSpec(memory_space=pltpu.SMEM)
 HBM = pl.BlockSpec(memory_space=pltpu.HBM)
-ANY = pl.BlockSpec(memory_space=pl.ANY)
 
 
 def limit(size):
     return pltpu.CompilerParams(vmem_limit_bytes=size * MIB)
 
 
-def small_call(kernel, outs, *args, scalars=0, after=None):
-    specs = [SMEM] * scalars + [VMEM] * (len(args) - scalars)
-    if after is not None:
-        specs, args = specs + [ANY], args + (after,)
+def small_call(kernel, outs, *args, scalars=0):
     return pl.pallas_call(
-        kernel, in_specs=specs, out_specs=[VMEM] * len(outs), out_shape=outs, compiler_params=limit(6)
+        kernel,
+        in_specs=[SMEM] * scalars + [VMEM] * (len(args) - scalars),
+        out_specs=[VMEM] * len(outs),
+        out_shape=outs,
+        compiler_params=limit(6),
     )(*args)
 
 
@@ -307,15 +278,15 @@
     )(info, grm_tiles, panel)
 
 
-def col_products(info, grm_tiles, packed, share):
+def col_products(info, grm_tiles, slab, after):
     slots, width, _ = grm_tiles.shape
-    lanes = packed.shape[2]
+    lanes = slab.shape[2]
     half = width // 2
     return pl.pallas_call(
         col_kernel,
-        in_specs=[SMEM, HBM, VMEM],
-        out_specs=[VMEM] * 4,
-        out_shape=[floats(share, lanes), floats(2, half, lanes), coded(half, lanes), coded(half, lanes)],
+        in_specs=[SMEM, HBM, VMEM, VMEM],
+        out_specs=[VMEM] * 3,
+        out_shape=[floats(2, half, lanes), coded(half, lanes), coded(half, lanes)],
         scratch_shapes=[
             pltpu.VMEM((lanes, CTD * width), jnp.float32),
             pltpu.VMEM((CTD * width, lanes), jnp.float32),
@@ -323,7 +294,7 @@
         + tile_scratch(grm_tiles),
         compiler_params=limit(24),
         cost_estimate=tile_cost(grm_tiles.shape, lanes),
-    )(info, grm_tiles, packed)
+    )(info, grm_tiles, slab, after)
 
 
 def swap(value, axis, flip):
@@ -339,67 +310,26 @@
         small_call(functools.partial(first_kernel, index), outs, keep, got)[0]
         for index, got in enumerate(gots)
     ]
+    begun = owns[0]
     gots = [swap(own, "row", flip[1]) for own, flip in zip(owns, flips)]
     owns = [small_call(second_kernel, outs, own, got)[0] for own, got in zip(owns, gots)]
     gots = [swap(own, "row", flip[2]) for own, flip in zip(owns, flips)]
     result = None
     for index in range(2):
         result = place_half(index, bits, owns[index], gots[index], result)
-    return result
-
-
-def permute(value, pairs):
-    return lax.ppermute(value, ("row", "col"), pairs)
-
-
-def send_pieces(bits, panel, owners, after):
-    lanes = panel.shape[1]
-    rows = panel.shape[0] // LINE
-    planes = [owner % PLANES for owner in owners]
-    home_y, home_x = divmod(owners[0] // PLANES, LINE)
-
-    def device(row, y, x, plane):
-        return ((row * LINE + y) * LINE + x) * PLANES + plane
-
-    got = [
-        permute(
-            panel[x * rows : (x + 1) * rows],
-            [(device(r, home_y, home_x, p), device(r, home_y, x, p)) for r, p in enumerate(planes)],
-        )
-        for x in range(LINE)
-        if x != home_x
-    ]
-    shape = jax.ShapeDtypeStruct((rows // LINE, lanes), panel.dtype)
-    pieces = small_call(
-        functools.partial(strip_kernel, home_x), [shape] * LINE, bits, panel, *got,
-        scalars=1, after=after,
-    )
-    got = [
-        permute(
-            pieces[y],
-            [
-                (device(r, home_y, x, p), device(r, y, x, p))
-                for r, p in enumerate(planes)
-                for x in range(LINE)
-            ],
-        )
-        for y in range(LINE)
-        if y != home_y
-    ]
-    piece = small_call(sum_kernel, [shape], pieces[home_y], *got)[0]
-    got = [
-        permute(
-            piece,
-            [
-                (device(r, y, x, p), device(r, y, x, (p + step) % PLANES))
-                for r, p in enumerate(planes)
-                for y in range(LINE)
-                for x in range(LINE)
-            ],
-        )
-        for step in range(1, PLANES)
-    ]
-    return [piece, *got]
+    return result, begun
+
+
+def spread(piece, planes):
+    got = []
+    for step in range(1, PLANES):
+        pairs = [
+            ((row * SITES + site) * PLANES + plane, (row * SITES + site) * PLANES + (plane + step) % PLANES)
+            for row, plane in enumerate(planes)
+            for site in range(SITES)
+        ]
+        got.append(lax.ppermute(piece, ("row", "col"), pairs))
+    return got
 
 
 def on_device(grm_tiles, tile_row, tile_col, panel):
@@ -420,30 +350,42 @@
     low = (row_index + high) % 2
     core = col_index % 2
     chip = col_index // 2 % 2
-    root = (col_index == (offset + base_row) // CTD).astype(jnp.int32)
-    bits = jnp.stack([low, high, core, chip, root]).astype(jnp.int32)
+    holds = (col_index % PLANES == (offset + base_row) // CTD % PLANES).astype(jnp.int32)
+    bits = jnp.stack([low, high, core, chip, holds]).astype(jnp.int32)
     info = jnp.stack(
         [local_row, local_col, kind, jnp.pad(bits[:2], (0, 2)), jnp.pad(bits[2:4], (0, 2))]
     ).astype(jnp.int32)
 
-    across = [[site_at(place) * PLANES + plane for place in range(SITES)] for plane in range(PLANES)]
+    across = [[site * PLANES + plane for site in range(SITES)] for plane in range(PLANES)]
     tiles = pltpu.with_memory_space_constraint(grm_tiles, pltpu.HBM)
+    size = panel.shape[0] // SITES
+    pieces = lax.all_to_all(
+        panel.reshape(SITES, size, lanes), "col", 0, 0, axis_index_groups=across
+    )
     keep, send = row_products(info, tiles, panel)
+    pieces, keep, send = lax.optimization_barrier((pieces, keep, send))
     half = keep.shape[0] // 2
     share = half // SITES
     mine, send_z = small_call(
         add_kernel, [floats(half, lanes), coded(half, lanes)], keep, swap(send, "col", 1)
     )
-    pieces = send_pieces(bits, panel, owners, keep)
-    size = pieces[0].shape[0]
+    piece = pieces[owners[0] // PLANES]
+    got = spread(piece, [owner % PLANES for owner in owners])
     packed = small_call(
         pack_kernel,
-        [jax.ShapeDtypeStruct((SITES, size + 2 * share, lanes), jnp.bfloat16)],
-        mine, swap(send_z, "col", 2), *pieces,
+        [jax.ShapeDtypeStruct((SITES, size, lanes), jnp.bfloat16)],
+        bits, piece, *got,
+        scalars=1,
     )[0]
-    packed = lax.all_to_all(packed, "col", 0, 0, axis_index_groups=across)
-    y_rows, keep, *sends = col_products(info, tiles, packed, share)
-    y_cols = sum_over_row(bits, keep, sends)
+    slab = lax.all_to_all(packed, "col", 0, 0, axis_index_groups=across)
+    got_z = swap(send_z, "col", 2)
+    keep, *sends = col_products(info, tiles, slab, got_z)
+    y_cols, begun = sum_over_row(bits, keep, sends)
+    rows = small_call(rows_kernel, [floats(half, lanes)], mine, got_z, begun)[0]
+    terms = lax.all_to_all(
+        rows.reshape(SITES, share, lanes), "col", 0, 0, axis_index_groups=across
+    )
+    y_rows = small_call(total_kernel, [floats(share, lanes)], terms)[0]
     return (y_rows, y_cols)
 
 

time: 89.1 us -> 82.9 us (0.930); the launches traced: 87.6 us -> 82.4 us
  blocking collectives: 21.3 us -> 0 us
  starting transfers between devices: 30.4 us -> 48.8 us
  waiting for transfers between devices: 17.2 us -> 13.6 us
  Pallas kernels: 15.8 us -> 17.2 us
    all_to_all x0 -> x3, starting transfers between devices: none -> 21.3 us  [the longest x1 7.81 us: on_device(): lax.all_to_all(rows.reshape(SITES, share, lanes), 'col', 0, 0, axis_index...]
    all_to_all x1 -> x0, blocking collectives: 21.3 us -> none  [on_device(): packed = lax.all_to_all(packed, 'col', 0, 0, axis_index_groups=across)]
    all_to_all x0 -> x3, waiting for transfers between devices: none -> 9.15 us  [the longest x1 7.78 us: on_device(): slab = lax.all_to_all(packed, 'col', 0, 0, axis_index_groups=across)]
    ppermute x9 -> x3, waiting for transfers between devices: 7.94 us -> 0.72 us  [spread(): got.append(lax.ppermute(piece, ('row', 'col'), pairs))]
    ppermute x8, waiting for transfers between devices: 9.27 us -> 3.74 us  [swap(): lax.ppermute(value, axis, [(k, k ^ flip) for k in range(lax.axis_size(axi...]
    ppermute x9 -> x3, starting transfers between devices: 8.5 us -> 6.51 us  [spread(): got.append(lax.ppermute(piece, ('row', 'col'), pairs))]
    pallas_call x9, Pallas kernels: 7.27 us -> 8.72 us  [the longest x1 5.27 us: col_products(): pl.pallas_call(col_kernel, in_specs=[SMEM, HBM, VMEM, VMEM], out_specs=[V...]
    ppermute x8, starting transfers between devices: 21.9 us -> 21 us  [swap(): lax.ppermute(value, axis, [(k, k ^ flip) for k in range(lax.axis_size(axi...]
  transfers between devices with their start and end apart: 17 -> 14, of which waited for: 9 -> 6; matrix products, arithmetic and copies ran while one was open for 0% -> 1% of each run, Pallas kernels for 3% -> 13%
where the time goes in v2:
time: 82.9 us; the launch traced here: 82.4 us
  starting transfers between devices  48.8 us (59%)
  Pallas kernels  17.2 us (21%)
  waiting for transfers between devices  13.6 us (16%)
  local copies, waits for them, and re-layouts  1.16 us (1%)
  other arithmetic  0.83 us (1%)
    ppermute x8, starting transfers between devices, swap(): lax.ppermute(value, axis, [(k, k ^ flip) for k in range(lax.axis_size(axi...  21 us
    all_to_all x1, starting transfers between devices, on_device(): lax.all_to_all(rows.reshape(SITES, share, lanes), 'col', 0, 0, axis_index...  7.81 us
    all_to_all x1, waiting for transfers between devices, on_device(): slab = lax.all_to_all(packed, 'col', 0, 0, axis_index_groups=across)  7.78 us
    all_to_all x1, starting transfers between devices, on_device(): lax.all_to_all(panel.reshape(SITES, size, lanes), 'col', 0, 0, axis_index...  7.43 us
    ppermute x3, starting transfers between devices, spread(): got.append(lax.ppermute(piece, ('row', 'col'), pairs))  6.51 us
    all_to_all x1, starting transfers between devices, on_device(): slab = lax.all_to_all(packed, 'col', 0, 0, axis_index_groups=across)  6.09 us
    pallas_call x1, Pallas kernels, row_products(): pl.pallas_call(row_kernel, in_specs=[SMEM, HBM, VMEM], out_specs=[VMEM, V...  5.64 us
    pallas_call x1, Pallas kernels, col_products(): pl.pallas_call(col_kernel, in_specs=[SMEM, HBM, VMEM, VMEM], out_specs=[V...  5.27 us
  transfers between devices with their start and end apart: 14, of which 6 were waited for; matrix products, arithmetic and copies ran while one was open for 1% of the time, Pallas kernels for 13%

profile of v2, /device:TPU:6, one launch (start us, length us, event | category | flops | bytes accessed | tf_op | source)
XLA Modules:
  0.0 82.4 jit_solution(11886799212310498436)
XLA Ops:
  0.6 7.4 %all-to-all-start = ((bf16[16,128,128]{2,1,0:T(8,128)(2,1)}), bf16[16,128,128]{2,1,0:T(8,128)(2,1)S(1)}, u32[]{:S(2)}, u32[]{:S(2)}) async-start(bf16[16,128,128]{2,1,0:T(8,128)(2,1)} %bitcast.19), calls=%async_computation | async-start | bytes 1048576 | tf_op jit(solution)/shard_map/all_to_all | solution.py:362
  8.2 0.7 fusion
  8.9 1.0 %copy-done = bf16[2048,128]{1,0:T(8,128)(2,1)S(1)} copy-done((bf16[2048,128]{1,0:T(8,128)(2,1)S(1)}, bf16[2048,128]{1,0:T(8,128)(2,1)}, u32[]{:S(2)}) %copy-start) | copy-done | bytes 524312
  10.0 5.6 %shard_map.59 = (f32[1024,128]{1,0:T(8,128)S(1)}, f32[1024,128]{1,0:T(8,128)S(1)}) custom-call(s32[5,4]{1,0:T(8,128)S(1)} %stack.54.info, bf16[4,1024,1024]{2,1,0:T(8,128)(2,1)} %tiles_ref.3, bf16[2048,128]{1,0:T(8,128)(2,1)S(1)} %copy-done), custom_call_target="tpu_custom_call" | custom-call | flops 1073741824 | bytes 10485760 | tf_op jit(solution)/shard_map/pallas_call | solution.py:270
  15.6 1.4 %all-to-all-done = bf16[16,128,128]{2,1,0:T(8,128)(2,1)S(1)} async-done(((bf16[16,128,128]{2,1,0:T(8,128)(2,1)}), bf16[16,128,128]{2,1,0:T(8,128)(2,1)S(1)}, u32[]{:S(2)}, u32[]{:S(2)}) %all-to-all-start) | async-done | bytes 524320 | tf_op jit(solution)/shard_map/all_to_all | solution.py:362
  17.0 3.9 %collective-permute-start.4 = (bf16[128,128]{1,0:T(8,128)(2,1)S(1)}, bf16[128,128]{1,0:T(8,128)(2,1)S(1)}, u32[]{:S(2)}, u32[]{:S(2)}) collective-permute-start(bf16[128,128]{1,0:T(8,128)(2,1)S(1)} %slice_bitcast_fusion.piece_ref), channel_id=1, source_target_pairs={{0,3},{4,7},{8,11},{12,15},{16,19},{20,23},{24,27},{28,31},{32,35}... | collective-permute-start | bytes 98312 | tf_op jit(solution)/shard_map/ppermute | solution.py:331
  20.9 1.3 %collective-permute-start.3 = (bf16[128,128]{1,0:T(8,128)(2,1)S(1)}, bf16[128,128]{1,0:T(8,128)(2,1)S(1)}, u32[]{:S(2)}, u32[]{:S(2)}) collective-permute-start(bf16[128,128]{1,0:T(8,128)(2,1)S(1)} %slice_bitcast_fusion.piece_ref), channel_id=1, source_target_pairs={{0,2},{4,6},{8,10},{12,14},{16,18},{20,22},{24,26},{28,30},{32,34}... | collective-permute-start | bytes 98312 | tf_op jit(solution)/shard_map/ppermute | solution.py:331
  22.2 1.3 %collective-permute-start.2 = (bf16[128,128]{1,0:T(8,128)(2,1)S(1)}, bf16[128,128]{1,0:T(8,128)(2,1)S(1)}, u32[]{:S(2)}, u32[]{:S(2)}) collective-permute-start(bf16[128,128]{1,0:T(8,128)(2,1)S(1)} %slice_bitcast_fusion.piece_ref), channel_id=1, source_target_pairs={{0,1},{4,5},{8,9},{12,13},{16,17},{20,21},{24,25},{28,29},{32,33},... | collective-permute-start | bytes 98312 | tf_op jit(solution)/shard_map/ppermute | solution.py:331
  24.4 1.4 %shard_map.61 = bf16[16,128,128]{2,1,0:T(8,128)(2,1)} custom-call(s32[5]{0:T(128)S(1)} %stack.57.bits, bf16[128,128]{1,0:T(8,128)(2,1)S(1)} %slice_bitcast_fusion.piece_ref, bf16[128,128]{1,0:T(8,128)(2,1)S(1)} %collective-permute-done.2.got1_ref, bf16[128,128]{1,0:T(8,128)(2,1)S(1)} %collective-permute-done.3.got2_ref, ...), custom_call_target="tpu_custom_call" | custom-call | tf_op jit(solution)/shard_map/pallas_call | solution.py:219
  25.7 6.1 %all-to-all-start.1 = ((bf16[16,128,128]{2,1,0:T(8,128)(2,1)}), bf16[16,128,128]{2,1,0:T(8,128)(2,1)S(1)}, u32[]{:S(2)}, u32[]{:S(2)}) async-start(bf16[16,128,128]{2,1,0:T(8,128)(2,1)} %shard_map.61), calls=%async_computation.1 | async-start | bytes 1048576 | tf_op jit(solution)/shard_map/all_to_all | solution.py:380
  32.0 1.8 %collective-permute-start.1 = (s16[528,128]{1,0:T(8,128)(2,1)S(1)}, s16[528,128]{1,0:T(8,128)(2,1)S(1)}, u32[]{:S(2)}, u32[]{:S(2)}) collective-permute-start(s16[528,128]{1,0:T(8,128)(2,1)S(1)} %get-tuple-element.17), channel_id=1, source_target_pairs={{0,2},{1,3},{2,0},{3,1},{4,6},{5,7},{6,4},{7,5},{8,10},{9,11},{10,... | collective-permute-start | bytes 405512 | tf_op jit(solution)/shard_map/ppermute | solution.py:301
  33.8 7.8 %all-to-all-done.1.slab_ref = bf16[16,128,128]{2,1,0:T(8,128)(2,1)S(1)} async-done(((bf16[16,128,128]{2,1,0:T(8,128)(2,1)}), bf16[16,128,128]{2,1,0:T(8,128)(2,1)S(1)}, u32[]{:S(2)}, u32[]{:S(2)}) %all-to-all-start.1) | async-done | bytes 524320 | tf_op jit(solution)/shard_map/all_to_all | solution.py:380
  41.6 5.3 %shard_map.62 = (f32[2,512,128]{2,1,0:T(8,128)S(1)}, s16[528,128]{1,0:T(8,128)(2,1)S(1)}, s16[528,128]{1,0:T(8,128)(2,1)S(1)}) custom-call(s32[5,4]{1,0:T(8,128)S(1)} %stack.54.info, bf16[4,1024,1024]{2,1,0:T(8,128)(2,1)} %tiles_ref.3, bf16[16,128,128]{2,1,0:T(8,128)(2,1)S(1)} %all-to-all-done.1.slab_ref, ...), custom_call_target="tpu_custom_call" | custom-call | flops 1073741824 | bytes 10485760 | tf_op jit(solution)/shard_map/pallas_call | solution.py:285
  47.0 5.8 %collective-permute-start.6 = (s16[528,128]{1,0:T(8,128)(2,1)S(1)}, s16[528,128]{1,0:T(8,128)(2,1)S(1)}, u32[]{:S(2)}, u32[]{:S(2)}) collective-permute-start(s16[528,128]{1,0:T(8,128)(2,1)S(1)} %get-tuple-element.21), channel_id=1, source_target_pairs={{0,192},{64,128},{128,64},{192,0},{1,193},{65,129},{129,65},{193,1... | collective-permute-start | bytes 405512 | tf_op jit(solution)/shard_map/ppermute | solution.py:301
  52.8 2.0 %collective-permute-done.5.got_ref = s16[528,128]{1,0:T(8,128)(2,1)S(1)} collective-permute-done((s16[528,128]{1,0:T(8,128)(2,1)S(1)}, s16[528,128]{1,0:T(8,128)(2,1)S(1)}, u32[]{:S(2)}, u32[]{:S(2)}) %collective-permute-start.5) | collective-permute-done | bytes 135200 | tf_op jit(solution)/shard_map/ppermute | solution.py:301
  54.9 4.7 %collective-permute-start.9 = (s16[528,128]{1,0:T(8,128)(2,1)S(1)}, s16[528,128]{1,0:T(8,128)(2,1)S(1)}, u32[]{:S(2)}, u32[]{:S(2)}) collective-permute-start(s16[528,128]{1,0:T(8,128)(2,1)S(1)} %shard_map.63.after_ref.own_ref), channel_id=1, source_target_pairs={{0,192},{64,128},{128,64},{192,0},{1,193},{65,129},{129,65},{193,1... | collective-permute-start | bytes 405512 | tf_op jit(solution)/shard_map/ppermute | solution.py:301
  59.8 0.7 collective-permute-start.7
  60.5 0.8 shard_map.64
  61.2 7.8 %all-to-all-start.2 = ((f32[16,32,128]{2,1,0:T(8,128)}), f32[16,32,128]{2,1,0:T(8,128)S(1)}, u32[]{:S(2)}, u32[]{:S(2)}) async-start(f32[16,32,128]{2,1,0:T(8,128)} %bitcast.12), calls=%async_computation.2 | async-start | bytes 524288 | tf_op jit(solution)/shard_map/all_to_all | solution.py:385
  69.2 3.0 %collective-permute-start.10 = (s16[528,128]{1,0:T(8,128)(2,1)S(1)}, s16[528,128]{1,0:T(8,128)(2,1)S(1)}, u32[]{:S(2)}, u32[]{:S(2)}) collective-permute-start(s16[528,128]{1,0:T(8,128)(2,1)S(1)} %shard_map.68.own_ref), channel_id=1, source_target_pairs={{0,64},{64,0},{128,192},{192,128},{1,65},{65,1},{129,193},{193,129... | collective-permute-start | bytes 405512 | tf_op jit(solution)/shard_map/ppermute | solution.py:301
  72.4 4.8 %collective-permute-start.8 = (s16[528,128]{1,0:T(8,128)(2,1)S(1)}, s16[528,128]{1,0:T(8,128)(2,1)S(1)}, u32[]{:S(2)}, u32[]{:S(2)}) collective-permute-start(s16[528,128]{1,0:T(8,128)(2,1)S(1)} %shard_map.67.own_ref), channel_id=1, source_target_pairs={{0,192},{64,128},{128,64},{192,0},{1,193},{65,129},{129,65},{193,1... | collective-permute-start | bytes 405512 | tf_op jit(solution)/shard_map/ppermute | solution.py:301
  77.8 1.4 %shard_map.69.refs_0_ = f32[2048,128]{1,0:T(8,128)} custom-call(s32[5]{0:T(128)S(1)} %stack.57.bits, s16[528,128]{1,0:T(8,128)(2,1)S(1)} %shard_map.68.own_ref, s16[528,128]{1,0:T(8,128)(2,1)S(1)} %collective-permute-done.10.got_ref), custom_call_target="tpu_custom_call" | custom-call | tf_op jit(solution)/shard_map/pallas_call | solution.py:231
  79.3 1.7 %collective-permute-done.8.got_ref = s16[528,128]{1,0:T(8,128)(2,1)S(1)} collective-permute-done((s16[528,128]{1,0:T(8,128)(2,1)S(1)}, s16[528,128]{1,0:T(8,128)(2,1)S(1)}, u32[]{:S(2)}, u32[]{:S(2)}) %collective-permute-start.8) | collective-permute-done | bytes 135200 | tf_op jit(solution)/shard_map/ppermute | solution.py:301
  81.0 1.4 %shard_map.70 = f32[2048,128]{1,0:T(8,128)} custom-call(s32[5]{0:T(128)S(1)} %stack.57.bits, s16[528,128]{1,0:T(8,128)(2,1)S(1)} %shard_map.67.own_ref, s16[528,128]{1,0:T(8,128)(2,1)S(1)} %collective-permute-done.8.got_ref, f32[2048,128]{1,0:T(8,128)} %shard_map.69.refs_0_), custom_call_target="tpu_custom_call", output_to_operand_aliasing={{}: (3, {})} | custom-call | tf_op jit(solution)/shard_map/pallas_call | solution.py:231
  (25 shorter events, 2.4 us)
Async XLA Ops:
  0.6 16.3 %all-to-all-start = ((bf16[16,128,128]{2,1,0:T(8,128)(2,1)}), bf16[16,128,128]{2,1,0:T(8,128)(2,1)S(1)}, u32[]{:S(2)}, u32[]{:S(2)}) async-start(bf16[16,128,128]{2,1,0:T(8,128)(2,1)} %bitcast.19), calls=%async_computation | async-start | bytes 1048576 | tf_op jit(solution)/shard_map/all_to_all | solution.py:362
  8.9 1.0 %copy-start = (bf16[2048,128]{1,0:T(8,128)(2,1)S(1)}, bf16[2048,128]{1,0:T(8,128)(2,1)}, u32[]{:S(2)}) copy-start(bf16[2048,128]{1,0:T(8,128)(2,1)} %panel_ref.1) | copy-start | bytes 1572868
  17.0 14.9 %collective-permute-start = (f32[1024,128]{1,0:T(8,128)S(1)}, f32[1024,128]{1,0:T(8,128)S(1)}, u32[]{:S(2)}, u32[]{:S(2)}) collective-permute-start(f32[1024,128]{1,0:T(8,128)S(1)} %get-tuple-element.15), channel_id=1, source_target_pairs={{0,1},{1,0},{2,3},{3,2},{4,5},{5,4},{6,7},{7,6},{8,9},{9,8},{10,11... | collective-permute-start | bytes 1572872 | tf_op jit(solution)/shard_map/ppermute | solution.py:301
  17.0 6.7 %collective-permute-start.4 = (bf16[128,128]{1,0:T(8,128)(2,1)S(1)}, bf16[128,128]{1,0:T(8,128)(2,1)S(1)}, u32[]{:S(2)}, u32[]{:S(2)}) collective-permute-start(bf16[128,128]{1,0:T(8,128)(2,1)S(1)} %slice_bitcast_fusion.piece_ref), channel_id=1, source_target_pairs={{0,3},{4,7},{8,11},{12,15},{16,19},{20,23},{24,27},{28,31},{32,35}... | collective-permute-start | bytes 98312 | tf_op jit(solution)/shard_map/ppermute | solution.py:331
  20.9 2.9 %collective-permute-start.3 = (bf16[128,128]{1,0:T(8,128)(2,1)S(1)}, bf16[128,128]{1,0:T(8,128)(2,1)S(1)}, u32[]{:S(2)}, u32[]{:S(2)}) collective-permute-start(bf16[128,128]{1,0:T(8,128)(2,1)S(1)} %slice_bitcast_fusion.piece_ref), channel_id=1, source_target_pairs={{0,2},{4,6},{8,10},{12,14},{16,18},{20,22},{24,26},{28,30},{32,34}... | collective-permute-start | bytes 98312 | tf_op jit(solution)/shard_map/ppermute | solution.py:331
  22.2 2.1 %collective-permute-start.2 = (bf16[128,128]{1,0:T(8,128)(2,1)S(1)}, bf16[128,128]{1,0:T(8,128)(2,1)S(1)}, u32[]{:S(2)}, u32[]{:S(2)}) collective-permute-start(bf16[128,128]{1,0:T(8,128)(2,1)S(1)} %slice_bitcast_fusion.piece_ref), channel_id=1, source_target_pairs={{0,1},{4,5},{8,9},{12,13},{16,17},{20,21},{24,25},{28,29},{32,33},... | collective-permute-start | bytes 98312 | tf_op jit(solution)/shard_map/ppermute | solution.py:331
  25.7 15.9 %all-to-all-start.1 = ((bf16[16,128,128]{2,1,0:T(8,128)(2,1)}), bf16[16,128,128]{2,1,0:T(8,128)(2,1)S(1)}, u32[]{:S(2)}, u32[]{:S(2)}) async-start(bf16[16,128,128]{2,1,0:T(8,128)(2,1)} %shard_map.61), calls=%async_computation.1 | async-start | bytes 1048576 | tf_op jit(solution)/shard_map/all_to_all | solution.py:380
  32.0 9.6 %collective-permute-start.1 = (s16[528,128]{1,0:T(8,128)(2,1)S(1)}, s16[528,128]{1,0:T(8,128)(2,1)S(1)}, u32[]{:S(2)}, u32[]{:S(2)}) collective-permute-start(s16[528,128]{1,0:T(8,128)(2,1)S(1)} %get-tuple-element.17), channel_id=1, source_target_pairs={{0,2},{1,3},{2,0},{3,1},{4,6},{5,7},{6,4},{7,5},{8,10},{9,11},{10,... | collective-permute-start | bytes 405512 | tf_op jit(solution)/shard_map/ppermute | solution.py:301
  46.9 7.9 %collective-permute-start.5 = (s16[528,128]{1,0:T(8,128)(2,1)S(1)}, s16[528,128]{1,0:T(8,128)(2,1)S(1)}, u32[]{:S(2)}, u32[]{:S(2)}) collective-permute-start(s16[528,128]{1,0:T(8,128)(2,1)S(1)} %get-tuple-element.20), channel_id=1, source_target_pairs={{0,64},{64,0},{128,192},{192,128},{1,65},{65,1},{129,193},{193,129... | collective-permute-start | bytes 405512 | tf_op jit(solution)/shard_map/ppermute | solution.py:301
  47.0 12.7 %collective-permute-start.6 = (s16[528,128]{1,0:T(8,128)(2,1)S(1)}, s16[528,128]{1,0:T(8,128)(2,1)S(1)}, u32[]{:S(2)}, u32[]{:S(2)}) collective-permute-start(s16[528,128]{1,0:T(8,128)(2,1)S(1)} %get-tuple-element.21), channel_id=1, source_target_pairs={{0,192},{64,128},{128,64},{192,0},{1,193},{65,129},{129,65},{193,1... | collective-permute-start | bytes 405512 | tf_op jit(solution)/shard_map/ppermute | solution.py:301
  54.9 14.1 %collective-permute-start.9 = (s16[528,128]{1,0:T(8,128)(2,1)S(1)}, s16[528,128]{1,0:T(8,128)(2,1)S(1)}, u32[]{:S(2)}, u32[]{:S(2)}) collective-permute-start(s16[528,128]{1,0:T(8,128)(2,1)S(1)} %shard_map.63.after_ref.own_ref), channel_id=1, source_target_pairs={{0,192},{64,128},{128,64},{192,0},{1,193},{65,129},{129,65},{193,1... | collective-permute-start | bytes 405512 | tf_op jit(solution)/shard_map/ppermute | solution.py:301
  59.8 12.4 %collective-permute-start.7 = (s16[528,128]{1,0:T(8,128)(2,1)S(1)}, s16[528,128]{1,0:T(8,128)(2,1)S(1)}, u32[]{:S(2)}, u32[]{:S(2)}) collective-permute-start(s16[528,128]{1,0:T(8,128)(2,1)S(1)} %shard_map.66.own_ref), channel_id=1, source_target_pairs={{0,64},{64,0},{128,192},{192,128},{1,65},{65,1},{129,193},{193,129... | collective-permute-start | bytes 405512 | tf_op jit(solution)/shard_map/ppermute | solution.py:301
  61.2 16.0 %all-to-all-start.2 = ((f32[16,32,128]{2,1,0:T(8,128)}), f32[16,32,128]{2,1,0:T(8,128)S(1)}, u32[]{:S(2)}, u32[]{:S(2)}) async-start(f32[16,32,128]{2,1,0:T(8,128)} %bitcast.12), calls=%async_computation.2 | async-start | bytes 524288 | tf_op jit(solution)/shard_map/all_to_all | solution.py:385
  69.2 8.6 %collective-permute-start.10 = (s16[528,128]{1,0:T(8,128)(2,1)S(1)}, s16[528,128]{1,0:T(8,128)(2,1)S(1)}, u32[]{:S(2)}, u32[]{:S(2)}) collective-permute-start(s16[528,128]{1,0:T(8,128)(2,1)S(1)} %shard_map.68.own_ref), channel_id=1, source_target_pairs={{0,64},{64,0},{128,192},{192,128},{1,65},{65,1},{129,193},{193,129... | collective-permute-start | bytes 405512 | tf_op jit(solution)/shard_map/ppermute | solution.py:301
  72.4 8.6 %collective-permute-start.8 = (s16[528,128]{1,0:T(8,128)(2,1)S(1)}, s16[528,128]{1,0:T(8,128)(2,1)S(1)}, u32[]{:S(2)}, u32[]{:S(2)}) collective-permute-start(s16[528,128]{1,0:T(8,128)(2,1)S(1)} %shard_map.67.own_ref), channel_id=1, source_target_pairs={{0,192},{64,128},{128,64},{192,0},{1,193},{65,129},{129,65},{193,1... | collective-permute-start | bytes 405512 | tf_op jit(solution)/shard_map/ppermute | solution.py:301

commit v3 on v2

--- a/solution.py
+++ b/solution.py
@@ -94,24 +94,29 @@
     encode(keep_ref[size:, :] + got_ref[size:, :], send_ref)
 
 
-def pack_kernel(bits, piece_ref, got1_ref, got2_ref, got3_ref, out_ref):
-    own = jnp.where(bits[4] == 1, piece_ref[...].astype(jnp.float32), 0.0)
-    rest = got1_ref[...].astype(jnp.float32) + got2_ref[...].astype(jnp.float32)
-    piece = (own + rest + got3_ref[...].astype(jnp.float32)).astype(jnp.bfloat16)
-    for site in range(out_ref.shape[0]):
-        out_ref[site] = piece
-
-
-def rows_kernel(mine_ref, got_ref, after_ref, out_ref):
-    del after_ref
-    out_ref[...] = mine_ref[...] + decode(got_ref)
-
-
-def total_kernel(terms_ref, out_ref):
-    total = terms_ref[0]
-    for site in range(1, terms_ref.shape[0]):
-        total += terms_ref[site]
-    out_ref[...] = total
+def select_kernel(bits, own_ref, got_ref, out_ref):
+    @pl.when(bits[4] == 1)
+    def _():
+        out_ref[...] = own_ref[...]
+
+    @pl.when(bits[4] == 0)
+    def _():
+        out_ref[...] = got_ref[...]
+
+
+def pack_kernel(bits, mine_ref, got_ref, piece_ref, other_ref, out_ref):
+    sites = out_ref.shape[0]
+    size = piece_ref.shape[0]
+    share = mine_ref.shape[0] // sites
+    own = piece_ref[...].astype(jnp.float32)
+    piece = jnp.where(bits[5] == 1, own, other_ref[...].astype(jnp.float32)).astype(jnp.bfloat16)
+    sums = mine_ref[...] + decode(got_ref)
+    high = jnp.clip(sums, -BF16_MOST, BF16_MOST).astype(jnp.bfloat16)
+    low = (sums - high.astype(jnp.float32)).astype(jnp.bfloat16)
+    for site in range(sites):
+        out_ref[site, :size, :] = piece
+        out_ref[site, size : size + share, :] = high[site * share : (site + 1) * share]
+        out_ref[site, size + share :, :] = low[site * share : (site + 1) * share]
 
 
 def block_rows(size):
@@ -151,16 +156,22 @@
 
 
 def col_kernel(
-    info, tiles_ref, slab_ref, after_ref, keep_ref, send0_ref, send1_ref, total, result, held, sems
+    info, tiles_ref, slab_ref, rows_ref, keep_ref, send0_ref, send1_ref, total, result, held, sems
 ):
-    del after_ref
     slots, width, _ = held.shape
     depth = width // STEPS
-    count = depth // slab_ref.shape[1]
+    size, share = slab_ref.shape[1], rows_ref.shape[0]
+    size = size - 2 * share
+    count = depth // size
     fetch = fetch_of(info, tiles_ref, held, sems)
     for index in range(slots * STEPS):
         fetch(index).start()
     total[...] = jnp.zeros_like(total)
+    sums = jnp.zeros(rows_ref.shape, jnp.float32)
+    for site in range(slab_ref.shape[0]):
+        sums += slab_ref[site, size : size + share, :].astype(jnp.float32)
+        sums += slab_ref[site, size + share :, :].astype(jnp.float32)
+    rows_ref[...] = sums
 
     @pl.loop(0, slots * STEPS)
     def _(index):
@@ -170,7 +181,7 @@
         @pl.when(info[2, slot] == 1)
         def _():
             first = (info[0, slot] * STEPS + part) * count
-            source = slab_ref[pl.ds(first, count), :, :].reshape(depth, slab_ref.shape[2])
+            source = slab_ref[pl.ds(first, count), :size, :].reshape(depth, slab_ref.shape[2])
             total[:, cols] += lax.dot_general(
                 source, held[slot, piece, :], (((0,), (0,)), ((), ())),
                 preferred_element_type=jnp.float32,
@@ -278,15 +289,15 @@
     )(info, grm_tiles, panel)
 
 
-def col_products(info, grm_tiles, slab, after):
+def col_products(info, grm_tiles, packed, share):
     slots, width, _ = grm_tiles.shape
-    lanes = slab.shape[2]
+    lanes = packed.shape[2]
     half = width // 2
     return pl.pallas_call(
         col_kernel,
-        in_specs=[SMEM, HBM, VMEM, VMEM],
-        out_specs=[VMEM] * 3,
-        out_shape=[floats(2, half, lanes), coded(half, lanes), coded(half, lanes)],
+        in_specs=[SMEM, HBM, VMEM],
+        out_specs=[VMEM] * 4,
+        out_shape=[floats(share, lanes), floats(2, half, lanes), coded(half, lanes), coded(half, lanes)],
         scratch_shapes=[
             pltpu.VMEM((lanes, CTD * width), jnp.float32),
             pltpu.VMEM((CTD * width, lanes), jnp.float32),
@@ -294,7 +305,7 @@
         + tile_scratch(grm_tiles),
         compiler_params=limit(24),
         cost_estimate=tile_cost(grm_tiles.shape, lanes),
-    )(info, grm_tiles, slab, after)
+    )(info, grm_tiles, packed)
 
 
 def swap(value, axis, flip):
@@ -310,26 +321,13 @@
         small_call(functools.partial(first_kernel, index), outs, keep, got)[0]
         for index, got in enumerate(gots)
     ]
-    begun = owns[0]
     gots = [swap(own, "row", flip[1]) for own, flip in zip(owns, flips)]
     owns = [small_call(second_kernel, outs, own, got)[0] for own, got in zip(owns, gots)]
     gots = [swap(own, "row", flip[2]) for own, flip in zip(owns, flips)]
     result = None
     for index in range(2):
         result = place_half(index, bits, owns[index], gots[index], result)
-    return result, begun
-
-
-def spread(piece, planes):
-    got = []
-    for step in range(1, PLANES):
-        pairs = [
-            ((row * SITES + site) * PLANES + plane, (row * SITES + site) * PLANES + (plane + step) % PLANES)
-            for row, plane in enumerate(planes)
-            for site in range(SITES)
-        ]
-        got.append(lax.ppermute(piece, ("row", "col"), pairs))
-    return got
+    return result
 
 
 def on_device(grm_tiles, tile_row, tile_col, panel):
@@ -350,8 +348,8 @@
     low = (row_index + high) % 2
     core = col_index % 2
     chip = col_index // 2 % 2
-    holds = (col_index % PLANES == (offset + base_row) // CTD % PLANES).astype(jnp.int32)
-    bits = jnp.stack([low, high, core, chip, holds]).astype(jnp.int32)
+    root = (offset + base_row) // CTD
+    bits = jnp.stack([low, high, core, chip, core == root % 2, chip == root // 2 % 2]).astype(jnp.int32)
     info = jnp.stack(
         [local_row, local_col, kind, jnp.pad(bits[:2], (0, 2)), jnp.pad(bits[2:4], (0, 2))]
     ).astype(jnp.int32)
@@ -363,29 +361,24 @@
         panel.reshape(SITES, size, lanes), "col", 0, 0, axis_index_groups=across
     )
     keep, send = row_products(info, tiles, panel)
-    pieces, keep, send = lax.optimization_barrier((pieces, keep, send))
+    pieces, keep = lax.optimization_barrier((pieces, keep))
     half = keep.shape[0] // 2
     share = half // SITES
     mine, send_z = small_call(
         add_kernel, [floats(half, lanes), coded(half, lanes)], keep, swap(send, "col", 1)
     )
     piece = pieces[owners[0] // PLANES]
-    got = spread(piece, [owner % PLANES for owner in owners])
+    outs = [jax.ShapeDtypeStruct((size, lanes), panel.dtype)]
+    piece = small_call(select_kernel, outs, bits, piece, swap(piece, "col", 1), scalars=1)[0]
     packed = small_call(
         pack_kernel,
-        [jax.ShapeDtypeStruct((SITES, size, lanes), jnp.bfloat16)],
-        bits, piece, *got,
+        [jax.ShapeDtypeStruct((SITES, size + 2 * share, lanes), jnp.bfloat16)],
+        bits, mine, swap(send_z, "col", 2), piece, swap(piece, "col", 2),
         scalars=1,
     )[0]
-    slab = lax.all_to_all(packed, "col", 0, 0, axis_index_groups=across)
-    got_z = swap(send_z, "col", 2)
-    keep, *sends = col_products(info, tiles, slab, got_z)
-    y_cols, begun = sum_over_row(bits, keep, sends)
-    rows = small_call(rows_kernel, [floats(half, lanes)], mine, got_z, begun)[0]
-    terms = lax.all_to_all(
-        rows.reshape(SITES, share, lanes), "col", 0, 0, axis_index_groups=across
-    )
-    y_rows = small_call(total_kernel, [floats(share, lanes)], terms)[0]
+    packed = lax.all_to_all(packed, "col", 0, 0, axis_index_groups=across)
+    y_rows, keep, *sends = col_products(info, tiles, packed, share)
+    y_cols = sum_over_row(bits, keep, sends)
     return (y_rows, y_cols)
 
 

time: 82.9 us -> 91.5 us (1.10)
  blocking collectives: 0 us -> 34.1 us
  starting transfers between devices: 48.8 us -> 19.8 us
  waiting for transfers between devices: 13.6 us -> 17.3 us
  Pallas kernels: 17.2 us -> 16.2 us
    all_to_all x0 -> x2, blocking collectives: none -> 34.1 us  [the longest x1 17.4 us: on_device(): lax.all_to_all(panel.reshape(SITES, size, lanes), 'col', 0, 0, axis_index...]
    all_to_all x3 -> x0, starting transfers between devices: 21.3 us -> none  [the longest x1 7.81 us: on_device(): lax.all_to_all(rows.reshape(SITES, share, lanes), 'col', 0, 0, axis_index...]
    ppermute x8 -> x10, waiting for transfers between devices: 3.74 us -> 17.3 us  [swap(): lax.ppermute(value, axis, [(k, k ^ flip) for k in range(lax.axis_size(axi...]
    all_to_all x3 -> x0, waiting for transfers between devices: 9.15 us -> none  [the longest x1 7.78 us: on_device(): slab = lax.all_to_all(packed, 'col', 0, 0, axis_index_groups=across)]
    ppermute x3 -> x0, starting transfers between devices: 6.51 us -> none  [spread(): got.append(lax.ppermute(piece, ('row', 'col'), pairs))]
    pallas_call x8 -> x7, Pallas kernels: 3.46 us -> 1.91 us  [small_call(): pl.pallas_call(kernel, in_specs=[SMEM] * scalars + [VMEM] * (len(args) -...]
    ppermute x8 -> x10, starting transfers between devices: 21 us -> 19.8 us  [swap(): lax.ppermute(value, axis, [(k, k ^ flip) for k in range(lax.axis_size(axi...]
  transfers between devices with their start and end apart: 14 -> 10, of which waited for: 6 -> 7; matrix products, arithmetic and copies ran while one was open for 1% -> 0% of each run, Pallas kernels for 13% -> 3%
where the time goes in v3:
time: 91.5 us; the launch traced here: 90.3 us
  blocking collectives  34.1 us (37%)
  starting transfers between devices  19.8 us (22%)
  waiting for transfers between devices  17.3 us (19%)
  Pallas kernels  16.2 us (18%)
  local copies, waits for them, and re-layouts  1.15 us (1%)
    ppermute x10, starting transfers between devices, swap(): lax.ppermute(value, axis, [(k, k ^ flip) for k in range(lax.axis_size(axi...  19.8 us
    all_to_all x1, blocking collectives, on_device(): lax.all_to_all(panel.reshape(SITES, size, lanes), 'col', 0, 0, axis_index...  17.4 us
    ppermute x10, waiting for transfers between devices, swap(): lax.ppermute(value, axis, [(k, k ^ flip) for k in range(lax.axis_size(axi...  17.3 us
    all_to_all x1, blocking collectives, on_device(): packed = lax.all_to_all(packed, 'col', 0, 0, axis_index_groups=across)  16.7 us
    pallas_call x1, Pallas kernels, col_products(): pl.pallas_call(col_kernel, in_specs=[SMEM, HBM, VMEM], out_specs=[VMEM] *...  5.8 us
    pallas_call x1, Pallas kernels, row_products(): pl.pallas_call(row_kernel, in_specs=[SMEM, HBM, VMEM], out_specs=[VMEM, V...  5.66 us
    pallas_call x2, Pallas kernels, place_half(): pl.pallas_call(functools.partial(place_kernel, index), in_specs=[SMEM, VM...  2.83 us
    pallas_call x7, Pallas kernels, small_call(): pl.pallas_call(kernel, in_specs=[SMEM] * scalars + [VMEM] * (len(args) -...  1.91 us
  transfers between devices with their start and end apart: 10, of which 7 were waited for; matrix products, arithmetic and copies ran while one was open for 0% of the time, Pallas kernels for 3%

profile of v3, /device:TPU:6, one launch (start us, length us, event | category | flops | bytes accessed | tf_op | source)
XLA Modules:
  0.0 90.3 jit_solution(18308042539436078055)
XLA Ops:
  0.8 0.7 fusion
  1.6 1.0 %copy-done = bf16[2048,128]{1,0:T(8,128)(2,1)S(1)} copy-done((bf16[2048,128]{1,0:T(8,128)(2,1)S(1)}, bf16[2048,128]{1,0:T(8,128)(2,1)}, u32[]{:S(2)}) %copy-start) | copy-done | bytes 524312
  2.6 5.7 %shard_map.59 = (f32[1024,128]{1,0:T(8,128)S(1)}, f32[1024,128]{1,0:T(8,128)S(1)}) custom-call(s32[5,4]{1,0:T(8,128)S(1)} %stack.60.info, bf16[4,1024,1024]{2,1,0:T(8,128)(2,1)} %tiles_ref.3, bf16[2048,128]{1,0:T(8,128)(2,1)S(1)} %copy-done), custom_call_target="tpu_custom_call" | custom-call | flops 1073741824 | bytes 10485760 | tf_op jit(solution)/shard_map/pallas_call | solution.py:281
  8.4 17.4 %all_to_all.10 = bf16[16,128,128]{2,1,0:T(8,128)(2,1)S(1)} all-to-all(bf16[16,128,128]{2,1,0:T(8,128)(2,1)S(1)} %bitcast.19), channel_id=1, replica_groups={{0,4,8,12,16,20,24,28,32,36,40,44,48,52,56,60},{1,5,9,13,17,21,25,29,33..., dimensions={0} | all-to-all | bytes 1048576 | tf_op jit(solution)/shard_map/all_to_all | solution.py:360
  25.9 1.3 %collective-permute-start.1 = (s16[528,128]{1,0:T(8,128)(2,1)S(1)}, s16[528,128]{1,0:T(8,128)(2,1)S(1)}, u32[]{:S(2)}, u32[]{:S(2)}) collective-permute-start(s16[528,128]{1,0:T(8,128)(2,1)S(1)} %get-tuple-element.16), channel_id=1, source_target_pairs={{0,2},{1,3},{2,0},{3,1},{4,6},{5,7},{6,4},{7,5},{8,10},{9,11},{10,... | collective-permute-start | bytes 405512 | tf_op jit(solution)/shard_map/ppermute | solution.py:312
  27.4 1.1 %collective-permute-done.2.got_ref = bf16[128,128]{1,0:T(8,128)(2,1)S(1)} collective-permute-done((bf16[128,128]{1,0:T(8,128)(2,1)S(1)}, bf16[128,128]{1,0:T(8,128)(2,1)S(1)}, u32[]{:S(2)}, u32[]{:S(2)}) %collective-permute-start.2) | collective-permute-done | bytes 32800 | tf_op jit(solution)/shard_map/ppermute | solution.py:312
  28.5 0.6 shard_map.61.piece_ref
  29.1 0.9 collective-permute-start.3
  29.9 3.1 %collective-permute-done.3.other_ref = bf16[128,128]{1,0:T(8,128)(2,1)S(1)} collective-permute-done((bf16[128,128]{1,0:T(8,128)(2,1)S(1)}, bf16[128,128]{1,0:T(8,128)(2,1)S(1)}, u32[]{:S(2)}, u32[]{:S(2)}) %collective-permute-start.3) | collective-permute-done | bytes 32800 | tf_op jit(solution)/shard_map/ppermute | solution.py:312
  33.1 0.7 shard_map.62
  33.7 16.7 %all_to_all.11.slab_ref = bf16[16,192,128]{2,1,0:T(8,128)(2,1)S(1)} all-to-all(bf16[16,192,128]{2,1,0:T(8,128)(2,1)S(1)} %shard_map.62), channel_id=1, replica_groups={{0,4,8,12,16,20,24,28,32,36,40,44,48,52,56,60},{1,5,9,13,17,21,25,29,33..., dimensions={0} | all-to-all | bytes 1572864 | tf_op jit(solution)/shard_map/all_to_all | solution.py:379
  50.4 5.8 %shard_map.63 = (f32[32,128]{1,0:T(8,128)}, f32[2,512,128]{2,1,0:T(8,128)S(1)}, s16[528,128]{1,0:T(8,128)(2,1)S(1)}, s16[528,128]{1,0:T(8,128)(2,1)S(1)}) custom-call(s32[5,4]{1,0:T(8,128)S(1)} %stack.60.info, bf16[4,1024,1024]{2,1,0:T(8,128)(2,1)} %tiles_ref.3, bf16[16,192,128]{2,1,0:T(8,128)(2,1)S(1)} %all_to_all.11.slab_ref), custom_call_target="tpu_custom_call" | custom-call | flops 1073741824 | bytes 10485760 | tf_op jit(solution)/shard_map/pallas_call | solution.py:296
  56.2 3.4 %collective-permute-start.7 = (s16[528,128]{1,0:T(8,128)(2,1)S(1)}, s16[528,128]{1,0:T(8,128)(2,1)S(1)}, u32[]{:S(2)}, u32[]{:S(2)}) collective-permute-start(s16[528,128]{1,0:T(8,128)(2,1)S(1)} %get-tuple-element.21), channel_id=1, source_target_pairs={{0,64},{64,0},{128,192},{192,128},{1,65},{65,1},{129,193},{193,129... | collective-permute-start | bytes 405512 | tf_op jit(solution)/shard_map/ppermute | solution.py:312
  59.6 4.3 %collective-permute-start.4 = (s16[528,128]{1,0:T(8,128)(2,1)S(1)}, s16[528,128]{1,0:T(8,128)(2,1)S(1)}, u32[]{:S(2)}, u32[]{:S(2)}) collective-permute-start(s16[528,128]{1,0:T(8,128)(2,1)S(1)} %get-tuple-element.20), channel_id=1, source_target_pairs={{0,192},{64,128},{128,64},{192,0},{1,193},{65,129},{129,65},{193,1... | collective-permute-start | bytes 405512 | tf_op jit(solution)/shard_map/ppermute | solution.py:312
  64.0 4.8 %collective-permute-start.8 = (s16[528,128]{1,0:T(8,128)(2,1)S(1)}, s16[528,128]{1,0:T(8,128)(2,1)S(1)}, u32[]{:S(2)}, u32[]{:S(2)}) collective-permute-start(s16[528,128]{1,0:T(8,128)(2,1)S(1)} %shard_map.66.own_ref), channel_id=1, source_target_pairs={{0,192},{64,128},{128,64},{192,0},{1,193},{65,129},{129,65},{193,1... | collective-permute-start | bytes 405512 | tf_op jit(solution)/shard_map/ppermute | solution.py:312
  68.8 3.1 %collective-permute-done.4.got_ref = s16[528,128]{1,0:T(8,128)(2,1)S(1)} collective-permute-done((s16[528,128]{1,0:T(8,128)(2,1)S(1)}, s16[528,128]{1,0:T(8,128)(2,1)S(1)}, u32[]{:S(2)}, u32[]{:S(2)}) %collective-permute-start.4) | collective-permute-done | bytes 135200 | tf_op jit(solution)/shard_map/ppermute | solution.py:312
  72.1 1.2 %collective-permute-done.8.got_ref = s16[528,128]{1,0:T(8,128)(2,1)S(1)} collective-permute-done((s16[528,128]{1,0:T(8,128)(2,1)S(1)}, s16[528,128]{1,0:T(8,128)(2,1)S(1)}, u32[]{:S(2)}, u32[]{:S(2)}) %collective-permute-start.8) | collective-permute-done | bytes 135200 | tf_op jit(solution)/shard_map/ppermute | solution.py:312
  73.3 0.2 shard_map.67.own_ref
  73.5 1.8 %collective-permute-start.9 = (s16[528,128]{1,0:T(8,128)(2,1)S(1)}, s16[528,128]{1,0:T(8,128)(2,1)S(1)}, u32[]{:S(2)}, u32[]{:S(2)}) collective-permute-start(s16[528,128]{1,0:T(8,128)(2,1)S(1)} %shard_map.67.own_ref), channel_id=1, source_target_pairs={{0,64},{64,0},{128,192},{192,128},{1,65},{65,1},{129,193},{193,129... | collective-permute-start | bytes 405512 | tf_op jit(solution)/shard_map/ppermute | solution.py:312
  75.3 6.2 %collective-permute-done.5.got_ref = s16[528,128]{1,0:T(8,128)(2,1)S(1)} collective-permute-done((s16[528,128]{1,0:T(8,128)(2,1)S(1)}, s16[528,128]{1,0:T(8,128)(2,1)S(1)}, u32[]{:S(2)}, u32[]{:S(2)}) %collective-permute-start.5) | collective-permute-done | bytes 135200 | tf_op jit(solution)/shard_map/ppermute | solution.py:312
  81.6 3.2 %collective-permute-start.6 = (s16[528,128]{1,0:T(8,128)(2,1)S(1)}, s16[528,128]{1,0:T(8,128)(2,1)S(1)}, u32[]{:S(2)}, u32[]{:S(2)}) collective-permute-start(s16[528,128]{1,0:T(8,128)(2,1)S(1)} %shard_map.65.own_ref), channel_id=1, source_target_pairs={{0,192},{64,128},{128,64},{192,0},{1,193},{65,129},{129,65},{193,1... | collective-permute-start | bytes 405512 | tf_op jit(solution)/shard_map/ppermute | solution.py:312
  84.8 1.4 %shard_map.68.refs_0_ = f32[2048,128]{1,0:T(8,128)} custom-call(s32[6]{0:T(128)S(1)} %stack.65.bits, s16[528,128]{1,0:T(8,128)(2,1)S(1)} %shard_map.67.own_ref, s16[528,128]{1,0:T(8,128)(2,1)S(1)} %collective-permute-done.9.got_ref), custom_call_target="tpu_custom_call" | custom-call | tf_op jit(solution)/shard_map/pallas_call | solution.py:242
  86.3 2.6 %collective-permute-done.6.got_ref = s16[528,128]{1,0:T(8,128)(2,1)S(1)} collective-permute-done((s16[528,128]{1,0:T(8,128)(2,1)S(1)}, s16[528,128]{1,0:T(8,128)(2,1)S(1)}, u32[]{:S(2)}, u32[]{:S(2)}) %collective-permute-start.6) | collective-permute-done | bytes 135200 | tf_op jit(solution)/shard_map/ppermute | solution.py:312
  88.8 1.4 %shard_map.69 = f32[2048,128]{1,0:T(8,128)} custom-call(s32[6]{0:T(128)S(1)} %stack.65.bits, s16[528,128]{1,0:T(8,128)(2,1)S(1)} %shard_map.65.own_ref, s16[528,128]{1,0:T(8,128)(2,1)S(1)} %collective-permute-done.6.got_ref, f32[2048,128]{1,0:T(8,128)} %shard_map.68.refs_0_), custom_call_target="tpu_custom_call", output_to_operand_aliasing={{}: (3, {})} | custom-call | tf_op jit(solution)/shard_map/pallas_call | solution.py:242
  (18 shorter events, 1.0 us)
Async XLA Ops:
  1.5 1.0 %copy-start = (bf16[2048,128]{1,0:T(8,128)(2,1)S(1)}, bf16[2048,128]{1,0:T(8,128)(2,1)}, u32[]{:S(2)}) copy-start(bf16[2048,128]{1,0:T(8,128)(2,1)} %panel_ref.1) | copy-start | bytes 1572868
  8.3 17.6 %collective-permute-start = (f32[1024,128]{1,0:T(8,128)S(1)}, f32[1024,128]{1,0:T(8,128)S(1)}, u32[]{:S(2)}, u32[]{:S(2)}) collective-permute-start(f32[1024,128]{1,0:T(8,128)S(1)} %get-tuple-element.14), channel_id=1, source_target_pairs={{0,1},{1,0},{2,3},{3,2},{4,5},{5,4},{6,7},{7,6},{8,9},{9,8},{10,11... | collective-permute-start | bytes 1572872 | tf_op jit(solution)/shard_map/ppermute | solution.py:312
  25.9 7.1 %collective-permute-start.1 = (s16[528,128]{1,0:T(8,128)(2,1)S(1)}, s16[528,128]{1,0:T(8,128)(2,1)S(1)}, u32[]{:S(2)}, u32[]{:S(2)}) collective-permute-start(s16[528,128]{1,0:T(8,128)(2,1)S(1)} %get-tuple-element.16), channel_id=1, source_target_pairs={{0,2},{1,3},{2,0},{3,1},{4,6},{5,7},{6,4},{7,5},{8,10},{9,11},{10,... | collective-permute-start | bytes 405512 | tf_op jit(solution)/shard_map/ppermute | solution.py:312
  27.3 1.2 %collective-permute-start.2 = (bf16[128,128]{1,0:T(8,128)(2,1)S(1)}, bf16[128,128]{1,0:T(8,128)(2,1)S(1)}, u32[]{:S(2)}, u32[]{:S(2)}) collective-permute-start(bf16[128,128]{1,0:T(8,128)(2,1)S(1)} %slice_bitcast_fusion.own_ref), channel_id=1, source_target_pairs={{0,1},{1,0},{2,3},{3,2},{4,5},{5,4},{6,7},{7,6},{8,9},{9,8},{10,11... | collective-permute-start | bytes 98312 | tf_op jit(solution)/shard_map/ppermute | solution.py:312
  29.1 4.0 %collective-permute-start.3 = (bf16[128,128]{1,0:T(8,128)(2,1)S(1)}, bf16[128,128]{1,0:T(8,128)(2,1)S(1)}, u32[]{:S(2)}, u32[]{:S(2)}) collective-permute-start(bf16[128,128]{1,0:T(8,128)(2,1)S(1)} %shard_map.61.piece_ref), channel_id=1, source_target_pairs={{0,2},{1,3},{2,0},{3,1},{4,6},{5,7},{6,4},{7,5},{8,10},{9,11},{10,... | collective-permute-start | bytes 98312 | tf_op jit(solution)/shard_map/ppermute | solution.py:312
  56.2 7.7 %collective-permute-start.7 = (s16[528,128]{1,0:T(8,128)(2,1)S(1)}, s16[528,128]{1,0:T(8,128)(2,1)S(1)}, u32[]{:S(2)}, u32[]{:S(2)}) collective-permute-start(s16[528,128]{1,0:T(8,128)(2,1)S(1)} %get-tuple-element.21), channel_id=1, source_target_pairs={{0,64},{64,0},{128,192},{192,128},{1,65},{65,1},{129,193},{193,129... | collective-permute-start | bytes 405512 | tf_op jit(solution)/shard_map/ppermute | solution.py:312
  59.6 12.3 %collective-permute-start.4 = (s16[528,128]{1,0:T(8,128)(2,1)S(1)}, s16[528,128]{1,0:T(8,128)(2,1)S(1)}, u32[]{:S(2)}, u32[]{:S(2)}) collective-permute-start(s16[528,128]{1,0:T(8,128)(2,1)S(1)} %get-tuple-element.20), channel_id=1, source_target_pairs={{0,192},{64,128},{128,64},{192,0},{1,193},{65,129},{129,65},{193,1... | collective-permute-start | bytes 405512 | tf_op jit(solution)/shard_map/ppermute | solution.py:312
  64.0 9.3 %collective-permute-start.8 = (s16[528,128]{1,0:T(8,128)(2,1)S(1)}, s16[528,128]{1,0:T(8,128)(2,1)S(1)}, u32[]{:S(2)}, u32[]{:S(2)}) collective-permute-start(s16[528,128]{1,0:T(8,128)(2,1)S(1)} %shard_map.66.own_ref), channel_id=1, source_target_pairs={{0,192},{64,128},{128,64},{192,0},{1,193},{65,129},{129,65},{193,1... | collective-permute-start | bytes 405512 | tf_op jit(solution)/shard_map/ppermute | solution.py:312
  72.0 9.5 %collective-permute-start.5 = (s16[528,128]{1,0:T(8,128)(2,1)S(1)}, s16[528,128]{1,0:T(8,128)(2,1)S(1)}, u32[]{:S(2)}, u32[]{:S(2)}) collective-permute-start(s16[528,128]{1,0:T(8,128)(2,1)S(1)} %shard_map.64.own_ref), channel_id=1, source_target_pairs={{0,64},{64,0},{128,192},{192,128},{1,65},{65,1},{129,193},{193,129... | collective-permute-start | bytes 405512 | tf_op jit(solution)/shard_map/ppermute | solution.py:312
  73.5 11.4 %collective-permute-start.9 = (s16[528,128]{1,0:T(8,128)(2,1)S(1)}, s16[528,128]{1,0:T(8,128)(2,1)S(1)}, u32[]{:S(2)}, u32[]{:S(2)}) collective-permute-start(s16[528,128]{1,0:T(8,128)(2,1)S(1)} %shard_map.67.own_ref), channel_id=1, source_target_pairs={{0,64},{64,0},{128,192},{192,128},{1,65},{65,1},{129,193},{193,129... | collective-permute-start | bytes 405512 | tf_op jit(solution)/shard_map/ppermute | solution.py:312
  81.6 7.2 %collective-permute-start.6 = (s16[528,128]{1,0:T(8,128)(2,1)S(1)}, s16[528,128]{1,0:T(8,128)(2,1)S(1)}, u32[]{:S(2)}, u32[]{:S(2)}) collective-permute-start(s16[528,128]{1,0:T(8,128)(2,1)S(1)} %shard_map.65.own_ref), channel_id=1, source_target_pairs={{0,192},{64,128},{128,64},{192,0},{1,193},{65,129},{129,65},{193,1... | collective-permute-start | bytes 405512 | tf_op jit(solution)/shard_map/ppermute | solution.py:312

commit v4 on v2

--- a/solution.py
+++ b/solution.py
@@ -94,10 +94,19 @@
     encode(keep_ref[size:, :] + got_ref[size:, :], send_ref)
 
 
-def pack_kernel(bits, piece_ref, got1_ref, got2_ref, got3_ref, out_ref):
-    own = jnp.where(bits[4] == 1, piece_ref[...].astype(jnp.float32), 0.0)
-    rest = got1_ref[...].astype(jnp.float32) + got2_ref[...].astype(jnp.float32)
-    piece = (own + rest + got3_ref[...].astype(jnp.float32)).astype(jnp.bfloat16)
+def select_kernel(bits, own_ref, got_ref, out_ref):
+    @pl.when(bits[4] == 1)
+    def _():
+        out_ref[...] = own_ref[...]
+
+    @pl.when(bits[4] == 0)
+    def _():
+        out_ref[...] = got_ref[...]
+
+
+def pack_kernel(bits, piece_ref, other_ref, out_ref):
+    own = piece_ref[...].astype(jnp.float32)
+    piece = jnp.where(bits[5] == 1, own, other_ref[...].astype(jnp.float32)).astype(jnp.bfloat16)
     for site in range(out_ref.shape[0]):
         out_ref[site] = piece
 
@@ -320,18 +329,6 @@
     return result, begun
 
 
-def spread(piece, planes):
-    got = []
-    for step in range(1, PLANES):
-        pairs = [
-            ((row * SITES + site) * PLANES + plane, (row * SITES + site) * PLANES + (plane + step) % PLANES)
-            for row, plane in enumerate(planes)
-            for site in range(SITES)
-        ]
-        got.append(lax.ppermute(piece, ("row", "col"), pairs))
-    return got
-
-
 def on_device(grm_tiles, tile_row, tile_col, panel):
     row_index = lax.axis_index("row")
     col_index = lax.axis_index("col")
@@ -350,8 +347,8 @@
     low = (row_index + high) % 2
     core = col_index % 2
     chip = col_index // 2 % 2
-    holds = (col_index % PLANES == (offset + base_row) // CTD % PLANES).astype(jnp.int32)
-    bits = jnp.stack([low, high, core, chip, holds]).astype(jnp.int32)
+    root = (offset + base_row) // CTD
+    bits = jnp.stack([low, high, core, chip, core == root % 2, chip == root // 2 % 2]).astype(jnp.int32)
     info = jnp.stack(
         [local_row, local_col, kind, jnp.pad(bits[:2], (0, 2)), jnp.pad(bits[2:4], (0, 2))]
     ).astype(jnp.int32)
@@ -370,11 +367,12 @@
         add_kernel, [floats(half, lanes), coded(half, lanes)], keep, swap(send, "col", 1)
     )
     piece = pieces[owners[0] // PLANES]
-    got = spread(piece, [owner % PLANES for owner in owners])
+    outs = [jax.ShapeDtypeStruct((size, lanes), panel.dtype)]
+    piece = small_call(select_kernel, outs, bits, piece, swap(piece, "col", 1), scalars=1)[0]
     packed = small_call(
         pack_kernel,
         [jax.ShapeDtypeStruct((SITES, size, lanes), jnp.bfloat16)],
-        bits, piece, *got,
+        bits, piece, swap(piece, "col", 2),
         scalars=1,
     )[0]
     slab = lax.all_to_all(packed, "col", 0, 0, axis_index_groups=across)

time: 82.9 us -> 82.8 us (level)
  the two profiles are of different devices: /device:TPU:6 before, /device:TPU:32 now
where the time goes in v4:
time: 82.8 us; the launch traced here: 82.4 us
  starting transfers between devices  39.7 us (48%)
  waiting for transfers between devices  22.2 us (27%)
  Pallas kernels  17.7 us (21%)
  local copies, waits for them, and re-layouts  1.15 us (1%)
  other arithmetic  0.83 us (1%)
    ppermute x10, starting transfers between devices, swap(): lax.ppermute(value, axis, [(k, k ^ flip) for k in range(lax.axis_size(axi...  25.6 us
    all_to_all x1, waiting for transfers between devices, on_device(): slab = lax.all_to_all(packed, 'col', 0, 0, axis_index_groups=across)  10.6 us
    ppermute x10, waiting for transfers between devices, swap(): lax.ppermute(value, axis, [(k, k ^ flip) for k in range(lax.axis_size(axi...  7.6 us
    all_to_all x1, starting transfers between devices, on_device(): lax.all_to_all(panel.reshape(SITES, size, lanes), 'col', 0, 0, axis_index...  7.05 us
    pallas_call x1, Pallas kernels, row_products(): pl.pallas_call(row_kernel, in_specs=[SMEM, HBM, VMEM], out_specs=[VMEM, V...  5.64 us
    pallas_call x1, Pallas kernels, col_products(): pl.pallas_call(col_kernel, in_specs=[SMEM, HBM, VMEM, VMEM], out_specs=[V...  5.26 us
    pallas_call x9, Pallas kernels, small_call(): pl.pallas_call(kernel, in_specs=[SMEM] * scalars + [VMEM] * (len(args) -...  4.01 us
    all_to_all x1, waiting for transfers between devices, on_device(): lax.all_to_all(panel.reshape(SITES, size, lanes), 'col', 0, 0, axis_index...  3.96 us
  transfers between devices with their start and end apart: 13, of which 6 were waited for; matrix products, arithmetic and copies ran while one was open for 1% of the time, Pallas kernels for 13%

profile of v4, /device:TPU:32, one launch (start us, length us, event | category | flops | bytes accessed | tf_op | source)
XLA Modules:
  0.0 82.4 jit_solution(3921810421147103021)
XLA Ops:
  0.6 7.0 %all-to-all-start = ((bf16[16,128,128]{2,1,0:T(8,128)(2,1)}), bf16[16,128,128]{2,1,0:T(8,128)(2,1)S(1)}, u32[]{:S(2)}, u32[]{:S(2)}) async-start(bf16[16,128,128]{2,1,0:T(8,128)(2,1)} %bitcast.20), calls=%async_computation | async-start | bytes 1048576 | tf_op jit(solution)/shard_map/all_to_all | solution.py:359
  7.9 0.7 fusion
  8.6 1.0 %copy-done = bf16[2048,128]{1,0:T(8,128)(2,1)S(1)} copy-done((bf16[2048,128]{1,0:T(8,128)(2,1)S(1)}, bf16[2048,128]{1,0:T(8,128)(2,1)}, u32[]{:S(2)}) %copy-start) | copy-done | bytes 524312
  9.6 5.6 %shard_map.59 = (f32[1024,128]{1,0:T(8,128)S(1)}, f32[1024,128]{1,0:T(8,128)S(1)}) custom-call(s32[5,4]{1,0:T(8,128)S(1)} %stack.60.info, bf16[4,1024,1024]{2,1,0:T(8,128)(2,1)} %tiles_ref.3, bf16[2048,128]{1,0:T(8,128)(2,1)S(1)} %copy-done), custom_call_target="tpu_custom_call" | custom-call | flops 1073741824 | bytes 10485760 | tf_op jit(solution)/shard_map/pallas_call | solution.py:279
  15.3 4.0 %all-to-all-done = bf16[16,128,128]{2,1,0:T(8,128)(2,1)S(1)} async-done(((bf16[16,128,128]{2,1,0:T(8,128)(2,1)}), bf16[16,128,128]{2,1,0:T(8,128)(2,1)S(1)}, u32[]{:S(2)}, u32[]{:S(2)}) %all-to-all-start) | async-done | bytes 524320 | tf_op jit(solution)/shard_map/all_to_all | solution.py:359
  19.8 1.4 %collective-permute-done.2.got_ref = bf16[128,128]{1,0:T(8,128)(2,1)S(1)} collective-permute-done((bf16[128,128]{1,0:T(8,128)(2,1)S(1)}, bf16[128,128]{1,0:T(8,128)(2,1)S(1)}, u32[]{:S(2)}, u32[]{:S(2)}) %collective-permute-start.2) | collective-permute-done | bytes 32800 | tf_op jit(solution)/shard_map/ppermute | solution.py:310
  21.2 0.6 shard_map.61.piece_ref
  21.9 3.8 %collective-permute-done.3.other_ref = bf16[128,128]{1,0:T(8,128)(2,1)S(1)} collective-permute-done((bf16[128,128]{1,0:T(8,128)(2,1)S(1)}, bf16[128,128]{1,0:T(8,128)(2,1)S(1)}, u32[]{:S(2)}, u32[]{:S(2)}) %collective-permute-start.3) | collective-permute-done | bytes 32800 | tf_op jit(solution)/shard_map/ppermute | solution.py:310
  25.7 1.4 %shard_map.62 = bf16[16,128,128]{2,1,0:T(8,128)(2,1)} custom-call(s32[6]{0:T(128)S(1)} %stack.65.bits, bf16[128,128]{1,0:T(8,128)(2,1)S(1)} %shard_map.61.piece_ref, bf16[128,128]{1,0:T(8,128)(2,1)S(1)} %collective-permute-done.3.other_ref), custom_call_target="tpu_custom_call" | custom-call | tf_op jit(solution)/shard_map/pallas_call | solution.py:228
  27.1 3.6 %all-to-all-start.1 = ((bf16[16,128,128]{2,1,0:T(8,128)(2,1)}), bf16[16,128,128]{2,1,0:T(8,128)(2,1)S(1)}, u32[]{:S(2)}, u32[]{:S(2)}) async-start(bf16[16,128,128]{2,1,0:T(8,128)(2,1)} %shard_map.62), calls=%async_computation.1 | async-start | bytes 1048576 | tf_op jit(solution)/shard_map/all_to_all | solution.py:378
  31.0 10.6 %all-to-all-done.1.slab_ref = bf16[16,128,128]{2,1,0:T(8,128)(2,1)S(1)} async-done(((bf16[16,128,128]{2,1,0:T(8,128)(2,1)}), bf16[16,128,128]{2,1,0:T(8,128)(2,1)S(1)}, u32[]{:S(2)}, u32[]{:S(2)}) %all-to-all-start.1) | async-done | bytes 524320 | tf_op jit(solution)/shard_map/all_to_all | solution.py:378
  41.6 5.3 %shard_map.63 = (f32[2,512,128]{2,1,0:T(8,128)S(1)}, s16[528,128]{1,0:T(8,128)(2,1)S(1)}, s16[528,128]{1,0:T(8,128)(2,1)S(1)}) custom-call(s32[5,4]{1,0:T(8,128)S(1)} %stack.60.info, bf16[4,1024,1024]{2,1,0:T(8,128)(2,1)} %tiles_ref.3, bf16[16,128,128]{2,1,0:T(8,128)(2,1)S(1)} %all-to-all-done.1.slab_ref, ...), custom_call_target="tpu_custom_call" | custom-call | flops 1073741824 | bytes 10485760 | tf_op jit(solution)/shard_map/pallas_call | solution.py:294
  46.9 3.4 %collective-permute-start.4 = (s16[528,128]{1,0:T(8,128)(2,1)S(1)}, s16[528,128]{1,0:T(8,128)(2,1)S(1)}, u32[]{:S(2)}, u32[]{:S(2)}) collective-permute-start(s16[528,128]{1,0:T(8,128)(2,1)S(1)} %get-tuple-element.20), channel_id=1, source_target_pairs={{0,64},{64,0},{128,192},{192,128},{1,65},{65,1},{129,193},{193,129... | collective-permute-start | bytes 405512 | tf_op jit(solution)/shard_map/ppermute | solution.py:310
  50.3 3.6 %collective-permute-start.5 = (s16[528,128]{1,0:T(8,128)(2,1)S(1)}, s16[528,128]{1,0:T(8,128)(2,1)S(1)}, u32[]{:S(2)}, u32[]{:S(2)}) collective-permute-start(s16[528,128]{1,0:T(8,128)(2,1)S(1)} %get-tuple-element.21), channel_id=1, source_target_pairs={{0,192},{64,128},{128,64},{192,0},{1,193},{65,129},{129,65},{193,1... | collective-permute-start | bytes 405512 | tf_op jit(solution)/shard_map/ppermute | solution.py:310
  54.3 5.6 %collective-permute-start.8 = (s16[528,128]{1,0:T(8,128)(2,1)S(1)}, s16[528,128]{1,0:T(8,128)(2,1)S(1)}, u32[]{:S(2)}, u32[]{:S(2)}) collective-permute-start(s16[528,128]{1,0:T(8,128)(2,1)S(1)} %shard_map.64.after_ref.own_ref), channel_id=1, source_target_pairs={{0,192},{64,128},{128,64},{192,0},{1,193},{65,129},{129,65},{193,1... | collective-permute-start | bytes 405512 | tf_op jit(solution)/shard_map/ppermute | solution.py:310
  60.0 1.7 %collective-permute-start.6 = (s16[528,128]{1,0:T(8,128)(2,1)S(1)}, s16[528,128]{1,0:T(8,128)(2,1)S(1)}, u32[]{:S(2)}, u32[]{:S(2)}) collective-permute-start(s16[528,128]{1,0:T(8,128)(2,1)S(1)} %shard_map.67.own_ref), channel_id=1, source_target_pairs={{0,64},{64,0},{128,192},{192,128},{1,65},{65,1},{129,193},{193,129... | collective-permute-start | bytes 405512 | tf_op jit(solution)/shard_map/ppermute | solution.py:310
  61.7 0.8 shard_map.65
  62.4 3.5 %all-to-all-start.2 = ((f32[16,32,128]{2,1,0:T(8,128)}), f32[16,32,128]{2,1,0:T(8,128)S(1)}, u32[]{:S(2)}, u32[]{:S(2)}) async-start(f32[16,32,128]{2,1,0:T(8,128)} %bitcast.13), calls=%async_computation.2 | async-start | bytes 524288 | tf_op jit(solution)/shard_map/all_to_all | solution.py:383
  66.1 1.6 %collective-permute-start.9 = (s16[528,128]{1,0:T(8,128)(2,1)S(1)}, s16[528,128]{1,0:T(8,128)(2,1)S(1)}, u32[]{:S(2)}, u32[]{:S(2)}) collective-permute-start(s16[528,128]{1,0:T(8,128)(2,1)S(1)} %shard_map.69.own_ref), channel_id=1, source_target_pairs={{0,64},{64,0},{128,192},{192,128},{1,65},{65,1},{129,193},{193,129... | collective-permute-start | bytes 405512 | tf_op jit(solution)/shard_map/ppermute | solution.py:310
  67.9 8.9 %collective-permute-start.7 = (s16[528,128]{1,0:T(8,128)(2,1)S(1)}, s16[528,128]{1,0:T(8,128)(2,1)S(1)}, u32[]{:S(2)}, u32[]{:S(2)}) collective-permute-start(s16[528,128]{1,0:T(8,128)(2,1)S(1)} %shard_map.68.own_ref), channel_id=1, source_target_pairs={{0,192},{64,128},{128,64},{192,0},{1,193},{65,129},{129,65},{193,1... | collective-permute-start | bytes 405512 | tf_op jit(solution)/shard_map/ppermute | solution.py:310
  76.8 0.6 shard_map.66
  77.4 1.4 %shard_map.70.refs_0_ = f32[2048,128]{1,0:T(8,128)} custom-call(s32[6]{0:T(128)S(1)} %stack.65.bits, s16[528,128]{1,0:T(8,128)(2,1)S(1)} %shard_map.69.own_ref, s16[528,128]{1,0:T(8,128)(2,1)S(1)} %collective-permute-done.9.got_ref), custom_call_target="tpu_custom_call" | custom-call | tf_op jit(solution)/shard_map/pallas_call | solution.py:240
  78.9 2.1 %collective-permute-done.7.got_ref = s16[528,128]{1,0:T(8,128)(2,1)S(1)} collective-permute-done((s16[528,128]{1,0:T(8,128)(2,1)S(1)}, s16[528,128]{1,0:T(8,128)(2,1)S(1)}, u32[]{:S(2)}, u32[]{:S(2)}) %collective-permute-start.7) | collective-permute-done | bytes 135200 | tf_op jit(solution)/shard_map/ppermute | solution.py:310
  81.0 1.4 %shard_map.71 = f32[2048,128]{1,0:T(8,128)} custom-call(s32[6]{0:T(128)S(1)} %stack.65.bits, s16[528,128]{1,0:T(8,128)(2,1)S(1)} %shard_map.68.own_ref, s16[528,128]{1,0:T(8,128)(2,1)S(1)} %collective-permute-done.7.got_ref, f32[2048,128]{1,0:T(8,128)} %shard_map.70.refs_0_), custom_call_target="tpu_custom_call", output_to_operand_aliasing={{}: (3, {})} | custom-call | tf_op jit(solution)/shard_map/pallas_call | solution.py:240
  (24 shorter events, 2.2 us)
Async XLA Ops:
  0.6 18.6 %all-to-all-start = ((bf16[16,128,128]{2,1,0:T(8,128)(2,1)}), bf16[16,128,128]{2,1,0:T(8,128)(2,1)S(1)}, u32[]{:S(2)}, u32[]{:S(2)}) async-start(bf16[16,128,128]{2,1,0:T(8,128)(2,1)} %bitcast.20), calls=%async_computation | async-start | bytes 1048576 | tf_op jit(solution)/shard_map/all_to_all | solution.py:359
  8.6 1.0 %copy-start = (bf16[2048,128]{1,0:T(8,128)(2,1)S(1)}, bf16[2048,128]{1,0:T(8,128)(2,1)}, u32[]{:S(2)}) copy-start(bf16[2048,128]{1,0:T(8,128)(2,1)} %panel_ref.1) | copy-start | bytes 1572868
  19.2 11.5 %collective-permute-start = (f32[1024,128]{1,0:T(8,128)S(1)}, f32[1024,128]{1,0:T(8,128)S(1)}, u32[]{:S(2)}, u32[]{:S(2)}) collective-permute-start(f32[1024,128]{1,0:T(8,128)S(1)} %get-tuple-element.15), channel_id=1, source_target_pairs={{0,1},{1,0},{2,3},{3,2},{4,5},{5,4},{6,7},{7,6},{8,9},{9,8},{10,11... | collective-permute-start | bytes 1572872 | tf_op jit(solution)/shard_map/ppermute | solution.py:310
  19.2 2.0 %collective-permute-start.2 = (bf16[128,128]{1,0:T(8,128)(2,1)S(1)}, bf16[128,128]{1,0:T(8,128)(2,1)S(1)}, u32[]{:S(2)}, u32[]{:S(2)}) collective-permute-start(bf16[128,128]{1,0:T(8,128)(2,1)S(1)} %slice_bitcast_fusion.own_ref), channel_id=1, source_target_pairs={{0,1},{1,0},{2,3},{3,2},{4,5},{5,4},{6,7},{7,6},{8,9},{9,8},{10,11... | collective-permute-start | bytes 98312 | tf_op jit(solution)/shard_map/ppermute | solution.py:310
  21.7 4.0 %collective-permute-start.3 = (bf16[128,128]{1,0:T(8,128)(2,1)S(1)}, bf16[128,128]{1,0:T(8,128)(2,1)S(1)}, u32[]{:S(2)}, u32[]{:S(2)}) collective-permute-start(bf16[128,128]{1,0:T(8,128)(2,1)S(1)} %shard_map.61.piece_ref), channel_id=1, source_target_pairs={{0,2},{1,3},{2,0},{3,1},{4,6},{5,7},{6,4},{7,5},{8,10},{9,11},{10,... | collective-permute-start | bytes 98312 | tf_op jit(solution)/shard_map/ppermute | solution.py:310
  27.1 14.5 %all-to-all-start.1 = ((bf16[16,128,128]{2,1,0:T(8,128)(2,1)}), bf16[16,128,128]{2,1,0:T(8,128)(2,1)S(1)}, u32[]{:S(2)}, u32[]{:S(2)}) async-start(bf16[16,128,128]{2,1,0:T(8,128)(2,1)} %shard_map.62), calls=%async_computation.1 | async-start | bytes 1048576 | tf_op jit(solution)/shard_map/all_to_all | solution.py:378
  30.9 10.8 %collective-permute-start.1 = (s16[528,128]{1,0:T(8,128)(2,1)S(1)}, s16[528,128]{1,0:T(8,128)(2,1)S(1)}, u32[]{:S(2)}, u32[]{:S(2)}) collective-permute-start(s16[528,128]{1,0:T(8,128)(2,1)S(1)} %get-tuple-element.17), channel_id=1, source_target_pairs={{0,2},{1,3},{2,0},{3,1},{4,6},{5,7},{6,4},{7,5},{8,10},{9,11},{10,... | collective-permute-start | bytes 405512 | tf_op jit(solution)/shard_map/ppermute | solution.py:310
  46.9 7.3 %collective-permute-start.4 = (s16[528,128]{1,0:T(8,128)(2,1)S(1)}, s16[528,128]{1,0:T(8,128)(2,1)S(1)}, u32[]{:S(2)}, u32[]{:S(2)}) collective-permute-start(s16[528,128]{1,0:T(8,128)(2,1)S(1)} %get-tuple-element.20), channel_id=1, source_target_pairs={{0,64},{64,0},{128,192},{192,128},{1,65},{65,1},{129,193},{193,129... | collective-permute-start | bytes 405512 | tf_op jit(solution)/shard_map/ppermute | solution.py:310
  50.3 9.6 %collective-permute-start.5 = (s16[528,128]{1,0:T(8,128)(2,1)S(1)}, s16[528,128]{1,0:T(8,128)(2,1)S(1)}, u32[]{:S(2)}, u32[]{:S(2)}) collective-permute-start(s16[528,128]{1,0:T(8,128)(2,1)S(1)} %get-tuple-element.21), channel_id=1, source_target_pairs={{0,192},{64,128},{128,64},{192,0},{1,193},{65,129},{129,65},{193,1... | collective-permute-start | bytes 405512 | tf_op jit(solution)/shard_map/ppermute | solution.py:310
  54.3 11.7 %collective-permute-start.8 = (s16[528,128]{1,0:T(8,128)(2,1)S(1)}, s16[528,128]{1,0:T(8,128)(2,1)S(1)}, u32[]{:S(2)}, u32[]{:S(2)}) collective-permute-start(s16[528,128]{1,0:T(8,128)(2,1)S(1)} %shard_map.64.after_ref.own_ref), channel_id=1, source_target_pairs={{0,192},{64,128},{128,64},{192,0},{1,193},{65,129},{129,65},{193,1... | collective-permute-start | bytes 405512 | tf_op jit(solution)/shard_map/ppermute | solution.py:310
  60.0 7.7 %collective-permute-start.6 = (s16[528,128]{1,0:T(8,128)(2,1)S(1)}, s16[528,128]{1,0:T(8,128)(2,1)S(1)}, u32[]{:S(2)}, u32[]{:S(2)}) collective-permute-start(s16[528,128]{1,0:T(8,128)(2,1)S(1)} %shard_map.67.own_ref), channel_id=1, source_target_pairs={{0,64},{64,0},{128,192},{192,128},{1,65},{65,1},{129,193},{193,129... | collective-permute-start | bytes 405512 | tf_op jit(solution)/shard_map/ppermute | solution.py:310
  62.4 14.4 %all-to-all-start.2 = ((f32[16,32,128]{2,1,0:T(8,128)}), f32[16,32,128]{2,1,0:T(8,128)S(1)}, u32[]{:S(2)}, u32[]{:S(2)}) async-start(f32[16,32,128]{2,1,0:T(8,128)} %bitcast.13), calls=%async_computation.2 | async-start | bytes 524288 | tf_op jit(solution)/shard_map/all_to_all | solution.py:383
  66.1 11.3 %collective-permute-start.9 = (s16[528,128]{1,0:T(8,128)(2,1)S(1)}, s16[528,128]{1,0:T(8,128)(2,1)S(1)}, u32[]{:S(2)}, u32[]{:S(2)}) collective-permute-start(s16[528,128]{1,0:T(8,128)(2,1)S(1)} %shard_map.69.own_ref), channel_id=1, source_target_pairs={{0,64},{64,0},{128,192},{192,128},{1,65},{65,1},{129,193},{193,129... | collective-permute-start | bytes 405512 | tf_op jit(solution)/shard_map/ppermute | solution.py:310
  67.9 13.1 %collective-permute-start.7 = (s16[528,128]{1,0:T(8,128)(2,1)S(1)}, s16[528,128]{1,0:T(8,128)(2,1)S(1)}, u32[]{:S(2)}, u32[]{:S(2)}) collective-permute-start(s16[528,128]{1,0:T(8,128)(2,1)S(1)} %shard_map.68.own_ref), channel_id=1, source_target_pairs={{0,192},{64,128},{128,64},{192,0},{1,193},{65,129},{129,65},{193,1... | collective-permute-start | bytes 405512 | tf_op jit(solution)/shard_map/ppermute | solution.py:310

commit v5 on v4

--- a/solution.py
+++ b/solution.py
@@ -94,21 +94,10 @@
     encode(keep_ref[size:, :] + got_ref[size:, :], send_ref)
 
 
-def select_kernel(bits, own_ref, got_ref, out_ref):
-    @pl.when(bits[4] == 1)
-    def _():
-        out_ref[...] = own_ref[...]
-
-    @pl.when(bits[4] == 0)
-    def _():
-        out_ref[...] = got_ref[...]
-
-
-def pack_kernel(bits, piece_ref, other_ref, out_ref):
-    own = piece_ref[...].astype(jnp.float32)
-    piece = jnp.where(bits[5] == 1, own, other_ref[...].astype(jnp.float32)).astype(jnp.bfloat16)
-    for site in range(out_ref.shape[0]):
-        out_ref[site] = piece
+def pack_kernel(bits, pieces_ref, out_ref):
+    piece = pieces_ref[bits[4]]
+    for index in range(out_ref.shape[0]):
+        out_ref[index] = piece
 
 
 def rows_kernel(mine_ref, got_ref, after_ref, out_ref):
@@ -160,16 +149,18 @@
 
 
 def col_kernel(
-    info, tiles_ref, slab_ref, after_ref, keep_ref, send0_ref, send1_ref, total, result, held, sems
+    info, tiles_ref, near_ref, far_ref, keep_ref, send0_ref, send1_ref, slab, total, result, held, sems
 ):
-    del after_ref
     slots, width, _ = held.shape
     depth = width // STEPS
-    count = depth // slab_ref.shape[1]
     fetch = fetch_of(info, tiles_ref, held, sems)
     for index in range(slots * STEPS):
         fetch(index).start()
     total[...] = jnp.zeros_like(total)
+    core = info[4, 0]
+    for ref, tile in ((near_ref, core), (far_ref, 1 - core)):
+        rows = pl.ds(pl.multiple_of(tile * width, width), width)
+        slab[rows, :] = ref[...].reshape(width, slab.shape[1])
 
     @pl.loop(0, slots * STEPS)
     def _(index):
@@ -178,10 +169,8 @@
 
         @pl.when(info[2, slot] == 1)
         def _():
-            first = (info[0, slot] * STEPS + part) * count
-            source = slab_ref[pl.ds(first, count), :, :].reshape(depth, slab_ref.shape[2])
             total[:, cols] += lax.dot_general(
-                source, held[slot, piece, :], (((0,), (0,)), ((), ())),
+                slab[rows, :], held[slot, piece, :], (((0,), (0,)), ((), ())),
                 preferred_element_type=jnp.float32,
             )
 
@@ -287,9 +276,9 @@
     )(info, grm_tiles, panel)
 
 
-def col_products(info, grm_tiles, slab, after):
+def col_products(info, grm_tiles, near, far):
     slots, width, _ = grm_tiles.shape
-    lanes = slab.shape[2]
+    lanes = near.shape[2]
     half = width // 2
     return pl.pallas_call(
         col_kernel,
@@ -297,13 +286,14 @@
         out_specs=[VMEM] * 3,
         out_shape=[floats(2, half, lanes), coded(half, lanes), coded(half, lanes)],
         scratch_shapes=[
+            pltpu.VMEM((RT_DEV * width, lanes), near.dtype),
             pltpu.VMEM((lanes, CTD * width), jnp.float32),
             pltpu.VMEM((CTD * width, lanes), jnp.float32),
         ]
         + tile_scratch(grm_tiles),
         compiler_params=limit(24),
         cost_estimate=tile_cost(grm_tiles.shape, lanes),
-    )(info, grm_tiles, slab, after)
+    )(info, grm_tiles, near, far)
 
 
 def swap(value, axis, flip):
@@ -348,16 +338,19 @@
     core = col_index % 2
     chip = col_index // 2 % 2
     root = (offset + base_row) // CTD
-    bits = jnp.stack([low, high, core, chip, core == root % 2, chip == root // 2 % 2]).astype(jnp.int32)
+    chips = col_count // 2
+    bits = jnp.stack([low, high, core, chip, root % 2 * chips + root // 2]).astype(jnp.int32)
     info = jnp.stack(
         [local_row, local_col, kind, jnp.pad(bits[:2], (0, 2)), jnp.pad(bits[2:4], (0, 2))]
     ).astype(jnp.int32)
 
     across = [[site * PLANES + plane for site in range(SITES)] for plane in range(PLANES)]
     tiles = pltpu.with_memory_space_constraint(grm_tiles, pltpu.HBM)
-    size = panel.shape[0] // SITES
+    one_core = [[chip * 2 + core for chip in range(chips)] for core in range(2)]
+    size = panel.shape[0] // col_count
     pieces = lax.all_to_all(
-        panel.reshape(SITES, size, lanes), "col", 0, 0, axis_index_groups=across
+        panel.reshape(col_count, size, lanes), "col", 0, 0,
+        axis_index_groups=[one_core[0] + one_core[1]],
     )
     keep, send = row_products(info, tiles, panel)
     pieces, keep, send = lax.optimization_barrier((pieces, keep, send))
@@ -366,18 +359,16 @@
     mine, send_z = small_call(
         add_kernel, [floats(half, lanes), coded(half, lanes)], keep, swap(send, "col", 1)
     )
-    piece = pieces[owners[0] // PLANES]
-    outs = [jax.ShapeDtypeStruct((size, lanes), panel.dtype)]
-    piece = small_call(select_kernel, outs, bits, piece, swap(piece, "col", 1), scalars=1)[0]
     packed = small_call(
         pack_kernel,
-        [jax.ShapeDtypeStruct((SITES, size, lanes), jnp.bfloat16)],
-        bits, piece, swap(piece, "col", 2),
+        [jax.ShapeDtypeStruct((chips, size, lanes), panel.dtype)],
+        bits, pieces,
         scalars=1,
     )[0]
-    slab = lax.all_to_all(packed, "col", 0, 0, axis_index_groups=across)
-    got_z = swap(send_z, "col", 2)
-    keep, *sends = col_products(info, tiles, slab, got_z)
+    near = lax.all_to_all(packed, "col", 0, 0, axis_index_groups=one_core)
+    near, got_z = lax.optimization_barrier((near, swap(send_z, "col", 2)))
+    far = swap(near, "col", 1)
+    keep, *sends = col_products(info, tiles, near, far)
     y_cols, begun = sum_over_row(bits, keep, sends)
     rows = small_call(rows_kernel, [floats(half, lanes)], mine, got_z, begun)[0]
     terms = lax.all_to_all(

time: 82.8 us -> 80.1 us (0.967)
  the two profiles are of different devices: /device:TPU:32 before, /device:TPU:6 now
where the time goes in v5:
time: 80.1 us; the launch traced here: 79.7 us
  starting transfers between devices  42.1 us (53%)
  waiting for transfers between devices  17.9 us (22%)
  Pallas kernels  17.1 us (21%)
  local copies, waits for them, and re-layouts  1.15 us (1%)
  other arithmetic  0.83 us (1%)
    ppermute x9, starting transfers between devices, swap(): lax.ppermute(value, axis, [(k, k ^ flip) for k in range(lax.axis_size(axi...  19.6 us
    all_to_all x1, starting transfers between devices, on_device(): lax.all_to_all(panel.reshape(col_count, size, lanes), 'col', 0, 0, axis_i...  9.33 us
    all_to_all x1, starting transfers between devices, on_device(): lax.all_to_all(rows.reshape(SITES, share, lanes), 'col', 0, 0, axis_index...  7.49 us
    ppermute x9, waiting for transfers between devices, swap(): lax.ppermute(value, axis, [(k, k ^ flip) for k in range(lax.axis_size(axi...  6.87 us
    all_to_all x1, waiting for transfers between devices, on_device(): near = lax.all_to_all(packed, 'col', 0, 0, axis_index_groups=one_core)  6.43 us
    all_to_all x1, starting transfers between devices, on_device(): near = lax.all_to_all(packed, 'col', 0, 0, axis_index_groups=one_core)  5.68 us
    pallas_call x1, Pallas kernels, row_products(): pl.pallas_call(row_kernel, in_specs=[SMEM, HBM, VMEM], out_specs=[VMEM, V...  5.64 us
    pallas_call x1, Pallas kernels, col_products(): pl.pallas_call(col_kernel, in_specs=[SMEM, HBM, VMEM, VMEM], out_specs=[V...  5.25 us
  transfers between devices with their start and end apart: 12, of which 8 were waited for; matrix products, arithmetic and copies ran while one was open for 1% of the time, Pallas kernels for 13%

profile of v5, /device:TPU:6, one launch (start us, length us, event | category | flops | bytes accessed | tf_op | source)
XLA Modules:
  0.0 79.7 jit_solution(5238611065035538041)
XLA Ops:
  0.6 9.3 %all-to-all-start = ((bf16[64,32,128]{2,1,0:T(8,128)(2,1)}), bf16[64,32,128]{2,1,0:T(8,128)(2,1)S(1)}, u32[]{:S(2)}, u32[]{:S(2)}) async-start(bf16[64,32,128]{2,1,0:T(8,128)(2,1)} %bitcast.17), calls=%async_computation | async-start | bytes 1048576 | tf_op jit(solution)/shard_map/all_to_all | solution.py:351
  10.2 0.7 fusion
  10.9 1.0 %copy-done = bf16[2048,128]{1,0:T(8,128)(2,1)S(1)} copy-done((bf16[2048,128]{1,0:T(8,128)(2,1)S(1)}, bf16[2048,128]{1,0:T(8,128)(2,1)}, u32[]{:S(2)}) %copy-start) | copy-done | bytes 524312
  11.9 5.6 %shard_map.59 = (f32[1024,128]{1,0:T(8,128)S(1)}, f32[1024,128]{1,0:T(8,128)S(1)}) custom-call(s32[5,4]{1,0:T(8,128)S(1)} %stack.51.info, bf16[4,1024,1024]{2,1,0:T(8,128)(2,1)} %tiles_ref.3, bf16[2048,128]{1,0:T(8,128)(2,1)S(1)} %copy-done), custom_call_target="tpu_custom_call" | custom-call | flops 1073741824 | bytes 10485760 | tf_op jit(solution)/shard_map/pallas_call | solution.py:268
  17.6 3.4 %all-to-all-done.pieces_ref = bf16[64,32,128]{2,1,0:T(8,128)(2,1)S(1)} async-done(((bf16[64,32,128]{2,1,0:T(8,128)(2,1)}), bf16[64,32,128]{2,1,0:T(8,128)(2,1)S(1)}, u32[]{:S(2)}, u32[]{:S(2)}) %all-to-all-start) | async-done | bytes 524320 | tf_op jit(solution)/shard_map/all_to_all | solution.py:351
  21.2 1.3 %shard_map.61 = bf16[32,32,128]{2,1,0:T(8,128)(2,1)} custom-call(s32[5]{0:T(128)S(1)} %stack.53.bits, bf16[64,32,128]{2,1,0:T(8,128)(2,1)S(1)} %all-to-all-done.pieces_ref), custom_call_target="tpu_custom_call" | custom-call | tf_op jit(solution)/shard_map/pallas_call | solution.py:217
  22.5 5.7 %all-to-all-start.1 = ((bf16[32,32,128]{2,1,0:T(8,128)(2,1)}), bf16[32,32,128]{2,1,0:T(8,128)(2,1)S(1)}, u32[]{:S(2)}, u32[]{:S(2)}) async-start(bf16[32,32,128]{2,1,0:T(8,128)(2,1)} %shard_map.61), calls=%async_computation.1 | async-start | bytes 524288 | tf_op jit(solution)/shard_map/all_to_all | solution.py:368
  28.3 1.6 %collective-permute-start.1 = (s16[528,128]{1,0:T(8,128)(2,1)S(1)}, s16[528,128]{1,0:T(8,128)(2,1)S(1)}, u32[]{:S(2)}, u32[]{:S(2)}) collective-permute-start(s16[528,128]{1,0:T(8,128)(2,1)S(1)} %get-tuple-element.20), channel_id=1, source_target_pairs={{0,2},{1,3},{2,0},{3,1},{4,6},{5,7},{6,4},{7,5},{8,10},{9,11},{10,... | collective-permute-start | bytes 405512 | tf_op jit(solution)/shard_map/ppermute | solution.py:300
  29.9 6.4 %all-to-all-done.1.near_ref = bf16[32,32,128]{2,1,0:T(8,128)(2,1)S(1)} async-done(((bf16[32,32,128]{2,1,0:T(8,128)(2,1)}), bf16[32,32,128]{2,1,0:T(8,128)(2,1)S(1)}, u32[]{:S(2)}, u32[]{:S(2)}) %all-to-all-start.1) | async-done | bytes 262176 | tf_op jit(solution)/shard_map/all_to_all | solution.py:368
  36.5 1.5 %collective-permute-done.2.far_ref = bf16[32,32,128]{2,1,0:T(8,128)(2,1)S(1)} collective-permute-done((bf16[32,32,128]{2,1,0:T(8,128)(2,1)S(1)}, bf16[32,32,128]{2,1,0:T(8,128)(2,1)S(1)}, u32[]{:S(2)}, u32[]{:S(2)}) %collective-permute-start.2) | collective-permute-done | bytes 262176 | tf_op jit(solution)/shard_map/ppermute | solution.py:300
  38.1 5.2 %shard_map.62 = (f32[2,512,128]{2,1,0:T(8,128)S(1)}, s16[528,128]{1,0:T(8,128)(2,1)S(1)}, s16[528,128]{1,0:T(8,128)(2,1)S(1)}) custom-call(s32[5,4]{1,0:T(8,128)S(1)} %stack.51.info, bf16[4,1024,1024]{2,1,0:T(8,128)(2,1)} %tiles_ref.3, bf16[32,32,128]{2,1,0:T(8,128)(2,1)S(1)} %all-to-all-done.1.near_ref, bf16[32,32,128]{2,1,0:T(8,128)(2,1)S(1)} %collective-permute-done.2.far_ref), custom_call_target="tpu_custom_call" | custom-call | flops 1073741824 | bytes 10485760 | tf_op jit(solution)/shard_map/pallas_call | solution.py:283
  43.3 3.4 %collective-permute-start.3 = (s16[528,128]{1,0:T(8,128)(2,1)S(1)}, s16[528,128]{1,0:T(8,128)(2,1)S(1)}, u32[]{:S(2)}, u32[]{:S(2)}) collective-permute-start(s16[528,128]{1,0:T(8,128)(2,1)S(1)} %get-tuple-element.24), channel_id=1, source_target_pairs={{0,64},{64,0},{128,192},{192,128},{1,65},{65,1},{129,193},{193,129... | collective-permute-start | bytes 405512 | tf_op jit(solution)/shard_map/ppermute | solution.py:300
  46.7 3.6 %collective-permute-start.4 = (s16[528,128]{1,0:T(8,128)(2,1)S(1)}, s16[528,128]{1,0:T(8,128)(2,1)S(1)}, u32[]{:S(2)}, u32[]{:S(2)}) collective-permute-start(s16[528,128]{1,0:T(8,128)(2,1)S(1)} %get-tuple-element.25), channel_id=1, source_target_pairs={{0,192},{64,128},{128,64},{192,0},{1,193},{65,129},{129,65},{193,1... | collective-permute-start | bytes 405512 | tf_op jit(solution)/shard_map/ppermute | solution.py:300
  50.2 3.3 %collective-permute-done.3.got_ref = s16[528,128]{1,0:T(8,128)(2,1)S(1)} collective-permute-done((s16[528,128]{1,0:T(8,128)(2,1)S(1)}, s16[528,128]{1,0:T(8,128)(2,1)S(1)}, u32[]{:S(2)}, u32[]{:S(2)}) %collective-permute-start.3) | collective-permute-done | bytes 135200 | tf_op jit(solution)/shard_map/ppermute | solution.py:300
  53.7 2.6 %collective-permute-start.7 = (s16[528,128]{1,0:T(8,128)(2,1)S(1)}, s16[528,128]{1,0:T(8,128)(2,1)S(1)}, u32[]{:S(2)}, u32[]{:S(2)}) collective-permute-start(s16[528,128]{1,0:T(8,128)(2,1)S(1)} %shard_map.63.after_ref.own_ref), channel_id=1, source_target_pairs={{0,192},{64,128},{128,64},{192,0},{1,193},{65,129},{129,65},{193,1... | collective-permute-start | bytes 405512 | tf_op jit(solution)/shard_map/ppermute | solution.py:300
  56.4 3.5 %collective-permute-start.5 = (s16[528,128]{1,0:T(8,128)(2,1)S(1)}, s16[528,128]{1,0:T(8,128)(2,1)S(1)}, u32[]{:S(2)}, u32[]{:S(2)}) collective-permute-start(s16[528,128]{1,0:T(8,128)(2,1)S(1)} %shard_map.66.own_ref), channel_id=1, source_target_pairs={{0,64},{64,0},{128,192},{192,128},{1,65},{65,1},{129,193},{193,129... | collective-permute-start | bytes 405512 | tf_op jit(solution)/shard_map/ppermute | solution.py:300
  59.9 0.8 shard_map.64
  60.7 7.5 %all-to-all-start.2 = ((f32[16,32,128]{2,1,0:T(8,128)}), f32[16,32,128]{2,1,0:T(8,128)S(1)}, u32[]{:S(2)}, u32[]{:S(2)}) async-start(f32[16,32,128]{2,1,0:T(8,128)} %bitcast.11), calls=%async_computation.2 | async-start | bytes 524288 | tf_op jit(solution)/shard_map/all_to_all | solution.py:374
  68.3 1.5 %collective-permute-start.8 = (s16[528,128]{1,0:T(8,128)(2,1)S(1)}, s16[528,128]{1,0:T(8,128)(2,1)S(1)}, u32[]{:S(2)}, u32[]{:S(2)}) collective-permute-start(s16[528,128]{1,0:T(8,128)(2,1)S(1)} %shard_map.68.own_ref), channel_id=1, source_target_pairs={{0,64},{64,0},{128,192},{192,128},{1,65},{65,1},{129,193},{193,129... | collective-permute-start | bytes 405512 | tf_op jit(solution)/shard_map/ppermute | solution.py:300
  70.0 3.3 %collective-permute-start.6 = (s16[528,128]{1,0:T(8,128)(2,1)S(1)}, s16[528,128]{1,0:T(8,128)(2,1)S(1)}, u32[]{:S(2)}, u32[]{:S(2)}) collective-permute-start(s16[528,128]{1,0:T(8,128)(2,1)S(1)} %shard_map.67.own_ref), channel_id=1, source_target_pairs={{0,192},{64,128},{128,64},{192,0},{1,193},{65,129},{129,65},{193,1... | collective-permute-start | bytes 405512 | tf_op jit(solution)/shard_map/ppermute | solution.py:300
  73.3 1.2 %all-to-all-done.2.terms_ref = f32[16,32,128]{2,1,0:T(8,128)S(1)} async-done(((f32[16,32,128]{2,1,0:T(8,128)}), f32[16,32,128]{2,1,0:T(8,128)S(1)}, u32[]{:S(2)}, u32[]{:S(2)}) %all-to-all-start.2) | async-done | bytes 262176 | tf_op jit(solution)/shard_map/all_to_all | solution.py:374
  75.3 1.4 %shard_map.69.refs_0_ = f32[2048,128]{1,0:T(8,128)} custom-call(s32[5]{0:T(128)S(1)} %stack.53.bits, s16[528,128]{1,0:T(8,128)(2,1)S(1)} %shard_map.68.own_ref, s16[528,128]{1,0:T(8,128)(2,1)S(1)} %collective-permute-done.8.got_ref), custom_call_target="tpu_custom_call" | custom-call | tf_op jit(solution)/shard_map/pallas_call | solution.py:229
  76.7 1.6 %collective-permute-done.6.got_ref = s16[528,128]{1,0:T(8,128)(2,1)S(1)} collective-permute-done((s16[528,128]{1,0:T(8,128)(2,1)S(1)}, s16[528,128]{1,0:T(8,128)(2,1)S(1)}, u32[]{:S(2)}, u32[]{:S(2)}) %collective-permute-start.6) | collective-permute-done | bytes 135200 | tf_op jit(solution)/shard_map/ppermute | solution.py:300
  78.3 1.4 %shard_map.70 = f32[2048,128]{1,0:T(8,128)} custom-call(s32[5]{0:T(128)S(1)} %stack.53.bits, s16[528,128]{1,0:T(8,128)(2,1)S(1)} %shard_map.67.own_ref, s16[528,128]{1,0:T(8,128)(2,1)S(1)} %collective-permute-done.6.got_ref, f32[2048,128]{1,0:T(8,128)} %shard_map.69.refs_0_), custom_call_target="tpu_custom_call", output_to_operand_aliasing={{}: (3, {})} | custom-call | tf_op jit(solution)/shard_map/pallas_call | solution.py:229
  (20 shorter events, 2.1 us)
Async XLA Ops:
  0.6 20.3 %all-to-all-start = ((bf16[64,32,128]{2,1,0:T(8,128)(2,1)}), bf16[64,32,128]{2,1,0:T(8,128)(2,1)S(1)}, u32[]{:S(2)}, u32[]{:S(2)}) async-start(bf16[64,32,128]{2,1,0:T(8,128)(2,1)} %bitcast.17), calls=%async_computation | async-start | bytes 1048576 | tf_op jit(solution)/shard_map/all_to_all | solution.py:351
  10.9 1.0 %copy-start = (bf16[2048,128]{1,0:T(8,128)(2,1)S(1)}, bf16[2048,128]{1,0:T(8,128)(2,1)}, u32[]{:S(2)}) copy-start(bf16[2048,128]{1,0:T(8,128)(2,1)} %panel_ref.1) | copy-start | bytes 1572868
  20.9 7.2 %collective-permute-start = (f32[1024,128]{1,0:T(8,128)S(1)}, f32[1024,128]{1,0:T(8,128)S(1)}, u32[]{:S(2)}, u32[]{:S(2)}) collective-permute-start(f32[1024,128]{1,0:T(8,128)S(1)} %get-tuple-element.17), channel_id=1, source_target_pairs={{0,1},{1,0},{2,3},{3,2},{4,5},{5,4},{6,7},{7,6},{8,9},{9,8},{10,11... | collective-permute-start | bytes 1572872 | tf_op jit(solution)/shard_map/ppermute | solution.py:300
  22.5 13.8 %all-to-all-start.1 = ((bf16[32,32,128]{2,1,0:T(8,128)(2,1)}), bf16[32,32,128]{2,1,0:T(8,128)(2,1)S(1)}, u32[]{:S(2)}, u32[]{:S(2)}) async-start(bf16[32,32,128]{2,1,0:T(8,128)(2,1)} %shard_map.61), calls=%async_computation.1 | async-start | bytes 524288 | tf_op jit(solution)/shard_map/all_to_all | solution.py:368
  28.3 8.2 %collective-permute-start.1 = (s16[528,128]{1,0:T(8,128)(2,1)S(1)}, s16[528,128]{1,0:T(8,128)(2,1)S(1)}, u32[]{:S(2)}, u32[]{:S(2)}) collective-permute-start(s16[528,128]{1,0:T(8,128)(2,1)S(1)} %get-tuple-element.20), channel_id=1, source_target_pairs={{0,2},{1,3},{2,0},{3,1},{4,6},{5,7},{6,4},{7,5},{8,10},{9,11},{10,... | collective-permute-start | bytes 405512 | tf_op jit(solution)/shard_map/ppermute | solution.py:300
  36.5 1.5 %collective-permute-start.2 = (bf16[32,32,128]{2,1,0:T(8,128)(2,1)S(1)}, bf16[32,32,128]{2,1,0:T(8,128)(2,1)S(1)}, u32[]{:S(2)}, u32[]{:S(2)}) collective-permute-start(bf16[32,32,128]{2,1,0:T(8,128)(2,1)S(1)} %all-to-all-done.1.near_ref), channel_id=1, source_target_pairs={{0,1},{1,0},{2,3},{3,2},{4,5},{5,4},{6,7},{7,6},{8,9},{9,8},{10,11... | collective-permute-start | bytes 786440 | tf_op jit(solution)/shard_map/ppermute | solution.py:300
  43.3 10.2 %collective-permute-start.3 = (s16[528,128]{1,0:T(8,128)(2,1)S(1)}, s16[528,128]{1,0:T(8,128)(2,1)S(1)}, u32[]{:S(2)}, u32[]{:S(2)}) collective-permute-start(s16[528,128]{1,0:T(8,128)(2,1)S(1)} %get-tuple-element.24), channel_id=1, source_target_pairs={{0,64},{64,0},{128,192},{192,128},{1,65},{65,1},{129,193},{193,129... | collective-permute-start | bytes 405512 | tf_op jit(solution)/shard_map/ppermute | solution.py:300
  46.7 9.6 %collective-permute-start.4 = (s16[528,128]{1,0:T(8,128)(2,1)S(1)}, s16[528,128]{1,0:T(8,128)(2,1)S(1)}, u32[]{:S(2)}, u32[]{:S(2)}) collective-permute-start(s16[528,128]{1,0:T(8,128)(2,1)S(1)} %get-tuple-element.25), channel_id=1, source_target_pairs={{0,192},{64,128},{128,64},{192,0},{1,193},{65,129},{129,65},{193,1... | collective-permute-start | bytes 405512 | tf_op jit(solution)/shard_map/ppermute | solution.py:300
  53.7 14.5 %collective-permute-start.7 = (s16[528,128]{1,0:T(8,128)(2,1)S(1)}, s16[528,128]{1,0:T(8,128)(2,1)S(1)}, u32[]{:S(2)}, u32[]{:S(2)}) collective-permute-start(s16[528,128]{1,0:T(8,128)(2,1)S(1)} %shard_map.63.after_ref.own_ref), channel_id=1, source_target_pairs={{0,192},{64,128},{128,64},{192,0},{1,193},{65,129},{129,65},{193,1... | collective-permute-start | bytes 405512 | tf_op jit(solution)/shard_map/ppermute | solution.py:300
  56.4 13.4 %collective-permute-start.5 = (s16[528,128]{1,0:T(8,128)(2,1)S(1)}, s16[528,128]{1,0:T(8,128)(2,1)S(1)}, u32[]{:S(2)}, u32[]{:S(2)}) collective-permute-start(s16[528,128]{1,0:T(8,128)(2,1)S(1)} %shard_map.66.own_ref), channel_id=1, source_target_pairs={{0,64},{64,0},{128,192},{192,128},{1,65},{65,1},{129,193},{193,129... | collective-permute-start | bytes 405512 | tf_op jit(solution)/shard_map/ppermute | solution.py:300
  60.7 13.8 %all-to-all-start.2 = ((f32[16,32,128]{2,1,0:T(8,128)}), f32[16,32,128]{2,1,0:T(8,128)S(1)}, u32[]{:S(2)}, u32[]{:S(2)}) async-start(f32[16,32,128]{2,1,0:T(8,128)} %bitcast.11), calls=%async_computation.2 | async-start | bytes 524288 | tf_op jit(solution)/shard_map/all_to_all | solution.py:374
  68.3 6.9 %collective-permute-start.8 = (s16[528,128]{1,0:T(8,128)(2,1)S(1)}, s16[528,128]{1,0:T(8,128)(2,1)S(1)}, u32[]{:S(2)}, u32[]{:S(2)}) collective-permute-start(s16[528,128]{1,0:T(8,128)(2,1)S(1)} %shard_map.68.own_ref), channel_id=1, source_target_pairs={{0,64},{64,0},{128,192},{192,128},{1,65},{65,1},{129,193},{193,129... | collective-permute-start | bytes 405512 | tf_op jit(solution)/shard_map/ppermute | solution.py:300
  70.0 8.4 %collective-permute-start.6 = (s16[528,128]{1,0:T(8,128)(2,1)S(1)}, s16[528,128]{1,0:T(8,128)(2,1)S(1)}, u32[]{:S(2)}, u32[]{:S(2)}) collective-permute-start(s16[528,128]{1,0:T(8,128)(2,1)S(1)} %shard_map.67.own_ref), channel_id=1, source_target_pairs={{0,192},{64,128},{128,64},{192,0},{1,193},{65,129},{129,65},{193,1... | collective-permute-start | bytes 405512 | tf_op jit(solution)/shard_map/ppermute | solution.py:300

commit v6 on v5

--- a/solution.py
+++ b/solution.py
@@ -92,12 +92,6 @@
     size = mine_ref.shape[0]
     mine_ref[...] = keep_ref[:size, :] + got_ref[:size, :]
     encode(keep_ref[size:, :] + got_ref[size:, :], send_ref)
-
-
-def pack_kernel(bits, pieces_ref, out_ref):
-    piece = pieces_ref[bits[4]]
-    for index in range(out_ref.shape[0]):
-        out_ref[index] = piece
 
 
 def rows_kernel(mine_ref, got_ref, after_ref, out_ref):
@@ -192,14 +186,13 @@
     encode(decode(own_ref) + decode(got_ref), out_ref)
 
 
-def place_kernel(index, bits, own_ref, got_ref, *refs):
+def place_kernel(index, far, bits, half_ref, *refs):
     out_ref, held, sem = refs[-3:]
-    size = own_ref.shape[0] - PAD
-    mine = pl.multiple_of(bits[index] * size, size)
-    other = pl.multiple_of((1 - bits[index]) * size, size)
-    held[pl.ds(mine, size), :] = decode(own_ref)
-    held[pl.ds(other, size), :] = decode(got_ref)
-    copy = pltpu.make_async_copy(held, out_ref.at[pl.ds(index * 2 * size, 2 * size)], sem)
+    size = held.shape[0]
+    held[...] = decode(half_ref)
+    side = 1 - bits[index] if far else bits[index]
+    first = pl.multiple_of((index * 2 + side) * size, size)
+    copy = pltpu.make_async_copy(held, out_ref.at[pl.ds(first, size)], sem)
     copy.start()
     copy.wait()
 
@@ -223,16 +216,16 @@
     )(*args)
 
 
-def place_half(index, bits, own, got, result):
-    size, lanes = own.shape[0] - PAD, own.shape[1]
-    args = (bits, own, got) + (() if result is None else (result,))
+def place_half(index, far, bits, half, result):
+    size, lanes = half.shape[0] - PAD, half.shape[1]
+    args = (bits, half) + (() if result is None else (result,))
     return pl.pallas_call(
-        functools.partial(place_kernel, index),
-        in_specs=[SMEM, VMEM, VMEM] + [HBM] * (len(args) - 3),
+        functools.partial(place_kernel, index, far),
+        in_specs=[SMEM, VMEM] + [HBM] * (len(args) - 2),
         out_specs=HBM,
         out_shape=floats(4 * size, lanes),
-        scratch_shapes=[pltpu.VMEM((2 * size, lanes), jnp.float32), pltpu.SemaphoreType.DMA],
-        input_output_aliases={} if result is None else {3: 0},
+        scratch_shapes=[pltpu.VMEM((size, lanes), jnp.float32), pltpu.SemaphoreType.DMA],
+        input_output_aliases={} if result is None else {2: 0},
         compiler_params=limit(6),
     )(*args)
 
@@ -314,8 +307,9 @@
     owns = [small_call(second_kernel, outs, own, got)[0] for own, got in zip(owns, gots)]
     gots = [swap(own, "row", flip[2]) for own, flip in zip(owns, flips)]
     result = None
-    for index in range(2):
-        result = place_half(index, bits, owns[index], gots[index], result)
+    for far, halves in enumerate((owns, gots)):
+        for index, half in enumerate(halves):
+            result = place_half(index, far, bits, half, result)
     return result, begun
 
 
@@ -339,7 +333,7 @@
     chip = col_index // 2 % 2
     root = (offset + base_row) // CTD
     chips = col_count // 2
-    bits = jnp.stack([low, high, core, chip, root % 2 * chips + root // 2]).astype(jnp.int32)
+    bits = jnp.stack([low, high, core, chip]).astype(jnp.int32)
     info = jnp.stack(
         [local_row, local_col, kind, jnp.pad(bits[:2], (0, 2)), jnp.pad(bits[2:4], (0, 2))]
     ).astype(jnp.int32)
@@ -359,12 +353,9 @@
     mine, send_z = small_call(
         add_kernel, [floats(half, lanes), coded(half, lanes)], keep, swap(send, "col", 1)
     )
-    packed = small_call(
-        pack_kernel,
-        [jax.ShapeDtypeStruct((chips, size, lanes), panel.dtype)],
-        bits, pieces,
-        scalars=1,
-    )[0]
+    place = root % 2 * chips + root // 2
+    piece = lax.dynamic_index_in_dim(pieces, place, 0)
+    packed = jnp.broadcast_to(piece, (chips, size, lanes))
     near = lax.all_to_all(packed, "col", 0, 0, axis_index_groups=one_core)
     near, got_z = lax.optimization_barrier((near, swap(send_z, "col", 2)))
     far = swap(near, "col", 1)

time: 80.1 us -> 79.8 us (level)
  waiting for transfers between devices: 17.9 us -> 16.6 us
  Pallas kernels: 17.1 us -> 18.1 us
  starting transfers between devices: 42.1 us -> 41.1 us
    pallas_call x2 -> x4, Pallas kernels: 2.83 us -> 5.16 us  [place_half(): pl.pallas_call(functools.partial(place_kernel, index, far), in_specs=[SME...]
    pallas_call x8 -> x7, Pallas kernels: 3.34 us -> 2.05 us  [small_call(): pl.pallas_call(kernel, in_specs=[SMEM] * scalars + [VMEM] * (len(args) -...]
    all_to_all x1, waiting for transfers between devices: 1.18 us -> 0.01 us  [on_device(): lax.all_to_all(rows.reshape(SITES, share, lanes), 'col', 0, 0, axis_index...]
    ppermute x9, starting transfers between devices: 19.6 us -> 18.6 us  [swap(): lax.ppermute(value, axis, [(k, k ^ flip) for k in range(lax.axis_size(axi...]
  transfers between devices with their start and end apart: 12 -> 12, of which waited for: 8 -> 6; matrix products, arithmetic and copies ran while one was open for 1% -> 2% of each run, Pallas kernels for 13% -> 15%
where the time goes in v6:
time: 79.8 us; the launch traced here: 79.4 us
  starting transfers between devices  41.1 us (52%)
  Pallas kernels  18.1 us (23%)
  waiting for transfers between devices  16.6 us (21%)
  local copies, waits for them, and re-layouts  1.81 us (2%)
  other arithmetic  0.9 us (1%)
  between operations  0.81 us (1%)
    ppermute x9, starting transfers between devices, swap(): lax.ppermute(value, axis, [(k, k ^ flip) for k in range(lax.axis_size(axi...  18.6 us
    all_to_all x1, starting transfers between devices, on_device(): lax.all_to_all(panel.reshape(col_count, size, lanes), 'col', 0, 0, axis_i...  9.33 us
    all_to_all x1, starting transfers between devices, on_device(): lax.all_to_all(rows.reshape(SITES, share, lanes), 'col', 0, 0, axis_index...  7.5 us
    ppermute x9, waiting for transfers between devices, swap(): lax.ppermute(value, axis, [(k, k ^ flip) for k in range(lax.axis_size(axi...  6.83 us
    all_to_all x1, waiting for transfers between devices, on_device(): near = lax.all_to_all(packed, 'col', 0, 0, axis_index_groups=one_core)  6.43 us
    all_to_all x1, starting transfers between devices, on_device(): near = lax.all_to_all(packed, 'col', 0, 0, axis_index_groups=one_core)  5.68 us
    pallas_call x1, Pallas kernels, row_products(): pl.pallas_call(row_kernel, in_specs=[SMEM, HBM, VMEM], out_specs=[VMEM, V...  5.64 us
    pallas_call x1, Pallas kernels, col_products(): pl.pallas_call(col_kernel, in_specs=[SMEM, HBM, VMEM, VMEM], out_specs=[V...  5.24 us
  transfers between devices with their start and end apart: 12, of which 6 were waited for; matrix products, arithmetic and copies ran while one was open for 2% of the time, Pallas kernels for 15%

profile of v6, /device:TPU:6, one launch (start us, length us, event | category | flops | bytes accessed | tf_op | source)
XLA Modules:
  0.0 79.4 jit_solution(944152449109591246)
XLA Ops:
  0.6 9.3 %all-to-all-start = ((bf16[64,32,128]{2,1,0:T(8,128)(2,1)}), bf16[64,32,128]{2,1,0:T(8,128)(2,1)S(1)}, u32[]{:S(2)}, u32[]{:S(2)}) async-start(bf16[64,32,128]{2,1,0:T(8,128)(2,1)} %bitcast.18), calls=%async_computation | async-start | bytes 1048576 | tf_op jit(solution)/shard_map/all_to_all | solution.py:345
  10.9 1.0 %copy-done = bf16[2048,128]{1,0:T(8,128)(2,1)S(1)} copy-done((bf16[2048,128]{1,0:T(8,128)(2,1)S(1)}, bf16[2048,128]{1,0:T(8,128)(2,1)}, u32[]{:S(2)}) %copy-start) | copy-done | bytes 524312
  11.9 5.6 %shard_map.59 = (f32[1024,128]{1,0:T(8,128)S(1)}, f32[1024,128]{1,0:T(8,128)S(1)}) custom-call(s32[5,4]{1,0:T(8,128)S(1)} %stack.48.info, bf16[4,1024,1024]{2,1,0:T(8,128)(2,1)} %tiles_ref.3, bf16[2048,128]{1,0:T(8,128)(2,1)S(1)} %copy-done), custom_call_target="tpu_custom_call" | custom-call | flops 1073741824 | bytes 10485760 | tf_op jit(solution)/shard_map/pallas_call | solution.py:261
  17.6 3.4 %all-to-all-done = bf16[64,32,128]{2,1,0:T(8,128)(2,1)S(1)} async-done(((bf16[64,32,128]{2,1,0:T(8,128)(2,1)}), bf16[64,32,128]{2,1,0:T(8,128)(2,1)S(1)}, u32[]{:S(2)}, u32[]{:S(2)}) %all-to-all-start) | async-done | bytes 524320 | tf_op jit(solution)/shard_map/all_to_all | solution.py:345
  21.1 0.7 broadcast_in_dim.20
  21.9 5.7 %all-to-all-start.1 = ((bf16[32,32,128]{2,1,0:T(8,128)(2,1)}), bf16[32,32,128]{2,1,0:T(8,128)(2,1)S(1)}, u32[]{:S(2)}, u32[]{:S(2)}) async-start(bf16[32,32,128]{2,1,0:T(8,128)(2,1)} %broadcast_in_dim.20), calls=%async_computation.1 | async-start | bytes 524288 | tf_op jit(solution)/shard_map/all_to_all | solution.py:359
  27.7 1.6 %collective-permute-start.1 = (s16[528,128]{1,0:T(8,128)(2,1)S(1)}, s16[528,128]{1,0:T(8,128)(2,1)S(1)}, u32[]{:S(2)}, u32[]{:S(2)}) collective-permute-start(s16[528,128]{1,0:T(8,128)(2,1)S(1)} %get-tuple-element.20), channel_id=1, source_target_pairs={{0,2},{1,3},{2,0},{3,1},{4,6},{5,7},{6,4},{7,5},{8,10},{9,11},{10,... | collective-permute-start | bytes 405512 | tf_op jit(solution)/shard_map/ppermute | solution.py:293
  29.2 6.4 %all-to-all-done.1.near_ref = bf16[32,32,128]{2,1,0:T(8,128)(2,1)S(1)} async-done(((bf16[32,32,128]{2,1,0:T(8,128)(2,1)}), bf16[32,32,128]{2,1,0:T(8,128)(2,1)S(1)}, u32[]{:S(2)}, u32[]{:S(2)}) %all-to-all-start.1) | async-done | bytes 262176 | tf_op jit(solution)/shard_map/all_to_all | solution.py:359
  35.9 1.5 %collective-permute-done.2.far_ref = bf16[32,32,128]{2,1,0:T(8,128)(2,1)S(1)} collective-permute-done((bf16[32,32,128]{2,1,0:T(8,128)(2,1)S(1)}, bf16[32,32,128]{2,1,0:T(8,128)(2,1)S(1)}, u32[]{:S(2)}, u32[]{:S(2)}) %collective-permute-start.2) | collective-permute-done | bytes 262176 | tf_op jit(solution)/shard_map/ppermute | solution.py:293
  37.4 5.2 %shard_map.61 = (f32[2,512,128]{2,1,0:T(8,128)S(1)}, s16[528,128]{1,0:T(8,128)(2,1)S(1)}, s16[528,128]{1,0:T(8,128)(2,1)S(1)}) custom-call(s32[5,4]{1,0:T(8,128)S(1)} %stack.48.info, bf16[4,1024,1024]{2,1,0:T(8,128)(2,1)} %tiles_ref.3, bf16[32,32,128]{2,1,0:T(8,128)(2,1)S(1)} %all-to-all-done.1.near_ref, bf16[32,32,128]{2,1,0:T(8,128)(2,1)S(1)} %collective-permute-done.2.far_ref), custom_call_target="tpu_custom_call" | custom-call | flops 1073741824 | bytes 10485760 | tf_op jit(solution)/shard_map/pallas_call | solution.py:276
  42.7 3.4 %collective-permute-start.3 = (s16[528,128]{1,0:T(8,128)(2,1)S(1)}, s16[528,128]{1,0:T(8,128)(2,1)S(1)}, u32[]{:S(2)}, u32[]{:S(2)}) collective-permute-start(s16[528,128]{1,0:T(8,128)(2,1)S(1)} %get-tuple-element.24), channel_id=1, source_target_pairs={{0,64},{64,0},{128,192},{192,128},{1,65},{65,1},{129,193},{193,129... | collective-permute-start | bytes 405512 | tf_op jit(solution)/shard_map/ppermute | solution.py:293
  46.0 3.6 %collective-permute-start.4 = (s16[528,128]{1,0:T(8,128)(2,1)S(1)}, s16[528,128]{1,0:T(8,128)(2,1)S(1)}, u32[]{:S(2)}, u32[]{:S(2)}) collective-permute-start(s16[528,128]{1,0:T(8,128)(2,1)S(1)} %get-tuple-element.25), channel_id=1, source_target_pairs={{0,192},{64,128},{128,64},{192,0},{1,193},{65,129},{129,65},{193,1... | collective-permute-start | bytes 405512 | tf_op jit(solution)/shard_map/ppermute | solution.py:293
  49.6 3.3 %collective-permute-done.3.got_ref = s16[528,128]{1,0:T(8,128)(2,1)S(1)} collective-permute-done((s16[528,128]{1,0:T(8,128)(2,1)S(1)}, s16[528,128]{1,0:T(8,128)(2,1)S(1)}, u32[]{:S(2)}, u32[]{:S(2)}) %collective-permute-start.3) | collective-permute-done | bytes 135200 | tf_op jit(solution)/shard_map/ppermute | solution.py:293
  53.0 2.6 %collective-permute-start.7 = (s16[528,128]{1,0:T(8,128)(2,1)S(1)}, s16[528,128]{1,0:T(8,128)(2,1)S(1)}, u32[]{:S(2)}, u32[]{:S(2)}) collective-permute-start(s16[528,128]{1,0:T(8,128)(2,1)S(1)} %shard_map.62.after_ref.own_ref), channel_id=1, source_target_pairs={{0,192},{64,128},{128,64},{192,0},{1,193},{65,129},{129,65},{193,1... | collective-permute-start | bytes 405512 | tf_op jit(solution)/shard_map/ppermute | solution.py:293
  55.8 3.5 %collective-permute-start.5 = (s16[528,128]{1,0:T(8,128)(2,1)S(1)}, s16[528,128]{1,0:T(8,128)(2,1)S(1)}, u32[]{:S(2)}, u32[]{:S(2)}) collective-permute-start(s16[528,128]{1,0:T(8,128)(2,1)S(1)} %shard_map.65.own_ref), channel_id=1, source_target_pairs={{0,64},{64,0},{128,192},{192,128},{1,65},{65,1},{129,193},{193,129... | collective-permute-start | bytes 405512 | tf_op jit(solution)/shard_map/ppermute | solution.py:293
  59.3 0.7 shard_map.63
  60.0 7.5 %all-to-all-start.2 = ((f32[16,32,128]{2,1,0:T(8,128)}), f32[16,32,128]{2,1,0:T(8,128)S(1)}, u32[]{:S(2)}, u32[]{:S(2)}) async-start(f32[16,32,128]{2,1,0:T(8,128)} %bitcast.11), calls=%async_computation.2 | async-start | bytes 524288 | tf_op jit(solution)/shard_map/all_to_all | solution.py:365
  67.7 1.5 %collective-permute-start.8 = (s16[528,128]{1,0:T(8,128)(2,1)S(1)}, s16[528,128]{1,0:T(8,128)(2,1)S(1)}, u32[]{:S(2)}, u32[]{:S(2)}) collective-permute-start(s16[528,128]{1,0:T(8,128)(2,1)S(1)} %shard_map.67.half_ref), channel_id=1, source_target_pairs={{0,64},{64,0},{128,192},{192,128},{1,65},{65,1},{129,193},{193,129... | collective-permute-start | bytes 405512 | tf_op jit(solution)/shard_map/ppermute | solution.py:293
  69.3 2.4 %collective-permute-start.6 = (s16[528,128]{1,0:T(8,128)(2,1)S(1)}, s16[528,128]{1,0:T(8,128)(2,1)S(1)}, u32[]{:S(2)}, u32[]{:S(2)}) collective-permute-start(s16[528,128]{1,0:T(8,128)(2,1)S(1)} %shard_map.66.half_ref), channel_id=1, source_target_pairs={{0,192},{64,128},{128,64},{192,0},{1,193},{65,129},{129,65},{193,1... | collective-permute-start | bytes 405512 | tf_op jit(solution)/shard_map/ppermute | solution.py:293
  71.8 1.3 %shard_map.68.refs_0_ = f32[2048,128]{1,0:T(8,128)} custom-call(s32[4]{0:T(128)S(1)} %pad_add_fusion.2.bits, s16[528,128]{1,0:T(8,128)(2,1)S(1)} %shard_map.67.half_ref), custom_call_target="tpu_custom_call" | custom-call | tf_op jit(solution)/shard_map/pallas_call | solution.py:222
  73.1 1.3 %shard_map.69.refs_0_ = f32[2048,128]{1,0:T(8,128)} custom-call(s32[4]{0:T(128)S(1)} %pad_add_fusion.2.bits, s16[528,128]{1,0:T(8,128)(2,1)S(1)} %shard_map.66.half_ref, f32[2048,128]{1,0:T(8,128)} %shard_map.68.refs_0_), custom_call_target="tpu_custom_call", output_to_operand_aliasing={{}: (2, {})} | custom-call | tf_op jit(solution)/shard_map/pallas_call | solution.py:222
  75.0 1.3 %shard_map.70.refs_0_ = f32[2048,128]{1,0:T(8,128)} custom-call(s32[4]{0:T(128)S(1)} %pad_add_fusion.2.bits, s16[528,128]{1,0:T(8,128)(2,1)S(1)} %collective-permute-done.8.half_ref, f32[2048,128]{1,0:T(8,128)} %shard_map.69.refs_0_), custom_call_target="tpu_custom_call", output_to_operand_aliasing={{}: (2, {})} | custom-call | tf_op jit(solution)/shard_map/pallas_call | solution.py:222
  76.3 1.8 %collective-permute-done.6.half_ref = s16[528,128]{1,0:T(8,128)(2,1)S(1)} collective-permute-done((s16[528,128]{1,0:T(8,128)(2,1)S(1)}, s16[528,128]{1,0:T(8,128)(2,1)S(1)}, u32[]{:S(2)}, u32[]{:S(2)}) %collective-permute-start.6) | collective-permute-done | bytes 135200 | tf_op jit(solution)/shard_map/ppermute | solution.py:293
  78.1 1.3 %shard_map.71 = f32[2048,128]{1,0:T(8,128)} custom-call(s32[4]{0:T(128)S(1)} %pad_add_fusion.2.bits, s16[528,128]{1,0:T(8,128)(2,1)S(1)} %collective-permute-done.6.half_ref, f32[2048,128]{1,0:T(8,128)} %shard_map.70.refs_0_), custom_call_target="tpu_custom_call", output_to_operand_aliasing={{}: (2, {})} | custom-call | tf_op jit(solution)/shard_map/pallas_call | solution.py:222
  (23 shorter events, 2.7 us)
Async XLA Ops:
  0.6 20.3 %all-to-all-start = ((bf16[64,32,128]{2,1,0:T(8,128)(2,1)}), bf16[64,32,128]{2,1,0:T(8,128)(2,1)S(1)}, u32[]{:S(2)}, u32[]{:S(2)}) async-start(bf16[64,32,128]{2,1,0:T(8,128)(2,1)} %bitcast.18), calls=%async_computation | async-start | bytes 1048576 | tf_op jit(solution)/shard_map/all_to_all | solution.py:345
  10.9 1.0 %copy-start = (bf16[2048,128]{1,0:T(8,128)(2,1)S(1)}, bf16[2048,128]{1,0:T(8,128)(2,1)}, u32[]{:S(2)}) copy-start(bf16[2048,128]{1,0:T(8,128)(2,1)} %panel_ref.1) | copy-start | bytes 1572868
  20.9 6.6 %collective-permute-start = (f32[1024,128]{1,0:T(8,128)S(1)}, f32[1024,128]{1,0:T(8,128)S(1)}, u32[]{:S(2)}, u32[]{:S(2)}) collective-permute-start(f32[1024,128]{1,0:T(8,128)S(1)} %get-tuple-element.17), channel_id=1, source_target_pairs={{0,1},{1,0},{2,3},{3,2},{4,5},{5,4},{6,7},{7,6},{8,9},{9,8},{10,11... | collective-permute-start | bytes 1572872 | tf_op jit(solution)/shard_map/ppermute | solution.py:293
  21.9 13.8 %all-to-all-start.1 = ((bf16[32,32,128]{2,1,0:T(8,128)(2,1)}), bf16[32,32,128]{2,1,0:T(8,128)(2,1)S(1)}, u32[]{:S(2)}, u32[]{:S(2)}) async-start(bf16[32,32,128]{2,1,0:T(8,128)(2,1)} %broadcast_in_dim.20), calls=%async_computation.1 | async-start | bytes 524288 | tf_op jit(solution)/shard_map/all_to_all | solution.py:359
  27.7 8.2 %collective-permute-start.1 = (s16[528,128]{1,0:T(8,128)(2,1)S(1)}, s16[528,128]{1,0:T(8,128)(2,1)S(1)}, u32[]{:S(2)}, u32[]{:S(2)}) collective-permute-start(s16[528,128]{1,0:T(8,128)(2,1)S(1)} %get-tuple-element.20), channel_id=1, source_target_pairs={{0,2},{1,3},{2,0},{3,1},{4,6},{5,7},{6,4},{7,5},{8,10},{9,11},{10,... | collective-permute-start | bytes 405512 | tf_op jit(solution)/shard_map/ppermute | solution.py:293
  35.9 1.5 %collective-permute-start.2 = (bf16[32,32,128]{2,1,0:T(8,128)(2,1)S(1)}, bf16[32,32,128]{2,1,0:T(8,128)(2,1)S(1)}, u32[]{:S(2)}, u32[]{:S(2)}) collective-permute-start(bf16[32,32,128]{2,1,0:T(8,128)(2,1)S(1)} %all-to-all-done.1.near_ref), channel_id=1, source_target_pairs={{0,1},{1,0},{2,3},{3,2},{4,5},{5,4},{6,7},{7,6},{8,9},{9,8},{10,11... | collective-permute-start | bytes 786440 | tf_op jit(solution)/shard_map/ppermute | solution.py:293
  42.7 10.2 %collective-permute-start.3 = (s16[528,128]{1,0:T(8,128)(2,1)S(1)}, s16[528,128]{1,0:T(8,128)(2,1)S(1)}, u32[]{:S(2)}, u32[]{:S(2)}) collective-permute-start(s16[528,128]{1,0:T(8,128)(2,1)S(1)} %get-tuple-element.24), channel_id=1, source_target_pairs={{0,64},{64,0},{128,192},{192,128},{1,65},{65,1},{129,193},{193,129... | collective-permute-start | bytes 405512 | tf_op jit(solution)/shard_map/ppermute | solution.py:293
  46.0 9.6 %collective-permute-start.4 = (s16[528,128]{1,0:T(8,128)(2,1)S(1)}, s16[528,128]{1,0:T(8,128)(2,1)S(1)}, u32[]{:S(2)}, u32[]{:S(2)}) collective-permute-start(s16[528,128]{1,0:T(8,128)(2,1)S(1)} %get-tuple-element.25), channel_id=1, source_target_pairs={{0,192},{64,128},{128,64},{192,0},{1,193},{65,129},{129,65},{193,1... | collective-permute-start | bytes 405512 | tf_op jit(solution)/shard_map/ppermute | solution.py:293
  53.0 14.5 %collective-permute-start.7 = (s16[528,128]{1,0:T(8,128)(2,1)S(1)}, s16[528,128]{1,0:T(8,128)(2,1)S(1)}, u32[]{:S(2)}, u32[]{:S(2)}) collective-permute-start(s16[528,128]{1,0:T(8,128)(2,1)S(1)} %shard_map.62.after_ref.own_ref), channel_id=1, source_target_pairs={{0,192},{64,128},{128,64},{192,0},{1,193},{65,129},{129,65},{193,1... | collective-permute-start | bytes 405512 | tf_op jit(solution)/shard_map/ppermute | solution.py:293
  55.8 13.4 %collective-permute-start.5 = (s16[528,128]{1,0:T(8,128)(2,1)S(1)}, s16[528,128]{1,0:T(8,128)(2,1)S(1)}, u32[]{:S(2)}, u32[]{:S(2)}) collective-permute-start(s16[528,128]{1,0:T(8,128)(2,1)S(1)} %shard_map.65.own_ref), channel_id=1, source_target_pairs={{0,64},{64,0},{128,192},{192,128},{1,65},{65,1},{129,193},{193,129... | collective-permute-start | bytes 405512 | tf_op jit(solution)/shard_map/ppermute | solution.py:293
  60.0 14.3 %all-to-all-start.2 = ((f32[16,32,128]{2,1,0:T(8,128)}), f32[16,32,128]{2,1,0:T(8,128)S(1)}, u32[]{:S(2)}, u32[]{:S(2)}) async-start(f32[16,32,128]{2,1,0:T(8,128)} %bitcast.11), calls=%async_computation.2 | async-start | bytes 524288 | tf_op jit(solution)/shard_map/all_to_all | solution.py:365
  67.7 7.3 %collective-permute-start.8 = (s16[528,128]{1,0:T(8,128)(2,1)S(1)}, s16[528,128]{1,0:T(8,128)(2,1)S(1)}, u32[]{:S(2)}, u32[]{:S(2)}) collective-permute-start(s16[528,128]{1,0:T(8,128)(2,1)S(1)} %shard_map.67.half_ref), channel_id=1, source_target_pairs={{0,64},{64,0},{128,192},{192,128},{1,65},{65,1},{129,193},{193,129... | collective-permute-start | bytes 405512 | tf_op jit(solution)/shard_map/ppermute | solution.py:293
  69.3 8.7 %collective-permute-start.6 = (s16[528,128]{1,0:T(8,128)(2,1)S(1)}, s16[528,128]{1,0:T(8,128)(2,1)S(1)}, u32[]{:S(2)}, u32[]{:S(2)}) collective-permute-start(s16[528,128]{1,0:T(8,128)(2,1)S(1)} %shard_map.66.half_ref), channel_id=1, source_target_pairs={{0,192},{64,128},{128,64},{192,0},{1,193},{65,129},{129,65},{193,1... | collective-permute-start | bytes 405512 | tf_op jit(solution)/shard_map/ppermute | solution.py:293

commit v7 on v6

--- a/solution.py
+++ b/solution.py
@@ -97,13 +97,6 @@
 def rows_kernel(mine_ref, got_ref, after_ref, out_ref):
     del after_ref
     out_ref[...] = mine_ref[...] + decode(got_ref)
-
-
-def total_kernel(terms_ref, out_ref):
-    total = terms_ref[0]
-    for site in range(1, terms_ref.shape[0]):
-        total += terms_ref[site]
-    out_ref[...] = total
 
 
 def block_rows(size):
@@ -142,14 +135,32 @@
     return jnp.concatenate(parts, axis=0)
 
 
+def fetch_kernel(tiles_ref, after_ref, held_ref, token_ref, sems):
+    del after_ref
+    slots, width, _ = held_ref.shape
+    depth = width // STEPS
+    copies = []
+    for index in range(slots * STEPS):
+        piece = pl.ds(index % STEPS * depth, depth)
+        copies.append(
+            pltpu.make_async_copy(
+                tiles_ref.at[index // STEPS, piece],
+                held_ref.at[index // STEPS, piece],
+                sems.at[index],
+            )
+        )
+    for copy in copies:
+        copy.start()
+    token_ref[...] = jnp.zeros_like(token_ref)
+    for copy in copies:
+        copy.wait()
+
+
 def col_kernel(
-    info, tiles_ref, near_ref, far_ref, keep_ref, send0_ref, send1_ref, slab, total, result, held, sems
+    info, held, near_ref, far_ref, keep_ref, send0_ref, send1_ref, slab, total, result
 ):
     slots, width, _ = held.shape
     depth = width // STEPS
-    fetch = fetch_of(info, tiles_ref, held, sems)
-    for index in range(slots * STEPS):
-        fetch(index).start()
     total[...] = jnp.zeros_like(total)
     core = info[4, 0]
     for ref, tile in ((near_ref, core), (far_ref, 1 - core)):
@@ -159,7 +170,6 @@
     @pl.loop(0, slots * STEPS)
     def _(index):
         slot, part, rows, cols, piece = place_of(info, index, depth, width)
-        fetch(index).wait()
 
         @pl.when(info[2, slot] == 1)
         def _():
@@ -186,15 +196,35 @@
     encode(decode(own_ref) + decode(got_ref), out_ref)
 
 
-def place_kernel(index, far, bits, half_ref, *refs):
-    out_ref, held, sem = refs[-3:]
-    size = held.shape[0]
-    held[...] = decode(half_ref)
-    side = 1 - bits[index] if far else bits[index]
-    first = pl.multiple_of((index * 2 + side) * size, size)
-    copy = pltpu.make_async_copy(held, out_ref.at[pl.ds(first, size)], sem)
-    copy.start()
-    copy.wait()
+def place_halves(far, half_refs, out_ref, held, sems):
+    size = held.shape[1]
+    row = lax.axis_index("row")
+    high = row // 2
+    copies = []
+    for index, (half_ref, bit) in enumerate(zip(half_refs, ((row + high) % 2, high))):
+        held[index] = decode(half_ref)
+        side = 1 - bit if far else bit
+        first = pl.multiple_of((index * 2 + side) * size, size)
+        copy = pltpu.make_async_copy(
+            held.at[index], out_ref.at[pl.ds(first, size)], sems.at[index]
+        )
+        copy.start()
+        copies.append(copy)
+    for copy in copies:
+        copy.wait()
+
+
+def own_kernel(half0_ref, half1_ref, out_ref, held, sems):
+    place_halves(False, (half0_ref, half1_ref), out_ref, held, sems)
+
+
+def last_kernel(half0_ref, half1_ref, terms_ref, result_ref, out_ref, rows_ref, held, sems):
+    del result_ref
+    total = terms_ref[0]
+    for site in range(1, terms_ref.shape[0]):
+        total += terms_ref[site]
+    rows_ref[...] = total
+    place_halves(True, (half0_ref, half1_ref), out_ref, held, sems)
 
 
 VMEM = pl.BlockSpec(memory_space=pltpu.VMEM)
@@ -216,18 +246,33 @@
     )(*args)
 
 
-def place_half(index, far, bits, half, result):
-    size, lanes = half.shape[0] - PAD, half.shape[1]
-    args = (bits, half) + (() if result is None else (result,))
-    return pl.pallas_call(
-        functools.partial(place_kernel, index, far),
-        in_specs=[SMEM, VMEM] + [HBM] * (len(args) - 2),
+def place_scratch(size, lanes):
+    return [pltpu.VMEM((2, size, lanes), jnp.float32), pltpu.SemaphoreType.DMA((2,))]
+
+
+def place_own(owns):
+    size, lanes = owns[0].shape[0] - PAD, owns[0].shape[1]
+    return pl.pallas_call(
+        own_kernel,
+        in_specs=[VMEM, VMEM],
         out_specs=HBM,
         out_shape=floats(4 * size, lanes),
-        scratch_shapes=[pltpu.VMEM((size, lanes), jnp.float32), pltpu.SemaphoreType.DMA],
-        input_output_aliases={} if result is None else {2: 0},
+        scratch_shapes=place_scratch(size, lanes),
         compiler_params=limit(6),
-    )(*args)
+    )(*owns)
+
+
+def place_last(gots, terms, result):
+    size, lanes = gots[0].shape[0] - PAD, gots[0].shape[1]
+    return pl.pallas_call(
+        last_kernel,
+        in_specs=[VMEM, VMEM, VMEM, HBM],
+        out_specs=[HBM, VMEM],
+        out_shape=[floats(4 * size, lanes), floats(*terms.shape[1:])],
+        scratch_shapes=place_scratch(size, lanes),
+        input_output_aliases={3: 0},
+        compiler_params=limit(6),
+    )(*gots, terms, result)
 
 
 def tile_cost(shape, lanes):
@@ -269,21 +314,31 @@
     )(info, grm_tiles, panel)
 
 
+def fetch_tiles(grm_tiles, after):
+    return pl.pallas_call(
+        fetch_kernel,
+        in_specs=[HBM, VMEM],
+        out_specs=[VMEM, VMEM],
+        out_shape=[pltpu.VMEM(grm_tiles.shape, grm_tiles.dtype), floats(8, 128)],
+        scratch_shapes=[pltpu.SemaphoreType.DMA((grm_tiles.shape[0] * STEPS,))],
+        compiler_params=limit(12),
+    )(grm_tiles, after)
+
+
 def col_products(info, grm_tiles, near, far):
     slots, width, _ = grm_tiles.shape
     lanes = near.shape[2]
     half = width // 2
     return pl.pallas_call(
         col_kernel,
-        in_specs=[SMEM, HBM, VMEM, VMEM],
+        in_specs=[SMEM, VMEM, VMEM, VMEM],
         out_specs=[VMEM] * 3,
         out_shape=[floats(2, half, lanes), coded(half, lanes), coded(half, lanes)],
         scratch_shapes=[
             pltpu.VMEM((RT_DEV * width, lanes), near.dtype),
             pltpu.VMEM((lanes, CTD * width), jnp.float32),
             pltpu.VMEM((CTD * width, lanes), jnp.float32),
-        ]
-        + tile_scratch(grm_tiles),
+        ],
         compiler_params=limit(24),
         cost_estimate=tile_cost(grm_tiles.shape, lanes),
     )(info, grm_tiles, near, far)
@@ -293,7 +348,7 @@
     return lax.ppermute(value, axis, [(k, k ^ flip) for k in range(lax.axis_size(axis))])
 
 
-def sum_over_row(bits, keep, sends):
+def sum_over_row(keep, sends):
     size, lanes = keep.shape[1:]
     outs = [coded(size, lanes)]
     flips = [(1, 3, 1), (3, 1, 3)]
@@ -306,11 +361,7 @@
     gots = [swap(own, "row", flip[1]) for own, flip in zip(owns, flips)]
     owns = [small_call(second_kernel, outs, own, got)[0] for own, got in zip(owns, gots)]
     gots = [swap(own, "row", flip[2]) for own, flip in zip(owns, flips)]
-    result = None
-    for far, halves in enumerate((owns, gots)):
-        for index, half in enumerate(halves):
-            result = place_half(index, far, bits, half, result)
-    return result, begun
+    return gots, place_own(owns), begun
 
 
 def on_device(grm_tiles, tile_row, tile_col, panel):
@@ -357,15 +408,17 @@
     piece = lax.dynamic_index_in_dim(pieces, place, 0)
     packed = jnp.broadcast_to(piece, (chips, size, lanes))
     near = lax.all_to_all(packed, "col", 0, 0, axis_index_groups=one_core)
-    near, got_z = lax.optimization_barrier((near, swap(send_z, "col", 2)))
+    got_z = swap(send_z, "col", 2)
+    held, token = fetch_tiles(tiles, send_z)
+    near, got_z, token = lax.optimization_barrier((near, got_z, token))
     far = swap(near, "col", 1)
-    keep, *sends = col_products(info, tiles, near, far)
-    y_cols, begun = sum_over_row(bits, keep, sends)
+    keep, *sends = col_products(info, held, near, far)
+    gots, result, begun = sum_over_row(keep, sends)
     rows = small_call(rows_kernel, [floats(half, lanes)], mine, got_z, begun)[0]
     terms = lax.all_to_all(
         rows.reshape(SITES, share, lanes), "col", 0, 0, axis_index_groups=across
     )
-    y_rows = small_call(total_kernel, [floats(share, lanes)], terms)[0]
+    y_cols, y_rows = place_last(gots, terms, result)
     return (y_rows, y_cols)
 
 

time: 79.8 us -> 81.5 us (1.021)
  starting transfers between devices: 41.1 us -> 43.1 us
    ppermute x9, starting transfers between devices: 18.6 us -> 20.6 us  [swap(): lax.ppermute(value, axis, [(k, k ^ flip) for k in range(lax.axis_size(axi...]
    pallas_call x7 -> x6, Pallas kernels: 2.05 us -> 1.43 us  [small_call(): pl.pallas_call(kernel, in_specs=[SMEM] * scalars + [VMEM] * (len(args) -...]
    pallas_call x5 -> x4, Pallas kernels: 10.4 us -> 10.4 us  [the longest x1 4.06 us: fetch_tiles(): pl.pallas_call(fetch_kernel, in_specs=[HBM, VMEM], out_specs=[VMEM, VMEM]...]
where the time goes in v7:
time: 81.5 us; the launch traced here: 81 us
  starting transfers between devices  43.1 us (53%)
  Pallas kernels  17.4 us (21%)
  waiting for transfers between devices  17 us (21%)
  local copies, waits for them, and re-layouts  1.81 us (2%)
  other arithmetic  0.83 us (1%)
    ppermute x9, starting transfers between devices, swap(): lax.ppermute(value, axis, [(k, k ^ flip) for k in range(lax.axis_size(axi...  20.6 us
    all_to_all x1, starting transfers between devices, on_device(): lax.all_to_all(panel.reshape(col_count, size, lanes), 'col', 0, 0, axis_i...  9.33 us
    all_to_all x1, starting transfers between devices, on_device(): lax.all_to_all(rows.reshape(SITES, share, lanes), 'col', 0, 0, axis_index...  7.5 us
    ppermute x9, waiting for transfers between devices, swap(): lax.ppermute(value, axis, [(k, k ^ flip) for k in range(lax.axis_size(axi...  7.17 us
    all_to_all x1, waiting for transfers between devices, on_device(): near = lax.all_to_all(packed, 'col', 0, 0, axis_index_groups=one_core)  6.43 us
    all_to_all x1, starting transfers between devices, on_device(): near = lax.all_to_all(packed, 'col', 0, 0, axis_index_groups=one_core)  5.68 us
    pallas_call x1, Pallas kernels, row_products(): pl.pallas_call(row_kernel, in_specs=[SMEM, HBM, VMEM], out_specs=[VMEM, V...  5.64 us
    pallas_call x1, Pallas kernels, fetch_tiles(): pl.pallas_call(fetch_kernel, in_specs=[HBM, VMEM], out_specs=[VMEM, VMEM]...  4.06 us
  transfers between devices with their start and end apart: 12, of which 6 were waited for; matrix products, arithmetic and copies ran while one was open for 2% of the time, Pallas kernels for 15%

profile of v7, /device:TPU:6, one launch (start us, length us, event | category | flops | bytes accessed | tf_op | source)
XLA Modules:
  0.0 81.0 jit_solution(1573421381584259660)
XLA Ops:
  0.6 9.3 %all-to-all-start = ((bf16[64,32,128]{2,1,0:T(8,128)(2,1)}), bf16[64,32,128]{2,1,0:T(8,128)(2,1)S(1)}, u32[]{:S(2)}, u32[]{:S(2)}) async-start(bf16[64,32,128]{2,1,0:T(8,128)(2,1)} %bitcast.18), calls=%async_computation | async-start | bytes 1048576 | tf_op jit(solution)/shard_map/all_to_all | solution.py:396
  10.2 0.7 fusion
  10.9 1.0 %copy-done = bf16[2048,128]{1,0:T(8,128)(2,1)S(1)} copy-done((bf16[2048,128]{1,0:T(8,128)(2,1)S(1)}, bf16[2048,128]{1,0:T(8,128)(2,1)}, u32[]{:S(2)}) %copy-start) | copy-done | bytes 524312
  11.9 5.6 %shard_map.59 = (f32[1024,128]{1,0:T(8,128)S(1)}, f32[1024,128]{1,0:T(8,128)S(1)}) custom-call(s32[5,4]{1,0:T(8,128)S(1)} %stack.46.info, bf16[4,1024,1024]{2,1,0:T(8,128)(2,1)} %tiles_ref.3, bf16[2048,128]{1,0:T(8,128)(2,1)S(1)} %copy-done), custom_call_target="tpu_custom_call" | custom-call | flops 1073741824 | bytes 10485760 | tf_op jit(solution)/shard_map/pallas_call | solution.py:306
  17.6 3.4 %all-to-all-done = bf16[64,32,128]{2,1,0:T(8,128)(2,1)S(1)} async-done(((bf16[64,32,128]{2,1,0:T(8,128)(2,1)}), bf16[64,32,128]{2,1,0:T(8,128)(2,1)S(1)}, u32[]{:S(2)}, u32[]{:S(2)}) %all-to-all-start) | async-done | bytes 524320 | tf_op jit(solution)/shard_map/all_to_all | solution.py:396
  21.1 0.7 broadcast_in_dim.20
  21.9 5.7 %all-to-all-start.1 = ((bf16[32,32,128]{2,1,0:T(8,128)(2,1)}), bf16[32,32,128]{2,1,0:T(8,128)(2,1)S(1)}, u32[]{:S(2)}, u32[]{:S(2)}) async-start(bf16[32,32,128]{2,1,0:T(8,128)(2,1)} %broadcast_in_dim.20), calls=%async_computation.1 | async-start | bytes 524288 | tf_op jit(solution)/shard_map/all_to_all | solution.py:410
  27.7 1.6 %collective-permute-start.1 = (s16[528,128]{1,0:T(8,128)(2,1)S(1)}, s16[528,128]{1,0:T(8,128)(2,1)S(1)}, u32[]{:S(2)}, u32[]{:S(2)}) collective-permute-start(s16[528,128]{1,0:T(8,128)(2,1)S(1)} %get-tuple-element.21.after_ref), channel_id=1, source_target_pairs={{0,2},{1,3},{2,0},{3,1},{4,6},{5,7},{6,4},{7,5},{8,10},{9,11},{10,... | collective-permute-start | bytes 405512 | tf_op jit(solution)/shard_map/ppermute | solution.py:348
  29.2 6.4 %all-to-all-done.1.near_ref = bf16[32,32,128]{2,1,0:T(8,128)(2,1)S(1)} async-done(((bf16[32,32,128]{2,1,0:T(8,128)(2,1)}), bf16[32,32,128]{2,1,0:T(8,128)(2,1)S(1)}, u32[]{:S(2)}, u32[]{:S(2)}) %all-to-all-start.1) | async-done | bytes 262176 | tf_op jit(solution)/shard_map/all_to_all | solution.py:410
  35.7 0.2 collective-permute-done.1.got_ref
  35.9 4.1 %shard_map.61 = (bf16[4,1024,1024]{2,1,0:T(8,128)(2,1)S(1)}, f32[8,128]{1,0:T(8,128)}) custom-call(bf16[4,1024,1024]{2,1,0:T(8,128)(2,1)} %tiles_ref.3, s16[528,128]{1,0:T(8,128)(2,1)S(1)} %get-tuple-element.21.after_ref), custom_call_target="tpu_custom_call" | custom-call | tf_op jit(solution)/shard_map/pallas_call | solution.py:318
  40.0 4.0 %shard_map.62 = (f32[2,512,128]{2,1,0:T(8,128)S(1)}, s16[528,128]{1,0:T(8,128)(2,1)S(1)}, s16[528,128]{1,0:T(8,128)(2,1)S(1)}) custom-call(s32[5,4]{1,0:T(8,128)S(1)} %stack.46.info, bf16[4,1024,1024]{2,1,0:T(8,128)(2,1)S(1)} %get-tuple-element.22.held, bf16[32,32,128]{2,1,0:T(8,128)(2,1)S(1)} %all-to-all-done.1.near_ref, ...), custom_call_target="tpu_custom_call" | custom-call | flops 1073741824 | bytes 10485760 | tf_op jit(solution)/shard_map/pallas_call | solution.py:332
  44.0 3.4 %collective-permute-start.3 = (s16[528,128]{1,0:T(8,128)(2,1)S(1)}, s16[528,128]{1,0:T(8,128)(2,1)S(1)}, u32[]{:S(2)}, u32[]{:S(2)}) collective-permute-start(s16[528,128]{1,0:T(8,128)(2,1)S(1)} %get-tuple-element.26), channel_id=1, source_target_pairs={{0,64},{64,0},{128,192},{192,128},{1,65},{65,1},{129,193},{193,129... | collective-permute-start | bytes 405512 | tf_op jit(solution)/shard_map/ppermute | solution.py:348
  47.4 3.6 %collective-permute-start.6 = (s16[528,128]{1,0:T(8,128)(2,1)S(1)}, s16[528,128]{1,0:T(8,128)(2,1)S(1)}, u32[]{:S(2)}, u32[]{:S(2)}) collective-permute-start(s16[528,128]{1,0:T(8,128)(2,1)S(1)} %get-tuple-element.27), channel_id=1, source_target_pairs={{0,192},{64,128},{128,64},{192,0},{1,193},{65,129},{129,65},{193,1... | collective-permute-start | bytes 405512 | tf_op jit(solution)/shard_map/ppermute | solution.py:348
  50.9 3.7 %collective-permute-done.3.got_ref = s16[528,128]{1,0:T(8,128)(2,1)S(1)} collective-permute-done((s16[528,128]{1,0:T(8,128)(2,1)S(1)}, s16[528,128]{1,0:T(8,128)(2,1)S(1)}, u32[]{:S(2)}, u32[]{:S(2)}) %collective-permute-start.3) | collective-permute-done | bytes 135200 | tf_op jit(solution)/shard_map/ppermute | solution.py:348
  54.8 2.6 %collective-permute-start.4 = (s16[528,128]{1,0:T(8,128)(2,1)S(1)}, s16[528,128]{1,0:T(8,128)(2,1)S(1)}, u32[]{:S(2)}, u32[]{:S(2)}) collective-permute-start(s16[528,128]{1,0:T(8,128)(2,1)S(1)} %shard_map.63.own_ref.after_ref), channel_id=1, source_target_pairs={{0,192},{64,128},{128,64},{192,0},{1,193},{65,129},{129,65},{193,1... | collective-permute-start | bytes 405512 | tf_op jit(solution)/shard_map/ppermute | solution.py:348
  57.5 3.5 %collective-permute-start.7 = (s16[528,128]{1,0:T(8,128)(2,1)S(1)}, s16[528,128]{1,0:T(8,128)(2,1)S(1)}, u32[]{:S(2)}, u32[]{:S(2)}) collective-permute-start(s16[528,128]{1,0:T(8,128)(2,1)S(1)} %shard_map.65.own_ref), channel_id=1, source_target_pairs={{0,64},{64,0},{128,192},{192,128},{1,65},{65,1},{129,193},{193,129... | collective-permute-start | bytes 405512 | tf_op jit(solution)/shard_map/ppermute | solution.py:348
  61.0 0.7 shard_map.67
  61.7 7.5 %all-to-all-start.2 = ((f32[16,32,128]{2,1,0:T(8,128)}), f32[16,32,128]{2,1,0:T(8,128)S(1)}, u32[]{:S(2)}, u32[]{:S(2)}) async-start(f32[16,32,128]{2,1,0:T(8,128)} %bitcast.11), calls=%async_computation.2 | async-start | bytes 524288 | tf_op jit(solution)/shard_map/all_to_all | solution.py:418
  69.4 1.4 %collective-permute-start.5 = (s16[528,128]{1,0:T(8,128)(2,1)S(1)}, s16[528,128]{1,0:T(8,128)(2,1)S(1)}, u32[]{:S(2)}, u32[]{:S(2)}) collective-permute-start(s16[528,128]{1,0:T(8,128)(2,1)S(1)} %shard_map.64.half0_ref), channel_id=1, source_target_pairs={{0,64},{64,0},{128,192},{192,128},{1,65},{65,1},{129,193},{193,129... | collective-permute-start | bytes 405512 | tf_op jit(solution)/shard_map/ppermute | solution.py:348
  71.0 4.4 %collective-permute-start.8 = (s16[528,128]{1,0:T(8,128)(2,1)S(1)}, s16[528,128]{1,0:T(8,128)(2,1)S(1)}, u32[]{:S(2)}, u32[]{:S(2)}) collective-permute-start(s16[528,128]{1,0:T(8,128)(2,1)S(1)} %shard_map.66.half1_ref), channel_id=1, source_target_pairs={{0,192},{64,128},{128,64},{192,0},{1,193},{65,129},{129,65},{193,1... | collective-permute-start | bytes 405512 | tf_op jit(solution)/shard_map/ppermute | solution.py:348
  75.4 0.8 %shard_map.68.result_ref = f32[2048,128]{1,0:T(8,128)} custom-call(s16[528,128]{1,0:T(8,128)(2,1)S(1)} %shard_map.64.half0_ref, s16[528,128]{1,0:T(8,128)(2,1)S(1)} %shard_map.66.half1_ref), custom_call_target="tpu_custom_call" | custom-call | tf_op jit(solution)/shard_map/pallas_call | solution.py:255
  76.4 3.1 %collective-permute-done.8.half1_ref = s16[528,128]{1,0:T(8,128)(2,1)S(1)} collective-permute-done((s16[528,128]{1,0:T(8,128)(2,1)S(1)}, s16[528,128]{1,0:T(8,128)(2,1)S(1)}, u32[]{:S(2)}, u32[]{:S(2)}) %collective-permute-start.8) | collective-permute-done | bytes 135200 | tf_op jit(solution)/shard_map/ppermute | solution.py:348
  79.5 1.4 %shard_map.69 = (f32[2048,128]{1,0:T(8,128)}, f32[32,128]{1,0:T(8,128)}) custom-call(s16[528,128]{1,0:T(8,128)(2,1)S(1)} %collective-permute-done.5.half0_ref, s16[528,128]{1,0:T(8,128)(2,1)S(1)} %collective-permute-done.8.half1_ref, f32[16,32,128]{2,1,0:T(8,128)S(1)} %all-to-all-done.2.terms_ref, ...), custom_call_target="tpu_custom_call", output_to_operand_aliasing={{0}: (3, {})} | custom-call | tf_op jit(solution)/shard_map/pallas_call | solution.py:267
  (20 shorter events, 1.2 us)
Async XLA Ops:
  0.6 20.3 %all-to-all-start = ((bf16[64,32,128]{2,1,0:T(8,128)(2,1)}), bf16[64,32,128]{2,1,0:T(8,128)(2,1)S(1)}, u32[]{:S(2)}, u32[]{:S(2)}) async-start(bf16[64,32,128]{2,1,0:T(8,128)(2,1)} %bitcast.18), calls=%async_computation | async-start | bytes 1048576 | tf_op jit(solution)/shard_map/all_to_all | solution.py:396
  10.9 1.0 %copy-start = (bf16[2048,128]{1,0:T(8,128)(2,1)S(1)}, bf16[2048,128]{1,0:T(8,128)(2,1)}, u32[]{:S(2)}) copy-start(bf16[2048,128]{1,0:T(8,128)(2,1)} %panel_ref.1) | copy-start | bytes 1572868
  20.9 6.6 %collective-permute-start = (f32[1024,128]{1,0:T(8,128)S(1)}, f32[1024,128]{1,0:T(8,128)S(1)}, u32[]{:S(2)}, u32[]{:S(2)}) collective-permute-start(f32[1024,128]{1,0:T(8,128)S(1)} %get-tuple-element.20), channel_id=1, source_target_pairs={{0,1},{1,0},{2,3},{3,2},{4,5},{5,4},{6,7},{7,6},{8,9},{9,8},{10,11... | collective-permute-start | bytes 1572872 | tf_op jit(solution)/shard_map/ppermute | solution.py:348
  21.9 13.8 %all-to-all-start.1 = ((bf16[32,32,128]{2,1,0:T(8,128)(2,1)}), bf16[32,32,128]{2,1,0:T(8,128)(2,1)S(1)}, u32[]{:S(2)}, u32[]{:S(2)}) async-start(bf16[32,32,128]{2,1,0:T(8,128)(2,1)} %broadcast_in_dim.20), calls=%async_computation.1 | async-start | bytes 524288 | tf_op jit(solution)/shard_map/all_to_all | solution.py:410
  27.7 8.2 %collective-permute-start.1 = (s16[528,128]{1,0:T(8,128)(2,1)S(1)}, s16[528,128]{1,0:T(8,128)(2,1)S(1)}, u32[]{:S(2)}, u32[]{:S(2)}) collective-permute-start(s16[528,128]{1,0:T(8,128)(2,1)S(1)} %get-tuple-element.21.after_ref), channel_id=1, source_target_pairs={{0,2},{1,3},{2,0},{3,1},{4,6},{5,7},{6,4},{7,5},{8,10},{9,11},{10,... | collective-permute-start | bytes 405512 | tf_op jit(solution)/shard_map/ppermute | solution.py:348
  35.9 4.1 %collective-permute-start.2 = (bf16[32,32,128]{2,1,0:T(8,128)(2,1)S(1)}, bf16[32,32,128]{2,1,0:T(8,128)(2,1)S(1)}, u32[]{:S(2)}, u32[]{:S(2)}) collective-permute-start(bf16[32,32,128]{2,1,0:T(8,128)(2,1)S(1)} %all-to-all-done.1.near_ref), channel_id=1, source_target_pairs={{0,1},{1,0},{2,3},{3,2},{4,5},{5,4},{6,7},{7,6},{8,9},{9,8},{10,11... | collective-permute-start | bytes 786440 | tf_op jit(solution)/shard_map/ppermute | solution.py:348
  44.0 10.6 %collective-permute-start.3 = (s16[528,128]{1,0:T(8,128)(2,1)S(1)}, s16[528,128]{1,0:T(8,128)(2,1)S(1)}, u32[]{:S(2)}, u32[]{:S(2)}) collective-permute-start(s16[528,128]{1,0:T(8,128)(2,1)S(1)} %get-tuple-element.26), channel_id=1, source_target_pairs={{0,64},{64,0},{128,192},{192,128},{1,65},{65,1},{129,193},{193,129... | collective-permute-start | bytes 405512 | tf_op jit(solution)/shard_map/ppermute | solution.py:348
  47.4 10.0 %collective-permute-start.6 = (s16[528,128]{1,0:T(8,128)(2,1)S(1)}, s16[528,128]{1,0:T(8,128)(2,1)S(1)}, u32[]{:S(2)}, u32[]{:S(2)}) collective-permute-start(s16[528,128]{1,0:T(8,128)(2,1)S(1)} %get-tuple-element.27), channel_id=1, source_target_pairs={{0,192},{64,128},{128,64},{192,0},{1,193},{65,129},{129,65},{193,1... | collective-permute-start | bytes 405512 | tf_op jit(solution)/shard_map/ppermute | solution.py:348
  54.8 14.5 %collective-permute-start.4 = (s16[528,128]{1,0:T(8,128)(2,1)S(1)}, s16[528,128]{1,0:T(8,128)(2,1)S(1)}, u32[]{:S(2)}, u32[]{:S(2)}) collective-permute-start(s16[528,128]{1,0:T(8,128)(2,1)S(1)} %shard_map.63.own_ref.after_ref), channel_id=1, source_target_pairs={{0,192},{64,128},{128,64},{192,0},{1,193},{65,129},{129,65},{193,1... | collective-permute-start | bytes 405512 | tf_op jit(solution)/shard_map/ppermute | solution.py:348
  57.5 13.4 %collective-permute-start.7 = (s16[528,128]{1,0:T(8,128)(2,1)S(1)}, s16[528,128]{1,0:T(8,128)(2,1)S(1)}, u32[]{:S(2)}, u32[]{:S(2)}) collective-permute-start(s16[528,128]{1,0:T(8,128)(2,1)S(1)} %shard_map.65.own_ref), channel_id=1, source_target_pairs={{0,64},{64,0},{128,192},{192,128},{1,65},{65,1},{129,193},{193,129... | collective-permute-start | bytes 405512 | tf_op jit(solution)/shard_map/ppermute | solution.py:348
  61.7 14.5 %all-to-all-start.2 = ((f32[16,32,128]{2,1,0:T(8,128)}), f32[16,32,128]{2,1,0:T(8,128)S(1)}, u32[]{:S(2)}, u32[]{:S(2)}) async-start(f32[16,32,128]{2,1,0:T(8,128)} %bitcast.11), calls=%async_computation.2 | async-start | bytes 524288 | tf_op jit(solution)/shard_map/all_to_all | solution.py:418
  69.4 7.0 %collective-permute-start.5 = (s16[528,128]{1,0:T(8,128)(2,1)S(1)}, s16[528,128]{1,0:T(8,128)(2,1)S(1)}, u32[]{:S(2)}, u32[]{:S(2)}) collective-permute-start(s16[528,128]{1,0:T(8,128)(2,1)S(1)} %shard_map.64.half0_ref), channel_id=1, source_target_pairs={{0,64},{64,0},{128,192},{192,128},{1,65},{65,1},{129,193},{193,129... | collective-permute-start | bytes 405512 | tf_op jit(solution)/shard_map/ppermute | solution.py:348
  71.0 8.5 %collective-permute-start.8 = (s16[528,128]{1,0:T(8,128)(2,1)S(1)}, s16[528,128]{1,0:T(8,128)(2,1)S(1)}, u32[]{:S(2)}, u32[]{:S(2)}) collective-permute-start(s16[528,128]{1,0:T(8,128)(2,1)S(1)} %shard_map.66.half1_ref), channel_id=1, source_target_pairs={{0,192},{64,128},{128,64},{192,0},{1,193},{65,129},{129,65},{193,1... | collective-permute-start | bytes 405512 | tf_op jit(solution)/shard_map/ppermute | solution.py:348

commit v8 on v7

--- a/solution.py
+++ b/solution.py
@@ -94,9 +94,16 @@
     encode(keep_ref[size:, :] + got_ref[size:, :], send_ref)
 
 
-def rows_kernel(mine_ref, got_ref, after_ref, out_ref):
-    del after_ref
+def rows_kernel(mine_ref, got_ref, after_ref, token_ref, out_ref):
+    del after_ref, token_ref
     out_ref[...] = mine_ref[...] + decode(got_ref)
+
+
+def total_kernel(terms_ref, out_ref):
+    total = terms_ref[0]
+    for site in range(1, terms_ref.shape[0]):
+        total += terms_ref[site]
+    out_ref[...] = total
 
 
 def block_rows(size):
@@ -218,12 +225,8 @@
     place_halves(False, (half0_ref, half1_ref), out_ref, held, sems)
 
 
-def last_kernel(half0_ref, half1_ref, terms_ref, result_ref, out_ref, rows_ref, held, sems):
+def last_kernel(half0_ref, half1_ref, result_ref, out_ref, held, sems):
     del result_ref
-    total = terms_ref[0]
-    for site in range(1, terms_ref.shape[0]):
-        total += terms_ref[site]
-    rows_ref[...] = total
     place_halves(True, (half0_ref, half1_ref), out_ref, held, sems)
 
 
@@ -262,17 +265,17 @@
     )(*owns)
 
 
-def place_last(gots, terms, result):
+def place_last(gots, result):
     size, lanes = gots[0].shape[0] - PAD, gots[0].shape[1]
     return pl.pallas_call(
         last_kernel,
-        in_specs=[VMEM, VMEM, VMEM, HBM],
-        out_specs=[HBM, VMEM],
-        out_shape=[floats(4 * size, lanes), floats(*terms.shape[1:])],
+        in_specs=[VMEM, VMEM, HBM],
+        out_specs=HBM,
+        out_shape=floats(4 * size, lanes),
         scratch_shapes=place_scratch(size, lanes),
-        input_output_aliases={3: 0},
+        input_output_aliases={2: 0},
         compiler_params=limit(6),
-    )(*gots, terms, result)
+    )(*gots, result)
 
 
 def tile_cost(shape, lanes):
@@ -414,11 +417,12 @@
     far = swap(near, "col", 1)
     keep, *sends = col_products(info, held, near, far)
     gots, result, begun = sum_over_row(keep, sends)
-    rows = small_call(rows_kernel, [floats(half, lanes)], mine, got_z, begun)[0]
+    rows = small_call(rows_kernel, [floats(half, lanes)], mine, got_z, begun, token)[0]
     terms = lax.all_to_all(
         rows.reshape(SITES, share, lanes), "col", 0, 0, axis_index_groups=across
     )
-    y_cols, y_rows = place_last(gots, terms, result)
+    y_rows = small_call(total_kernel, [floats(share, lanes)], terms)[0]
+    y_cols = place_last(gots, result)
     return (y_rows, y_cols)
 
 

time: 81.5 us -> 81.5 us (level)
  local copies, waits for them, and re-layouts: 1.81 us -> 8.44 us
  waiting for transfers between devices: 17 us -> 10.8 us
    unnamed x2 -> x6, local copies, waits for them, and re-layouts: 1.04 us -> 7.67 us
    all_to_all x1, waiting for transfers between devices: 6.43 us -> 0.01 us  [on_device(): near = lax.all_to_all(packed, 'col', 0, 0, axis_index_groups=one_core)]
    pallas_call x6 -> x7, Pallas kernels: 1.43 us -> 2.06 us  [small_call(): pl.pallas_call(kernel, in_specs=[SMEM] * scalars + [VMEM] * (len(args) -...]
  transfers between devices with their start and end apart: 12 -> 12, of which waited for: 6 -> 4; matrix products, arithmetic and copies ran while one was open for 2% -> 2% of each run, Pallas kernels for 15% -> 15%
where the time goes in v8:
time: 81.5 us; the launch traced here: 80.9 us
  starting transfers between devices  43.2 us (53%)
  Pallas kernels  16.9 us (21%)
  waiting for transfers between devices  10.8 us (13%)
  local copies, waits for them, and re-layouts  8.44 us (10%)
  other arithmetic  0.83 us (1%)
  between operations  0.82 us (1%)
    ppermute x9, starting transfers between devices, swap(): lax.ppermute(value, axis, [(k, k ^ flip) for k in range(lax.axis_size(axi...  20.7 us
    all_to_all x1, starting transfers between devices, on_device(): lax.all_to_all(panel.reshape(col_count, size, lanes), 'col', 0, 0, axis_i...  9.33 us
    unnamed x6, local copies, waits for them, and re-layouts  7.67 us
    all_to_all x1, starting transfers between devices, on_device(): lax.all_to_all(rows.reshape(SITES, share, lanes), 'col', 0, 0, axis_index...  7.45 us
    ppermute x9, waiting for transfers between devices, swap(): lax.ppermute(value, axis, [(k, k ^ flip) for k in range(lax.axis_size(axi...  7.38 us
    all_to_all x1, starting transfers between devices, on_device(): near = lax.all_to_all(packed, 'col', 0, 0, axis_index_groups=one_core)  5.68 us
    pallas_call x1, Pallas kernels, row_products(): pl.pallas_call(row_kernel, in_specs=[SMEM, HBM, VMEM], out_specs=[VMEM, V...  5.64 us
    pallas_call x1, Pallas kernels, col_products(): pl.pallas_call(col_kernel, in_specs=[SMEM, VMEM, VMEM, VMEM], out_specs=[...  4.01 us
  transfers between devices with their start and end apart: 12, of which 4 were waited for; matrix products, arithmetic and copies ran while one was open for 2% of the time, Pallas kernels for 15%

profile of v8, /device:TPU:6, one launch (start us, length us, event | category | flops | bytes accessed | tf_op | source)
XLA Modules:
  0.0 80.9 jit_solution(13531906815602032702)
XLA Ops:
  0.6 9.3 %all-to-all-start = ((bf16[64,32,128]{2,1,0:T(8,128)(2,1)}), bf16[64,32,128]{2,1,0:T(8,128)(2,1)S(1)}, u32[]{:S(2)}, u32[]{:S(2)}) async-start(bf16[64,32,128]{2,1,0:T(8,128)(2,1)} %bitcast.18), calls=%async_computation | async-start | bytes 1048576 | tf_op jit(solution)/shard_map/all_to_all | solution.py:399
  10.9 1.0 %copy-done.2 = bf16[2048,128]{1,0:T(8,128)(2,1)S(1)} copy-done((bf16[2048,128]{1,0:T(8,128)(2,1)S(1)}, bf16[2048,128]{1,0:T(8,128)(2,1)}, u32[]{:S(2)}) %copy-start.2) | copy-done | bytes 524312
  11.9 5.6 %shard_map.59 = (f32[1024,128]{1,0:T(8,128)S(1)}, f32[1024,128]{1,0:T(8,128)S(1)}) custom-call(s32[5,4]{1,0:T(8,128)S(1)} %stack.46.info, bf16[4,1024,1024]{2,1,0:T(8,128)(2,1)} %tiles_ref.3, bf16[2048,128]{1,0:T(8,128)(2,1)S(1)} %copy-done.2), custom_call_target="tpu_custom_call" | custom-call | flops 1073741824 | bytes 10485760 | tf_op jit(solution)/shard_map/pallas_call | solution.py:309
  17.6 3.4 %all-to-all-done = bf16[64,32,128]{2,1,0:T(8,128)(2,1)S(1)} async-done(((bf16[64,32,128]{2,1,0:T(8,128)(2,1)}), bf16[64,32,128]{2,1,0:T(8,128)(2,1)S(1)}, u32[]{:S(2)}, u32[]{:S(2)}) %all-to-all-start) | async-done | bytes 524320 | tf_op jit(solution)/shard_map/all_to_all | solution.py:399
  21.1 0.7 broadcast_in_dim.20
  21.9 5.7 %all-to-all-start.1 = ((bf16[32,32,128]{2,1,0:T(8,128)(2,1)}), bf16[32,32,128]{2,1,0:T(8,128)(2,1)S(1)}, u32[]{:S(2)}, u32[]{:S(2)}) async-start(bf16[32,32,128]{2,1,0:T(8,128)(2,1)} %broadcast_in_dim.20), calls=%async_computation.1 | async-start | bytes 524288 | tf_op jit(solution)/shard_map/all_to_all | solution.py:413
  27.7 1.6 %collective-permute-start.1 = (s16[528,128]{1,0:T(8,128)(2,1)S(1)}, s16[528,128]{1,0:T(8,128)(2,1)S(1)}, u32[]{:S(2)}, u32[]{:S(2)}) collective-permute-start(s16[528,128]{1,0:T(8,128)(2,1)S(1)} %get-tuple-element.23.after_ref), channel_id=1, source_target_pairs={{0,2},{1,3},{2,0},{3,1},{4,6},{5,7},{6,4},{7,5},{8,10},{9,11},{10,... | collective-permute-start | bytes 405512 | tf_op jit(solution)/shard_map/ppermute | solution.py:351
  29.2 3.5 %shard_map.61 = (bf16[4,1024,1024]{2,1,0:T(8,128)(2,1)S(1)}, f32[8,128]{1,0:T(8,128)S(1)}) custom-call(bf16[4,1024,1024]{2,1,0:T(8,128)(2,1)} %tiles_ref.3, s16[528,128]{1,0:T(8,128)(2,1)S(1)} %get-tuple-element.23.after_ref), custom_call_target="tpu_custom_call" | custom-call | tf_op jit(solution)/shard_map/pallas_call | solution.py:321
  32.7 3.2 %copy-done = bf16[4,1024,1024]{2,1,0:T(8,128)(2,1)} copy-done((bf16[4,1024,1024]{2,1,0:T(8,128)(2,1)}, bf16[4,1024,1024]{2,1,0:T(8,128)(2,1)S(1)}, u32[]{:S(2)}) %copy-start) | copy-done | bytes 8388632
  36.0 1.5 %collective-permute-done.2.far_ref = bf16[32,32,128]{2,1,0:T(8,128)(2,1)S(1)} collective-permute-done((bf16[32,32,128]{2,1,0:T(8,128)(2,1)S(1)}, bf16[32,32,128]{2,1,0:T(8,128)(2,1)S(1)}, u32[]{:S(2)}, u32[]{:S(2)}) %collective-permute-start.2) | collective-permute-done | bytes 262176 | tf_op jit(solution)/shard_map/ppermute | solution.py:351
  37.5 3.4 %copy-done.1 = bf16[4,1024,1024]{2,1,0:T(8,128)(2,1)S(1)} copy-done((bf16[4,1024,1024]{2,1,0:T(8,128)(2,1)S(1)}, bf16[4,1024,1024]{2,1,0:T(8,128)(2,1)}, u32[]{:S(2)}) %copy-start.1) | copy-done | bytes 8388632
  40.9 4.0 %shard_map.62 = (f32[2,512,128]{2,1,0:T(8,128)S(1)}, s16[528,128]{1,0:T(8,128)(2,1)S(1)}, s16[528,128]{1,0:T(8,128)(2,1)S(1)}) custom-call(s32[5,4]{1,0:T(8,128)S(1)} %stack.46.info, bf16[4,1024,1024]{2,1,0:T(8,128)(2,1)S(1)} %copy-done.1, bf16[32,32,128]{2,1,0:T(8,128)(2,1)S(1)} %all-to-all-done.1.near_ref, ...), custom_call_target="tpu_custom_call" | custom-call | flops 1073741824 | bytes 10485760 | tf_op jit(solution)/shard_map/pallas_call | solution.py:335
  44.9 3.4 %collective-permute-start.3 = (s16[528,128]{1,0:T(8,128)(2,1)S(1)}, s16[528,128]{1,0:T(8,128)(2,1)S(1)}, u32[]{:S(2)}, u32[]{:S(2)}) collective-permute-start(s16[528,128]{1,0:T(8,128)(2,1)S(1)} %get-tuple-element.29), channel_id=1, source_target_pairs={{0,64},{64,0},{128,192},{192,128},{1,65},{65,1},{129,193},{193,129... | collective-permute-start | bytes 405512 | tf_op jit(solution)/shard_map/ppermute | solution.py:351
  48.3 3.6 %collective-permute-start.6 = (s16[528,128]{1,0:T(8,128)(2,1)S(1)}, s16[528,128]{1,0:T(8,128)(2,1)S(1)}, u32[]{:S(2)}, u32[]{:S(2)}) collective-permute-start(s16[528,128]{1,0:T(8,128)(2,1)S(1)} %get-tuple-element.31), channel_id=1, source_target_pairs={{0,192},{64,128},{128,64},{192,0},{1,193},{65,129},{129,65},{193,1... | collective-permute-start | bytes 405512 | tf_op jit(solution)/shard_map/ppermute | solution.py:351
  51.9 3.3 %collective-permute-done.3.got_ref = s16[528,128]{1,0:T(8,128)(2,1)S(1)} collective-permute-done((s16[528,128]{1,0:T(8,128)(2,1)S(1)}, s16[528,128]{1,0:T(8,128)(2,1)S(1)}, u32[]{:S(2)}, u32[]{:S(2)}) %collective-permute-start.3) | collective-permute-done | bytes 135200 | tf_op jit(solution)/shard_map/ppermute | solution.py:351
  55.3 2.7 %collective-permute-start.4 = (s16[528,128]{1,0:T(8,128)(2,1)S(1)}, s16[528,128]{1,0:T(8,128)(2,1)S(1)}, u32[]{:S(2)}, u32[]{:S(2)}) collective-permute-start(s16[528,128]{1,0:T(8,128)(2,1)S(1)} %shard_map.63.after_ref.own_ref), channel_id=1, source_target_pairs={{0,192},{64,128},{128,64},{192,0},{1,193},{65,129},{129,65},{193,1... | collective-permute-start | bytes 405512 | tf_op jit(solution)/shard_map/ppermute | solution.py:351
  58.1 3.5 %collective-permute-start.7 = (s16[528,128]{1,0:T(8,128)(2,1)S(1)}, s16[528,128]{1,0:T(8,128)(2,1)S(1)}, u32[]{:S(2)}, u32[]{:S(2)}) collective-permute-start(s16[528,128]{1,0:T(8,128)(2,1)S(1)} %shard_map.67.own_ref), channel_id=1, source_target_pairs={{0,64},{64,0},{128,192},{192,128},{1,65},{65,1},{129,193},{193,129... | collective-permute-start | bytes 405512 | tf_op jit(solution)/shard_map/ppermute | solution.py:351
  61.6 0.7 shard_map.64
  62.3 7.4 %all-to-all-start.2 = ((f32[16,32,128]{2,1,0:T(8,128)}), f32[16,32,128]{2,1,0:T(8,128)S(1)}, u32[]{:S(2)}, u32[]{:S(2)}) async-start(f32[16,32,128]{2,1,0:T(8,128)} %bitcast.11), calls=%async_computation.2 | async-start | bytes 524288 | tf_op jit(solution)/shard_map/all_to_all | solution.py:421
  69.9 1.5 %collective-permute-start.5 = (s16[528,128]{1,0:T(8,128)(2,1)S(1)}, s16[528,128]{1,0:T(8,128)(2,1)S(1)}, u32[]{:S(2)}, u32[]{:S(2)}) collective-permute-start(s16[528,128]{1,0:T(8,128)(2,1)S(1)} %shard_map.66.half0_ref), channel_id=1, source_target_pairs={{0,64},{64,0},{128,192},{192,128},{1,65},{65,1},{129,193},{193,129... | collective-permute-start | bytes 405512 | tf_op jit(solution)/shard_map/ppermute | solution.py:351
  71.6 4.4 %collective-permute-start.8 = (s16[528,128]{1,0:T(8,128)(2,1)S(1)}, s16[528,128]{1,0:T(8,128)(2,1)S(1)}, u32[]{:S(2)}, u32[]{:S(2)}) collective-permute-start(s16[528,128]{1,0:T(8,128)(2,1)S(1)} %shard_map.68.half1_ref), channel_id=1, source_target_pairs={{0,192},{64,128},{128,64},{192,0},{1,193},{65,129},{129,65},{193,1... | collective-permute-start | bytes 405512 | tf_op jit(solution)/shard_map/ppermute | solution.py:351
  76.0 0.8 %shard_map.69.result_ref = f32[2048,128]{1,0:T(8,128)} custom-call(s16[528,128]{1,0:T(8,128)(2,1)S(1)} %shard_map.66.half0_ref, s16[528,128]{1,0:T(8,128)(2,1)S(1)} %shard_map.68.half1_ref), custom_call_target="tpu_custom_call" | custom-call | tf_op jit(solution)/shard_map/pallas_call | solution.py:258
  77.5 2.6 %collective-permute-done.8.half1_ref = s16[528,128]{1,0:T(8,128)(2,1)S(1)} collective-permute-done((s16[528,128]{1,0:T(8,128)(2,1)S(1)}, s16[528,128]{1,0:T(8,128)(2,1)S(1)}, u32[]{:S(2)}, u32[]{:S(2)}) %collective-permute-start.8) | collective-permute-done | bytes 135200 | tf_op jit(solution)/shard_map/ppermute | solution.py:351
  80.0 0.8 %shard_map.70 = f32[2048,128]{1,0:T(8,128)} custom-call(s16[528,128]{1,0:T(8,128)(2,1)S(1)} %collective-permute-done.5.half0_ref, s16[528,128]{1,0:T(8,128)(2,1)S(1)} %collective-permute-done.8.half1_ref, f32[2048,128]{1,0:T(8,128)} %shard_map.69.result_ref), custom_call_target="tpu_custom_call", output_to_operand_aliasing={{}: (2, {})} | custom-call | tf_op jit(solution)/shard_map/pallas_call | solution.py:270
  (25 shorter events, 2.4 us)
Async XLA Ops:
  0.6 20.3 %all-to-all-start = ((bf16[64,32,128]{2,1,0:T(8,128)(2,1)}), bf16[64,32,128]{2,1,0:T(8,128)(2,1)S(1)}, u32[]{:S(2)}, u32[]{:S(2)}) async-start(bf16[64,32,128]{2,1,0:T(8,128)(2,1)} %bitcast.18), calls=%async_computation | async-start | bytes 1048576 | tf_op jit(solution)/shard_map/all_to_all | solution.py:399
  10.9 1.0 %copy-start.2 = (bf16[2048,128]{1,0:T(8,128)(2,1)S(1)}, bf16[2048,128]{1,0:T(8,128)(2,1)}, u32[]{:S(2)}) copy-start(bf16[2048,128]{1,0:T(8,128)(2,1)} %panel_ref.1) | copy-start | bytes 1572868
  20.9 6.6 %collective-permute-start = (f32[1024,128]{1,0:T(8,128)S(1)}, f32[1024,128]{1,0:T(8,128)S(1)}, u32[]{:S(2)}, u32[]{:S(2)}) collective-permute-start(f32[1024,128]{1,0:T(8,128)S(1)} %get-tuple-element.20), channel_id=1, source_target_pairs={{0,1},{1,0},{2,3},{3,2},{4,5},{5,4},{6,7},{7,6},{8,9},{9,8},{10,11... | collective-permute-start | bytes 1572872 | tf_op jit(solution)/shard_map/ppermute | solution.py:351
  21.9 14.1 %all-to-all-start.1 = ((bf16[32,32,128]{2,1,0:T(8,128)(2,1)}), bf16[32,32,128]{2,1,0:T(8,128)(2,1)S(1)}, u32[]{:S(2)}, u32[]{:S(2)}) async-start(bf16[32,32,128]{2,1,0:T(8,128)(2,1)} %broadcast_in_dim.20), calls=%async_computation.1 | async-start | bytes 524288 | tf_op jit(solution)/shard_map/all_to_all | solution.py:413
  27.7 8.3 %collective-permute-start.1 = (s16[528,128]{1,0:T(8,128)(2,1)S(1)}, s16[528,128]{1,0:T(8,128)(2,1)S(1)}, u32[]{:S(2)}, u32[]{:S(2)}) collective-permute-start(s16[528,128]{1,0:T(8,128)(2,1)S(1)} %get-tuple-element.23.after_ref), channel_id=1, source_target_pairs={{0,2},{1,3},{2,0},{3,1},{4,6},{5,7},{6,4},{7,5},{8,10},{9,11},{10,... | collective-permute-start | bytes 405512 | tf_op jit(solution)/shard_map/ppermute | solution.py:351
  32.7 3.3 %copy-start = (bf16[4,1024,1024]{2,1,0:T(8,128)(2,1)}, bf16[4,1024,1024]{2,1,0:T(8,128)(2,1)S(1)}, u32[]{:S(2)}) copy-start(bf16[4,1024,1024]{2,1,0:T(8,128)(2,1)S(1)} %get-tuple-element.26.held) | copy-start | bytes 25165828
  36.0 1.5 %collective-permute-start.2 = (bf16[32,32,128]{2,1,0:T(8,128)(2,1)S(1)}, bf16[32,32,128]{2,1,0:T(8,128)(2,1)S(1)}, u32[]{:S(2)}, u32[]{:S(2)}) collective-permute-start(bf16[32,32,128]{2,1,0:T(8,128)(2,1)S(1)} %all-to-all-done.1.near_ref), channel_id=1, source_target_pairs={{0,1},{1,0},{2,3},{3,2},{4,5},{5,4},{6,7},{7,6},{8,9},{9,8},{10,11... | collective-permute-start | bytes 786440 | tf_op jit(solution)/shard_map/ppermute | solution.py:351
  37.5 3.4 %copy-start.1 = (bf16[4,1024,1024]{2,1,0:T(8,128)(2,1)S(1)}, bf16[4,1024,1024]{2,1,0:T(8,128)(2,1)}, u32[]{:S(2)}) copy-start(bf16[4,1024,1024]{2,1,0:T(8,128)(2,1)} %copy-done) | copy-start | bytes 25165828
  44.9 10.2 %collective-permute-start.3 = (s16[528,128]{1,0:T(8,128)(2,1)S(1)}, s16[528,128]{1,0:T(8,128)(2,1)S(1)}, u32[]{:S(2)}, u32[]{:S(2)}) collective-permute-start(s16[528,128]{1,0:T(8,128)(2,1)S(1)} %get-tuple-element.29), channel_id=1, source_target_pairs={{0,64},{64,0},{128,192},{192,128},{1,65},{65,1},{129,193},{193,129... | collective-permute-start | bytes 405512 | tf_op jit(solution)/shard_map/ppermute | solution.py:351
  48.3 9.7 %collective-permute-start.6 = (s16[528,128]{1,0:T(8,128)(2,1)S(1)}, s16[528,128]{1,0:T(8,128)(2,1)S(1)}, u32[]{:S(2)}, u32[]{:S(2)}) collective-permute-start(s16[528,128]{1,0:T(8,128)(2,1)S(1)} %get-tuple-element.31), channel_id=1, source_target_pairs={{0,192},{64,128},{128,64},{192,0},{1,193},{65,129},{129,65},{193,1... | collective-permute-start | bytes 405512 | tf_op jit(solution)/shard_map/ppermute | solution.py:351
  55.3 14.5 %collective-permute-start.4 = (s16[528,128]{1,0:T(8,128)(2,1)S(1)}, s16[528,128]{1,0:T(8,128)(2,1)S(1)}, u32[]{:S(2)}, u32[]{:S(2)}) collective-permute-start(s16[528,128]{1,0:T(8,128)(2,1)S(1)} %shard_map.63.after_ref.own_ref), channel_id=1, source_target_pairs={{0,192},{64,128},{128,64},{192,0},{1,193},{65,129},{129,65},{193,1... | collective-permute-start | bytes 405512 | tf_op jit(solution)/shard_map/ppermute | solution.py:351
  58.1 13.3 %collective-permute-start.7 = (s16[528,128]{1,0:T(8,128)(2,1)S(1)}, s16[528,128]{1,0:T(8,128)(2,1)S(1)}, u32[]{:S(2)}, u32[]{:S(2)}) collective-permute-start(s16[528,128]{1,0:T(8,128)(2,1)S(1)} %shard_map.67.own_ref), channel_id=1, source_target_pairs={{0,64},{64,0},{128,192},{192,128},{1,65},{65,1},{129,193},{193,129... | collective-permute-start | bytes 405512 | tf_op jit(solution)/shard_map/ppermute | solution.py:351
  62.3 14.5 %all-to-all-start.2 = ((f32[16,32,128]{2,1,0:T(8,128)}), f32[16,32,128]{2,1,0:T(8,128)S(1)}, u32[]{:S(2)}, u32[]{:S(2)}) async-start(f32[16,32,128]{2,1,0:T(8,128)} %bitcast.11), calls=%async_computation.2 | async-start | bytes 524288 | tf_op jit(solution)/shard_map/all_to_all | solution.py:421
  69.9 7.5 %collective-permute-start.5 = (s16[528,128]{1,0:T(8,128)(2,1)S(1)}, s16[528,128]{1,0:T(8,128)(2,1)S(1)}, u32[]{:S(2)}, u32[]{:S(2)}) collective-permute-start(s16[528,128]{1,0:T(8,128)(2,1)S(1)} %shard_map.66.half0_ref), channel_id=1, source_target_pairs={{0,64},{64,0},{128,192},{192,128},{1,65},{65,1},{129,193},{193,129... | collective-permute-start | bytes 405512 | tf_op jit(solution)/shard_map/ppermute | solution.py:351
  71.6 8.5 %collective-permute-start.8 = (s16[528,128]{1,0:T(8,128)(2,1)S(1)}, s16[528,128]{1,0:T(8,128)(2,1)S(1)}, u32[]{:S(2)}, u32[]{:S(2)}) collective-permute-start(s16[528,128]{1,0:T(8,128)(2,1)S(1)} %shard_map.68.half1_ref), channel_id=1, source_target_pairs={{0,192},{64,128},{128,64},{192,0},{1,193},{65,129},{129,65},{193,1... | collective-permute-start | bytes 405512 | tf_op jit(solution)/shard_map/ppermute | solution.py:351

commit v9 on v8

--- a/solution.py
+++ b/solution.py
@@ -94,8 +94,8 @@
     encode(keep_ref[size:, :] + got_ref[size:, :], send_ref)
 
 
-def rows_kernel(mine_ref, got_ref, after_ref, token_ref, out_ref):
-    del after_ref, token_ref
+def rows_kernel(mine_ref, got_ref, after_ref, out_ref):
+    del after_ref
     out_ref[...] = mine_ref[...] + decode(got_ref)
 
 
@@ -142,32 +142,14 @@
     return jnp.concatenate(parts, axis=0)
 
 
-def fetch_kernel(tiles_ref, after_ref, held_ref, token_ref, sems):
-    del after_ref
-    slots, width, _ = held_ref.shape
-    depth = width // STEPS
-    copies = []
-    for index in range(slots * STEPS):
-        piece = pl.ds(index % STEPS * depth, depth)
-        copies.append(
-            pltpu.make_async_copy(
-                tiles_ref.at[index // STEPS, piece],
-                held_ref.at[index // STEPS, piece],
-                sems.at[index],
-            )
-        )
-    for copy in copies:
-        copy.start()
-    token_ref[...] = jnp.zeros_like(token_ref)
-    for copy in copies:
-        copy.wait()
-
-
 def col_kernel(
-    info, held, near_ref, far_ref, keep_ref, send0_ref, send1_ref, slab, total, result
+    info, tiles_ref, near_ref, far_ref, keep_ref, send0_ref, send1_ref, slab, total, result, held, sems
 ):
     slots, width, _ = held.shape
     depth = width // STEPS
+    fetch = fetch_of(info, tiles_ref, held, sems)
+    for index in range(slots * STEPS):
+        fetch(index).start()
     total[...] = jnp.zeros_like(total)
     core = info[4, 0]
     for ref, tile in ((near_ref, core), (far_ref, 1 - core)):
@@ -177,6 +159,7 @@
     @pl.loop(0, slots * STEPS)
     def _(index):
         slot, part, rows, cols, piece = place_of(info, index, depth, width)
+        fetch(index).wait()
 
         @pl.when(info[2, slot] == 1)
         def _():
@@ -317,31 +300,21 @@
     )(info, grm_tiles, panel)
 
 
-def fetch_tiles(grm_tiles, after):
-    return pl.pallas_call(
-        fetch_kernel,
-        in_specs=[HBM, VMEM],
-        out_specs=[VMEM, VMEM],
-        out_shape=[pltpu.VMEM(grm_tiles.shape, grm_tiles.dtype), floats(8, 128)],
-        scratch_shapes=[pltpu.SemaphoreType.DMA((grm_tiles.shape[0] * STEPS,))],
-        compiler_params=limit(12),
-    )(grm_tiles, after)
-
-
 def col_products(info, grm_tiles, near, far):
     slots, width, _ = grm_tiles.shape
     lanes = near.shape[2]
     half = width // 2
     return pl.pallas_call(
         col_kernel,
-        in_specs=[SMEM, VMEM, VMEM, VMEM],
+        in_specs=[SMEM, HBM, VMEM, VMEM],
         out_specs=[VMEM] * 3,
         out_shape=[floats(2, half, lanes), coded(half, lanes), coded(half, lanes)],
         scratch_shapes=[
             pltpu.VMEM((RT_DEV * width, lanes), near.dtype),
             pltpu.VMEM((lanes, CTD * width), jnp.float32),
             pltpu.VMEM((CTD * width, lanes), jnp.float32),
-        ],
+        ]
+        + tile_scratch(grm_tiles),
         compiler_params=limit(24),
         cost_estimate=tile_cost(grm_tiles.shape, lanes),
     )(info, grm_tiles, near, far)
@@ -411,13 +384,11 @@
     piece = lax.dynamic_index_in_dim(pieces, place, 0)
     packed = jnp.broadcast_to(piece, (chips, size, lanes))
     near = lax.all_to_all(packed, "col", 0, 0, axis_index_groups=one_core)
-    got_z = swap(send_z, "col", 2)
-    held, token = fetch_tiles(tiles, send_z)
-    near, got_z, token = lax.optimization_barrier((near, got_z, token))
+    near, got_z = lax.optimization_barrier((near, swap(send_z, "col", 2)))
     far = swap(near, "col", 1)
-    keep, *sends = col_products(info, held, near, far)
+    keep, *sends = col_products(info, tiles, near, far)
     gots, result, begun = sum_over_row(keep, sends)
-    rows = small_call(rows_kernel, [floats(half, lanes)], mine, got_z, begun, token)[0]
+    rows = small_call(rows_kernel, [floats(half, lanes)], mine, got_z, begun)[0]
     terms = lax.all_to_all(
         rows.reshape(SITES, share, lanes), "col", 0, 0, axis_index_groups=across
     )

time: 81.5 us -> 79.1 us (0.971)
  waiting for transfers between devices: 10.8 us -> 19.8 us
  local copies, waits for them, and re-layouts: 8.44 us -> 1.81 us
  Pallas kernels: 16.9 us -> 14.6 us
  starting transfers between devices: 43.2 us -> 41.1 us
    unnamed x6 -> x2, local copies, waits for them, and re-layouts: 7.67 us -> 1.04 us
    all_to_all x1, waiting for transfers between devices: 0.01 us -> 6.43 us  [on_device(): near = lax.all_to_all(packed, 'col', 0, 0, axis_index_groups=one_core)]
    pallas_call x2 -> x1, Pallas kernels: 7.48 us -> 5.24 us  [col_products(): pl.pallas_call(col_kernel, in_specs=[SMEM, HBM, VMEM, VMEM], out_specs=[V...]
    ppermute x9, starting transfers between devices: 20.7 us -> 18.6 us  [swap(): lax.ppermute(value, axis, [(k, k ^ flip) for k in range(lax.axis_size(axi...]
    all_to_all x1, waiting for transfers between devices: 0.01 us -> 1.3 us  [on_device(): lax.all_to_all(rows.reshape(SITES, share, lanes), 'col', 0, 0, axis_index...]
    ppermute x9, waiting for transfers between devices: 7.38 us -> 8.66 us  [swap(): lax.ppermute(value, axis, [(k, k ^ flip) for k in range(lax.axis_size(axi...]
  transfers between devices with their start and end apart: 12 -> 12, of which waited for: 4 -> 8; matrix products, arithmetic and copies ran while one was open for 2% -> 2% of each run, Pallas kernels for 15% -> 11%
where the time goes in v9:
time: 79.1 us; the launch traced here: 78.9 us
  starting transfers between devices  41.1 us (52%)
  waiting for transfers between devices  19.8 us (25%)
  Pallas kernels  14.6 us (18%)
  local copies, waits for them, and re-layouts  1.81 us (2%)
  other arithmetic  0.83 us (1%)
    ppermute x9, starting transfers between devices, swap(): lax.ppermute(value, axis, [(k, k ^ flip) for k in range(lax.axis_size(axi...  18.6 us
    all_to_all x1, starting transfers between devices, on_device(): lax.all_to_all(panel.reshape(col_count, size, lanes), 'col', 0, 0, axis_i...  9.33 us
    ppermute x9, waiting for transfers between devices, swap(): lax.ppermute(value, axis, [(k, k ^ flip) for k in range(lax.axis_size(axi...  8.66 us
    all_to_all x1, starting transfers between devices, on_device(): lax.all_to_all(rows.reshape(SITES, share, lanes), 'col', 0, 0, axis_index...  7.5 us
    all_to_all x1, waiting for transfers between devices, on_device(): near = lax.all_to_all(packed, 'col', 0, 0, axis_index_groups=one_core)  6.43 us
    all_to_all x1, starting transfers between devices, on_device(): near = lax.all_to_all(packed, 'col', 0, 0, axis_index_groups=one_core)  5.68 us
    pallas_call x1, Pallas kernels, row_products(): pl.pallas_call(row_kernel, in_specs=[SMEM, HBM, VMEM], out_specs=[VMEM, V...  5.64 us
    pallas_call x1, Pallas kernels, col_products(): pl.pallas_call(col_kernel, in_specs=[SMEM, HBM, VMEM, VMEM], out_specs=[V...  5.24 us
  transfers between devices with their start and end apart: 12, of which 8 were waited for; matrix products, arithmetic and copies ran while one was open for 2% of the time, Pallas kernels for 11%

profile of v9, /device:TPU:6, one launch (start us, length us, event | category | flops | bytes accessed | tf_op | source)
XLA Modules:
  0.0 78.9 jit_solution(12720138744998116813)
XLA Ops:
  0.6 9.3 %all-to-all-start = ((bf16[64,32,128]{2,1,0:T(8,128)(2,1)}), bf16[64,32,128]{2,1,0:T(8,128)(2,1)S(1)}, u32[]{:S(2)}, u32[]{:S(2)}) async-start(bf16[64,32,128]{2,1,0:T(8,128)(2,1)} %bitcast.18), calls=%async_computation | async-start | bytes 1048576 | tf_op jit(solution)/shard_map/all_to_all | solution.py:372
  10.2 0.7 fusion
  10.9 1.0 %copy-done = bf16[2048,128]{1,0:T(8,128)(2,1)S(1)} copy-done((bf16[2048,128]{1,0:T(8,128)(2,1)S(1)}, bf16[2048,128]{1,0:T(8,128)(2,1)}, u32[]{:S(2)}) %copy-start) | copy-done | bytes 524312
  11.9 5.6 %shard_map.59 = (f32[1024,128]{1,0:T(8,128)S(1)}, f32[1024,128]{1,0:T(8,128)S(1)}) custom-call(s32[5,4]{1,0:T(8,128)S(1)} %stack.46.info, bf16[4,1024,1024]{2,1,0:T(8,128)(2,1)} %tiles_ref.3, bf16[2048,128]{1,0:T(8,128)(2,1)S(1)} %copy-done), custom_call_target="tpu_custom_call" | custom-call | flops 1073741824 | bytes 10485760 | tf_op jit(solution)/shard_map/pallas_call | solution.py:292
  17.6 3.4 %all-to-all-done = bf16[64,32,128]{2,1,0:T(8,128)(2,1)S(1)} async-done(((bf16[64,32,128]{2,1,0:T(8,128)(2,1)}), bf16[64,32,128]{2,1,0:T(8,128)(2,1)S(1)}, u32[]{:S(2)}, u32[]{:S(2)}) %all-to-all-start) | async-done | bytes 524320 | tf_op jit(solution)/shard_map/all_to_all | solution.py:372
  21.1 0.7 broadcast_in_dim.20
  21.9 5.7 %all-to-all-start.1 = ((bf16[32,32,128]{2,1,0:T(8,128)(2,1)}), bf16[32,32,128]{2,1,0:T(8,128)(2,1)S(1)}, u32[]{:S(2)}, u32[]{:S(2)}) async-start(bf16[32,32,128]{2,1,0:T(8,128)(2,1)} %broadcast_in_dim.20), calls=%async_computation.1 | async-start | bytes 524288 | tf_op jit(solution)/shard_map/all_to_all | solution.py:386
  27.7 1.6 %collective-permute-start.1 = (s16[528,128]{1,0:T(8,128)(2,1)S(1)}, s16[528,128]{1,0:T(8,128)(2,1)S(1)}, u32[]{:S(2)}, u32[]{:S(2)}) collective-permute-start(s16[528,128]{1,0:T(8,128)(2,1)S(1)} %get-tuple-element.20), channel_id=1, source_target_pairs={{0,2},{1,3},{2,0},{3,1},{4,6},{5,7},{6,4},{7,5},{8,10},{9,11},{10,... | collective-permute-start | bytes 405512 | tf_op jit(solution)/shard_map/ppermute | solution.py:324
  29.2 6.4 %all-to-all-done.1.near_ref = bf16[32,32,128]{2,1,0:T(8,128)(2,1)S(1)} async-done(((bf16[32,32,128]{2,1,0:T(8,128)(2,1)}), bf16[32,32,128]{2,1,0:T(8,128)(2,1)S(1)}, u32[]{:S(2)}, u32[]{:S(2)}) %all-to-all-start.1) | async-done | bytes 262176 | tf_op jit(solution)/shard_map/all_to_all | solution.py:386
  35.9 1.5 %collective-permute-done.2.far_ref = bf16[32,32,128]{2,1,0:T(8,128)(2,1)S(1)} collective-permute-done((bf16[32,32,128]{2,1,0:T(8,128)(2,1)S(1)}, bf16[32,32,128]{2,1,0:T(8,128)(2,1)S(1)}, u32[]{:S(2)}, u32[]{:S(2)}) %collective-permute-start.2) | collective-permute-done | bytes 262176 | tf_op jit(solution)/shard_map/ppermute | solution.py:324
  37.4 5.2 %shard_map.61 = (f32[2,512,128]{2,1,0:T(8,128)S(1)}, s16[528,128]{1,0:T(8,128)(2,1)S(1)}, s16[528,128]{1,0:T(8,128)(2,1)S(1)}) custom-call(s32[5,4]{1,0:T(8,128)S(1)} %stack.46.info, bf16[4,1024,1024]{2,1,0:T(8,128)(2,1)} %tiles_ref.3, bf16[32,32,128]{2,1,0:T(8,128)(2,1)S(1)} %all-to-all-done.1.near_ref, bf16[32,32,128]{2,1,0:T(8,128)(2,1)S(1)} %collective-permute-done.2.far_ref), custom_call_target="tpu_custom_call" | custom-call | flops 1073741824 | bytes 10485760 | tf_op jit(solution)/shard_map/pallas_call | solution.py:307
  42.7 3.4 %collective-permute-start.3 = (s16[528,128]{1,0:T(8,128)(2,1)S(1)}, s16[528,128]{1,0:T(8,128)(2,1)S(1)}, u32[]{:S(2)}, u32[]{:S(2)}) collective-permute-start(s16[528,128]{1,0:T(8,128)(2,1)S(1)} %get-tuple-element.24), channel_id=1, source_target_pairs={{0,64},{64,0},{128,192},{192,128},{1,65},{65,1},{129,193},{193,129... | collective-permute-start | bytes 405512 | tf_op jit(solution)/shard_map/ppermute | solution.py:324
  46.0 3.6 %collective-permute-start.6 = (s16[528,128]{1,0:T(8,128)(2,1)S(1)}, s16[528,128]{1,0:T(8,128)(2,1)S(1)}, u32[]{:S(2)}, u32[]{:S(2)}) collective-permute-start(s16[528,128]{1,0:T(8,128)(2,1)S(1)} %get-tuple-element.25), channel_id=1, source_target_pairs={{0,192},{64,128},{128,64},{192,0},{1,193},{65,129},{129,65},{193,1... | collective-permute-start | bytes 405512 | tf_op jit(solution)/shard_map/ppermute | solution.py:324
  49.6 3.3 %collective-permute-done.3.got_ref = s16[528,128]{1,0:T(8,128)(2,1)S(1)} collective-permute-done((s16[528,128]{1,0:T(8,128)(2,1)S(1)}, s16[528,128]{1,0:T(8,128)(2,1)S(1)}, u32[]{:S(2)}, u32[]{:S(2)}) %collective-permute-start.3) | collective-permute-done | bytes 135200 | tf_op jit(solution)/shard_map/ppermute | solution.py:324
  53.0 2.6 %collective-permute-start.4 = (s16[528,128]{1,0:T(8,128)(2,1)S(1)}, s16[528,128]{1,0:T(8,128)(2,1)S(1)}, u32[]{:S(2)}, u32[]{:S(2)}) collective-permute-start(s16[528,128]{1,0:T(8,128)(2,1)S(1)} %shard_map.62.after_ref.own_ref), channel_id=1, source_target_pairs={{0,192},{64,128},{128,64},{192,0},{1,193},{65,129},{129,65},{193,1... | collective-permute-start | bytes 405512 | tf_op jit(solution)/shard_map/ppermute | solution.py:324
  55.8 3.5 %collective-permute-start.7 = (s16[528,128]{1,0:T(8,128)(2,1)S(1)}, s16[528,128]{1,0:T(8,128)(2,1)S(1)}, u32[]{:S(2)}, u32[]{:S(2)}) collective-permute-start(s16[528,128]{1,0:T(8,128)(2,1)S(1)} %shard_map.66.own_ref), channel_id=1, source_target_pairs={{0,64},{64,0},{128,192},{192,128},{1,65},{65,1},{129,193},{193,129... | collective-permute-start | bytes 405512 | tf_op jit(solution)/shard_map/ppermute | solution.py:324
  59.3 0.7 shard_map.63
  60.0 7.5 %all-to-all-start.2 = ((f32[16,32,128]{2,1,0:T(8,128)}), f32[16,32,128]{2,1,0:T(8,128)S(1)}, u32[]{:S(2)}, u32[]{:S(2)}) async-start(f32[16,32,128]{2,1,0:T(8,128)} %bitcast.11), calls=%async_computation.2 | async-start | bytes 524288 | tf_op jit(solution)/shard_map/all_to_all | solution.py:392
  67.7 1.5 %collective-permute-start.5 = (s16[528,128]{1,0:T(8,128)(2,1)S(1)}, s16[528,128]{1,0:T(8,128)(2,1)S(1)}, u32[]{:S(2)}, u32[]{:S(2)}) collective-permute-start(s16[528,128]{1,0:T(8,128)(2,1)S(1)} %shard_map.65.half0_ref), channel_id=1, source_target_pairs={{0,64},{64,0},{128,192},{192,128},{1,65},{65,1},{129,193},{193,129... | collective-permute-start | bytes 405512 | tf_op jit(solution)/shard_map/ppermute | solution.py:324
  69.3 2.4 %collective-permute-start.8 = (s16[528,128]{1,0:T(8,128)(2,1)S(1)}, s16[528,128]{1,0:T(8,128)(2,1)S(1)}, u32[]{:S(2)}, u32[]{:S(2)}) collective-permute-start(s16[528,128]{1,0:T(8,128)(2,1)S(1)} %shard_map.67.half1_ref), channel_id=1, source_target_pairs={{0,192},{64,128},{128,64},{192,0},{1,193},{65,129},{129,65},{193,1... | collective-permute-start | bytes 405512 | tf_op jit(solution)/shard_map/ppermute | solution.py:324
  71.7 0.8 %shard_map.68.result_ref = f32[2048,128]{1,0:T(8,128)} custom-call(s16[528,128]{1,0:T(8,128)(2,1)S(1)} %shard_map.65.half0_ref, s16[528,128]{1,0:T(8,128)(2,1)S(1)} %shard_map.67.half1_ref), custom_call_target="tpu_custom_call" | custom-call | tf_op jit(solution)/shard_map/pallas_call | solution.py:241
  72.5 1.3 %all-to-all-done.2.terms_ref = f32[16,32,128]{2,1,0:T(8,128)S(1)} async-done(((f32[16,32,128]{2,1,0:T(8,128)}), f32[16,32,128]{2,1,0:T(8,128)S(1)}, u32[]{:S(2)}, u32[]{:S(2)}) %all-to-all-start.2) | async-done | bytes 262176 | tf_op jit(solution)/shard_map/all_to_all | solution.py:392
  74.6 3.4 %collective-permute-done.8.half1_ref = s16[528,128]{1,0:T(8,128)(2,1)S(1)} collective-permute-done((s16[528,128]{1,0:T(8,128)(2,1)S(1)}, s16[528,128]{1,0:T(8,128)(2,1)S(1)}, u32[]{:S(2)}, u32[]{:S(2)}) %collective-permute-start.8) | collective-permute-done | bytes 135200 | tf_op jit(solution)/shard_map/ppermute | solution.py:324
  78.1 0.8 %shard_map.69 = f32[2048,128]{1,0:T(8,128)} custom-call(s16[528,128]{1,0:T(8,128)(2,1)S(1)} %collective-permute-done.5.half0_ref, s16[528,128]{1,0:T(8,128)(2,1)S(1)} %collective-permute-done.8.half1_ref, f32[2048,128]{1,0:T(8,128)} %shard_map.68.result_ref), custom_call_target="tpu_custom_call", output_to_operand_aliasing={{}: (2, {})} | custom-call | tf_op jit(solution)/shard_map/pallas_call | solution.py:253
  (20 shorter events, 2.1 us)
Async XLA Ops:
  0.6 20.3 %all-to-all-start = ((bf16[64,32,128]{2,1,0:T(8,128)(2,1)}), bf16[64,32,128]{2,1,0:T(8,128)(2,1)S(1)}, u32[]{:S(2)}, u32[]{:S(2)}) async-start(bf16[64,32,128]{2,1,0:T(8,128)(2,1)} %bitcast.18), calls=%async_computation | async-start | bytes 1048576 | tf_op jit(solution)/shard_map/all_to_all | solution.py:372
  10.9 1.0 %copy-start = (bf16[2048,128]{1,0:T(8,128)(2,1)S(1)}, bf16[2048,128]{1,0:T(8,128)(2,1)}, u32[]{:S(2)}) copy-start(bf16[2048,128]{1,0:T(8,128)(2,1)} %panel_ref.1) | copy-start | bytes 1572868
  20.9 6.6 %collective-permute-start = (f32[1024,128]{1,0:T(8,128)S(1)}, f32[1024,128]{1,0:T(8,128)S(1)}, u32[]{:S(2)}, u32[]{:S(2)}) collective-permute-start(f32[1024,128]{1,0:T(8,128)S(1)} %get-tuple-element.17), channel_id=1, source_target_pairs={{0,1},{1,0},{2,3},{3,2},{4,5},{5,4},{6,7},{7,6},{8,9},{9,8},{10,11... | collective-permute-start | bytes 1572872 | tf_op jit(solution)/shard_map/ppermute | solution.py:324
  21.9 13.8 %all-to-all-start.1 = ((bf16[32,32,128]{2,1,0:T(8,128)(2,1)}), bf16[32,32,128]{2,1,0:T(8,128)(2,1)S(1)}, u32[]{:S(2)}, u32[]{:S(2)}) async-start(bf16[32,32,128]{2,1,0:T(8,128)(2,1)} %broadcast_in_dim.20), calls=%async_computation.1 | async-start | bytes 524288 | tf_op jit(solution)/shard_map/all_to_all | solution.py:386
  27.7 8.2 %collective-permute-start.1 = (s16[528,128]{1,0:T(8,128)(2,1)S(1)}, s16[528,128]{1,0:T(8,128)(2,1)S(1)}, u32[]{:S(2)}, u32[]{:S(2)}) collective-permute-start(s16[528,128]{1,0:T(8,128)(2,1)S(1)} %get-tuple-element.20), channel_id=1, source_target_pairs={{0,2},{1,3},{2,0},{3,1},{4,6},{5,7},{6,4},{7,5},{8,10},{9,11},{10,... | collective-permute-start | bytes 405512 | tf_op jit(solution)/shard_map/ppermute | solution.py:324
  35.9 1.5 %collective-permute-start.2 = (bf16[32,32,128]{2,1,0:T(8,128)(2,1)S(1)}, bf16[32,32,128]{2,1,0:T(8,128)(2,1)S(1)}, u32[]{:S(2)}, u32[]{:S(2)}) collective-permute-start(bf16[32,32,128]{2,1,0:T(8,128)(2,1)S(1)} %all-to-all-done.1.near_ref), channel_id=1, source_target_pairs={{0,1},{1,0},{2,3},{3,2},{4,5},{5,4},{6,7},{7,6},{8,9},{9,8},{10,11... | collective-permute-start | bytes 786440 | tf_op jit(solution)/shard_map/ppermute | solution.py:324
  42.7 10.2 %collective-permute-start.3 = (s16[528,128]{1,0:T(8,128)(2,1)S(1)}, s16[528,128]{1,0:T(8,128)(2,1)S(1)}, u32[]{:S(2)}, u32[]{:S(2)}) collective-permute-start(s16[528,128]{1,0:T(8,128)(2,1)S(1)} %get-tuple-element.24), channel_id=1, source_target_pairs={{0,64},{64,0},{128,192},{192,128},{1,65},{65,1},{129,193},{193,129... | collective-permute-start | bytes 405512 | tf_op jit(solution)/shard_map/ppermute | solution.py:324
  46.0 9.6 %collective-permute-start.6 = (s16[528,128]{1,0:T(8,128)(2,1)S(1)}, s16[528,128]{1,0:T(8,128)(2,1)S(1)}, u32[]{:S(2)}, u32[]{:S(2)}) collective-permute-start(s16[528,128]{1,0:T(8,128)(2,1)S(1)} %get-tuple-element.25), channel_id=1, source_target_pairs={{0,192},{64,128},{128,64},{192,0},{1,193},{65,129},{129,65},{193,1... | collective-permute-start | bytes 405512 | tf_op jit(solution)/shard_map/ppermute | solution.py:324
  53.0 14.5 %collective-permute-start.4 = (s16[528,128]{1,0:T(8,128)(2,1)S(1)}, s16[528,128]{1,0:T(8,128)(2,1)S(1)}, u32[]{:S(2)}, u32[]{:S(2)}) collective-permute-start(s16[528,128]{1,0:T(8,128)(2,1)S(1)} %shard_map.62.after_ref.own_ref), channel_id=1, source_target_pairs={{0,192},{64,128},{128,64},{192,0},{1,193},{65,129},{129,65},{193,1... | collective-permute-start | bytes 405512 | tf_op jit(solution)/shard_map/ppermute | solution.py:324
  55.8 13.4 %collective-permute-start.7 = (s16[528,128]{1,0:T(8,128)(2,1)S(1)}, s16[528,128]{1,0:T(8,128)(2,1)S(1)}, u32[]{:S(2)}, u32[]{:S(2)}) collective-permute-start(s16[528,128]{1,0:T(8,128)(2,1)S(1)} %shard_map.66.own_ref), channel_id=1, source_target_pairs={{0,64},{64,0},{128,192},{192,128},{1,65},{65,1},{129,193},{193,129... | collective-permute-start | bytes 405512 | tf_op jit(solution)/shard_map/ppermute | solution.py:324
  60.0 13.8 %all-to-all-start.2 = ((f32[16,32,128]{2,1,0:T(8,128)}), f32[16,32,128]{2,1,0:T(8,128)S(1)}, u32[]{:S(2)}, u32[]{:S(2)}) async-start(f32[16,32,128]{2,1,0:T(8,128)} %bitcast.11), calls=%async_computation.2 | async-start | bytes 524288 | tf_op jit(solution)/shard_map/all_to_all | solution.py:392
  67.7 6.9 %collective-permute-start.5 = (s16[528,128]{1,0:T(8,128)(2,1)S(1)}, s16[528,128]{1,0:T(8,128)(2,1)S(1)}, u32[]{:S(2)}, u32[]{:S(2)}) collective-permute-start(s16[528,128]{1,0:T(8,128)(2,1)S(1)} %shard_map.65.half0_ref), channel_id=1, source_target_pairs={{0,64},{64,0},{128,192},{192,128},{1,65},{65,1},{129,193},{193,129... | collective-permute-start | bytes 405512 | tf_op jit(solution)/shard_map/ppermute | solution.py:324
  69.3 8.7 %collective-permute-start.8 = (s16[528,128]{1,0:T(8,128)(2,1)S(1)}, s16[528,128]{1,0:T(8,128)(2,1)S(1)}, u32[]{:S(2)}, u32[]{:S(2)}) collective-permute-start(s16[528,128]{1,0:T(8,128)(2,1)S(1)} %shard_map.67.half1_ref), channel_id=1, source_target_pairs={{0,192},{64,128},{128,64},{192,0},{1,193},{65,129},{129,65},{193,1... | collective-permute-start | bytes 405512 | tf_op jit(solution)/shard_map/ppermute | solution.py:324

commit v10 on v9

--- a/solution.py
+++ b/solution.py
@@ -143,18 +143,25 @@
 
 
 def col_kernel(
-    info, tiles_ref, near_ref, far_ref, keep_ref, send0_ref, send1_ref, slab, total, result, held, sems
+    info_ref, tiles_ref, near_ref, far_ref, keep_ref, send0_ref, send1_ref, slab, total, result, held, sems, info, info_sem
 ):
     slots, width, _ = held.shape
     depth = width // STEPS
+    info_copy = pltpu.make_async_copy(info_ref, info, info_sem)
+    info_copy.start()
     fetch = fetch_of(info, tiles_ref, held, sems)
     for index in range(slots * STEPS):
-        fetch(index).start()
+        slot, piece = index // STEPS, pl.ds(index % STEPS * depth, depth)
+        pltpu.make_async_copy(
+            tiles_ref.at[slot, piece], held.at[slot, piece], sems.at[index]
+        ).start()
     total[...] = jnp.zeros_like(total)
-    core = info[4, 0]
+    core = lax.axis_index("col") % 2
     for ref, tile in ((near_ref, core), (far_ref, 1 - core)):
         rows = pl.ds(pl.multiple_of(tile * width, width), width)
         slab[rows, :] = ref[...].reshape(width, slab.shape[1])
+
+    info_copy.wait()
 
     @pl.loop(0, slots * STEPS)
     def _(index):
@@ -306,7 +313,7 @@
     half = width // 2
     return pl.pallas_call(
         col_kernel,
-        in_specs=[SMEM, HBM, VMEM, VMEM],
+        in_specs=[pl.BlockSpec(memory_space=pl.ANY), HBM, VMEM, VMEM],
         out_specs=[VMEM] * 3,
         out_shape=[floats(2, half, lanes), coded(half, lanes), coded(half, lanes)],
         scratch_shapes=[
@@ -314,7 +321,8 @@
             pltpu.VMEM((lanes, CTD * width), jnp.float32),
             pltpu.VMEM((CTD * width, lanes), jnp.float32),
         ]
-        + tile_scratch(grm_tiles),
+        + tile_scratch(grm_tiles)
+        + [pltpu.SMEM(info.shape, info.dtype), pltpu.SemaphoreType.DMA],
         compiler_params=limit(24),
         cost_estimate=tile_cost(grm_tiles.shape, lanes),
     )(info, grm_tiles, near, far)

time: 79.1 us -> 78.2 us (0.989)
  waiting for transfers between devices: 19.8 us -> 18.1 us
  starting transfers between devices: 41.1 us -> 42.3 us
    all_to_all x1, waiting for transfers between devices: 1.3 us -> 0.13 us  [on_device(): lax.all_to_all(rows.reshape(SITES, share, lanes), 'col', 0, 0, axis_index...]
    ppermute x9, starting transfers between devices: 18.6 us -> 19.8 us  [swap(): lax.ppermute(value, axis, [(k, k ^ flip) for k in range(lax.axis_size(axi...]
where the time goes in v10:
time: 78.2 us; the launch traced here: 77.8 us
  starting transfers between devices  42.3 us (54%)
  waiting for transfers between devices  18.1 us (23%)
  Pallas kernels  14 us (18%)
  local copies, waits for them, and re-layouts  1.81 us (2%)
  other arithmetic  0.83 us (1%)
  between operations  0.79 us (1%)
    ppermute x9, starting transfers between devices, swap(): lax.ppermute(value, axis, [(k, k ^ flip) for k in range(lax.axis_size(axi...  19.8 us
    all_to_all x1, starting transfers between devices, on_device(): lax.all_to_all(panel.reshape(col_count, size, lanes), 'col', 0, 0, axis_i...  9.33 us
    ppermute x9, waiting for transfers between devices, swap(): lax.ppermute(value, axis, [(k, k ^ flip) for k in range(lax.axis_size(axi...  8.14 us
    all_to_all x1, starting transfers between devices, on_device(): lax.all_to_all(rows.reshape(SITES, share, lanes), 'col', 0, 0, axis_index...  7.5 us
    all_to_all x1, waiting for transfers between devices, on_device(): near = lax.all_to_all(packed, 'col', 0, 0, axis_index_groups=one_core)  6.43 us
    all_to_all x1, starting transfers between devices, on_device(): near = lax.all_to_all(packed, 'col', 0, 0, axis_index_groups=one_core)  5.68 us
    pallas_call x1, Pallas kernels, row_products(): pl.pallas_call(row_kernel, in_specs=[SMEM, HBM, VMEM], out_specs=[VMEM, V...  5.64 us
    pallas_call x1, Pallas kernels, col_products(): pl.pallas_call(col_kernel, in_specs=[pl.BlockSpec(memory_space=pl.ANY), H...  4.65 us
  transfers between devices with their start and end apart: 12, of which 8 were waited for; matrix products, arithmetic and copies ran while one was open for 2% of the time, Pallas kernels for 11%

profile of v10, /device:TPU:6, one launch (start us, length us, event | category | flops | bytes accessed | tf_op | source)
XLA Modules:
  0.0 77.8 jit_solution(9322240816763829420)
XLA Ops:
  0.6 9.3 %all-to-all-start = ((bf16[64,32,128]{2,1,0:T(8,128)(2,1)}), bf16[64,32,128]{2,1,0:T(8,128)(2,1)S(1)}, u32[]{:S(2)}, u32[]{:S(2)}) async-start(bf16[64,32,128]{2,1,0:T(8,128)(2,1)} %bitcast.18), calls=%async_computation | async-start | bytes 1048576 | tf_op jit(solution)/shard_map/all_to_all | solution.py:380
  10.2 0.7 fusion
  10.9 1.0 %copy-done = bf16[2048,128]{1,0:T(8,128)(2,1)S(1)} copy-done((bf16[2048,128]{1,0:T(8,128)(2,1)S(1)}, bf16[2048,128]{1,0:T(8,128)(2,1)}, u32[]{:S(2)}) %copy-start) | copy-done | bytes 524312
  11.9 5.6 %shard_map.59 = (f32[1024,128]{1,0:T(8,128)S(1)}, f32[1024,128]{1,0:T(8,128)S(1)}) custom-call(s32[5,4]{1,0:T(8,128)S(1)} %stack.46.info.info_ref, bf16[4,1024,1024]{2,1,0:T(8,128)(2,1)} %tiles_ref.3, bf16[2048,128]{1,0:T(8,128)(2,1)S(1)} %copy-done), custom_call_target="tpu_custom_call" | custom-call | flops 1073741824 | bytes 10485760 | tf_op jit(solution)/shard_map/pallas_call | solution.py:299
  17.6 3.4 %all-to-all-done = bf16[64,32,128]{2,1,0:T(8,128)(2,1)S(1)} async-done(((bf16[64,32,128]{2,1,0:T(8,128)(2,1)}), bf16[64,32,128]{2,1,0:T(8,128)(2,1)S(1)}, u32[]{:S(2)}, u32[]{:S(2)}) %all-to-all-start) | async-done | bytes 524320 | tf_op jit(solution)/shard_map/all_to_all | solution.py:380
  21.1 0.7 broadcast_in_dim.20
  21.9 5.7 %all-to-all-start.1 = ((bf16[32,32,128]{2,1,0:T(8,128)(2,1)}), bf16[32,32,128]{2,1,0:T(8,128)(2,1)S(1)}, u32[]{:S(2)}, u32[]{:S(2)}) async-start(bf16[32,32,128]{2,1,0:T(8,128)(2,1)} %broadcast_in_dim.20), calls=%async_computation.1 | async-start | bytes 524288 | tf_op jit(solution)/shard_map/all_to_all | solution.py:394
  27.7 1.6 %collective-permute-start.1 = (s16[528,128]{1,0:T(8,128)(2,1)S(1)}, s16[528,128]{1,0:T(8,128)(2,1)S(1)}, u32[]{:S(2)}, u32[]{:S(2)}) collective-permute-start(s16[528,128]{1,0:T(8,128)(2,1)S(1)} %get-tuple-element.20), channel_id=1, source_target_pairs={{0,2},{1,3},{2,0},{3,1},{4,6},{5,7},{6,4},{7,5},{8,10},{9,11},{10,... | collective-permute-start | bytes 405512 | tf_op jit(solution)/shard_map/ppermute | solution.py:332
  29.2 6.4 %all-to-all-done.1.near_ref = bf16[32,32,128]{2,1,0:T(8,128)(2,1)S(1)} async-done(((bf16[32,32,128]{2,1,0:T(8,128)(2,1)}), bf16[32,32,128]{2,1,0:T(8,128)(2,1)S(1)}, u32[]{:S(2)}, u32[]{:S(2)}) %all-to-all-start.1) | async-done | bytes 262176 | tf_op jit(solution)/shard_map/all_to_all | solution.py:394
  35.9 1.5 %collective-permute-done.2.far_ref = bf16[32,32,128]{2,1,0:T(8,128)(2,1)S(1)} collective-permute-done((bf16[32,32,128]{2,1,0:T(8,128)(2,1)S(1)}, bf16[32,32,128]{2,1,0:T(8,128)(2,1)S(1)}, u32[]{:S(2)}, u32[]{:S(2)}) %collective-permute-start.2) | collective-permute-done | bytes 262176 | tf_op jit(solution)/shard_map/ppermute | solution.py:332
  37.4 4.7 %shard_map.61 = (f32[2,512,128]{2,1,0:T(8,128)S(1)}, s16[528,128]{1,0:T(8,128)(2,1)S(1)}, s16[528,128]{1,0:T(8,128)(2,1)S(1)}) custom-call(s32[5,4]{1,0:T(8,128)S(1)} %stack.46.info.info_ref, bf16[4,1024,1024]{2,1,0:T(8,128)(2,1)} %tiles_ref.3, bf16[32,32,128]{2,1,0:T(8,128)(2,1)S(1)} %all-to-all-done.1.near_ref, ...), custom_call_target="tpu_custom_call" | custom-call | flops 1073741824 | bytes 10485760 | tf_op jit(solution)/shard_map/pallas_call | solution.py:314
  42.1 3.4 %collective-permute-start.3 = (s16[528,128]{1,0:T(8,128)(2,1)S(1)}, s16[528,128]{1,0:T(8,128)(2,1)S(1)}, u32[]{:S(2)}, u32[]{:S(2)}) collective-permute-start(s16[528,128]{1,0:T(8,128)(2,1)S(1)} %get-tuple-element.24), channel_id=1, source_target_pairs={{0,64},{64,0},{128,192},{192,128},{1,65},{65,1},{129,193},{193,129... | collective-permute-start | bytes 405512 | tf_op jit(solution)/shard_map/ppermute | solution.py:332
  45.5 3.6 %collective-permute-start.6 = (s16[528,128]{1,0:T(8,128)(2,1)S(1)}, s16[528,128]{1,0:T(8,128)(2,1)S(1)}, u32[]{:S(2)}, u32[]{:S(2)}) collective-permute-start(s16[528,128]{1,0:T(8,128)(2,1)S(1)} %get-tuple-element.25), channel_id=1, source_target_pairs={{0,192},{64,128},{128,64},{192,0},{1,193},{65,129},{129,65},{193,1... | collective-permute-start | bytes 405512 | tf_op jit(solution)/shard_map/ppermute | solution.py:332
  49.0 3.3 %collective-permute-done.3.got_ref = s16[528,128]{1,0:T(8,128)(2,1)S(1)} collective-permute-done((s16[528,128]{1,0:T(8,128)(2,1)S(1)}, s16[528,128]{1,0:T(8,128)(2,1)S(1)}, u32[]{:S(2)}, u32[]{:S(2)}) %collective-permute-start.3) | collective-permute-done | bytes 135200 | tf_op jit(solution)/shard_map/ppermute | solution.py:332
  52.5 2.6 %collective-permute-start.4 = (s16[528,128]{1,0:T(8,128)(2,1)S(1)}, s16[528,128]{1,0:T(8,128)(2,1)S(1)}, u32[]{:S(2)}, u32[]{:S(2)}) collective-permute-start(s16[528,128]{1,0:T(8,128)(2,1)S(1)} %shard_map.62.after_ref.own_ref), channel_id=1, source_target_pairs={{0,192},{64,128},{128,64},{192,0},{1,193},{65,129},{129,65},{193,1... | collective-permute-start | bytes 405512 | tf_op jit(solution)/shard_map/ppermute | solution.py:332
  55.2 3.5 %collective-permute-start.7 = (s16[528,128]{1,0:T(8,128)(2,1)S(1)}, s16[528,128]{1,0:T(8,128)(2,1)S(1)}, u32[]{:S(2)}, u32[]{:S(2)}) collective-permute-start(s16[528,128]{1,0:T(8,128)(2,1)S(1)} %shard_map.66.own_ref), channel_id=1, source_target_pairs={{0,64},{64,0},{128,192},{192,128},{1,65},{65,1},{129,193},{193,129... | collective-permute-start | bytes 405512 | tf_op jit(solution)/shard_map/ppermute | solution.py:332
  58.7 0.7 shard_map.63
  59.4 7.5 %all-to-all-start.2 = ((f32[16,32,128]{2,1,0:T(8,128)}), f32[16,32,128]{2,1,0:T(8,128)S(1)}, u32[]{:S(2)}, u32[]{:S(2)}) async-start(f32[16,32,128]{2,1,0:T(8,128)} %bitcast.11), calls=%async_computation.2 | async-start | bytes 524288 | tf_op jit(solution)/shard_map/all_to_all | solution.py:400
  67.1 1.5 %collective-permute-start.5 = (s16[528,128]{1,0:T(8,128)(2,1)S(1)}, s16[528,128]{1,0:T(8,128)(2,1)S(1)}, u32[]{:S(2)}, u32[]{:S(2)}) collective-permute-start(s16[528,128]{1,0:T(8,128)(2,1)S(1)} %shard_map.65.half0_ref), channel_id=1, source_target_pairs={{0,64},{64,0},{128,192},{192,128},{1,65},{65,1},{129,193},{193,129... | collective-permute-start | bytes 405512 | tf_op jit(solution)/shard_map/ppermute | solution.py:332
  68.7 3.5 %collective-permute-start.8 = (s16[528,128]{1,0:T(8,128)(2,1)S(1)}, s16[528,128]{1,0:T(8,128)(2,1)S(1)}, u32[]{:S(2)}, u32[]{:S(2)}) collective-permute-start(s16[528,128]{1,0:T(8,128)(2,1)S(1)} %shard_map.67.half1_ref), channel_id=1, source_target_pairs={{0,192},{64,128},{128,64},{192,0},{1,193},{65,129},{129,65},{193,1... | collective-permute-start | bytes 405512 | tf_op jit(solution)/shard_map/ppermute | solution.py:332
  72.3 0.8 %shard_map.68.result_ref = f32[2048,128]{1,0:T(8,128)} custom-call(s16[528,128]{1,0:T(8,128)(2,1)S(1)} %shard_map.65.half0_ref, s16[528,128]{1,0:T(8,128)(2,1)S(1)} %shard_map.67.half1_ref), custom_call_target="tpu_custom_call" | custom-call | tf_op jit(solution)/shard_map/pallas_call | solution.py:248
  73.2 0.6 shard_map.64
  74.0 2.9 %collective-permute-done.8.half1_ref = s16[528,128]{1,0:T(8,128)(2,1)S(1)} collective-permute-done((s16[528,128]{1,0:T(8,128)(2,1)S(1)}, s16[528,128]{1,0:T(8,128)(2,1)S(1)}, u32[]{:S(2)}, u32[]{:S(2)}) %collective-permute-start.8) | collective-permute-done | bytes 135200 | tf_op jit(solution)/shard_map/ppermute | solution.py:332
  77.0 0.8 %shard_map.69 = f32[2048,128]{1,0:T(8,128)} custom-call(s16[528,128]{1,0:T(8,128)(2,1)S(1)} %collective-permute-done.5.half0_ref, s16[528,128]{1,0:T(8,128)(2,1)S(1)} %collective-permute-done.8.half1_ref, f32[2048,128]{1,0:T(8,128)} %shard_map.68.result_ref), custom_call_target="tpu_custom_call", output_to_operand_aliasing={{}: (2, {})} | custom-call | tf_op jit(solution)/shard_map/pallas_call | solution.py:260
  (20 shorter events, 1.6 us)
Async XLA Ops:
  0.6 20.3 %all-to-all-start = ((bf16[64,32,128]{2,1,0:T(8,128)(2,1)}), bf16[64,32,128]{2,1,0:T(8,128)(2,1)S(1)}, u32[]{:S(2)}, u32[]{:S(2)}) async-start(bf16[64,32,128]{2,1,0:T(8,128)(2,1)} %bitcast.18), calls=%async_computation | async-start | bytes 1048576 | tf_op jit(solution)/shard_map/all_to_all | solution.py:380
  10.9 1.0 %copy-start = (bf16[2048,128]{1,0:T(8,128)(2,1)S(1)}, bf16[2048,128]{1,0:T(8,128)(2,1)}, u32[]{:S(2)}) copy-start(bf16[2048,128]{1,0:T(8,128)(2,1)} %panel_ref.1) | copy-start | bytes 1572868
  20.9 6.6 %collective-permute-start = (f32[1024,128]{1,0:T(8,128)S(1)}, f32[1024,128]{1,0:T(8,128)S(1)}, u32[]{:S(2)}, u32[]{:S(2)}) collective-permute-start(f32[1024,128]{1,0:T(8,128)S(1)} %get-tuple-element.17), channel_id=1, source_target_pairs={{0,1},{1,0},{2,3},{3,2},{4,5},{5,4},{6,7},{7,6},{8,9},{9,8},{10,11... | collective-permute-start | bytes 1572872 | tf_op jit(solution)/shard_map/ppermute | solution.py:332
  21.9 13.8 %all-to-all-start.1 = ((bf16[32,32,128]{2,1,0:T(8,128)(2,1)}), bf16[32,32,128]{2,1,0:T(8,128)(2,1)S(1)}, u32[]{:S(2)}, u32[]{:S(2)}) async-start(bf16[32,32,128]{2,1,0:T(8,128)(2,1)} %broadcast_in_dim.20), calls=%async_computation.1 | async-start | bytes 524288 | tf_op jit(solution)/shard_map/all_to_all | solution.py:394
  27.7 8.2 %collective-permute-start.1 = (s16[528,128]{1,0:T(8,128)(2,1)S(1)}, s16[528,128]{1,0:T(8,128)(2,1)S(1)}, u32[]{:S(2)}, u32[]{:S(2)}) collective-permute-start(s16[528,128]{1,0:T(8,128)(2,1)S(1)} %get-tuple-element.20), channel_id=1, source_target_pairs={{0,2},{1,3},{2,0},{3,1},{4,6},{5,7},{6,4},{7,5},{8,10},{9,11},{10,... | collective-permute-start | bytes 405512 | tf_op jit(solution)/shard_map/ppermute | solution.py:332
  35.9 1.5 %collective-permute-start.2 = (bf16[32,32,128]{2,1,0:T(8,128)(2,1)S(1)}, bf16[32,32,128]{2,1,0:T(8,128)(2,1)S(1)}, u32[]{:S(2)}, u32[]{:S(2)}) collective-permute-start(bf16[32,32,128]{2,1,0:T(8,128)(2,1)S(1)} %all-to-all-done.1.near_ref), channel_id=1, source_target_pairs={{0,1},{1,0},{2,3},{3,2},{4,5},{5,4},{6,7},{7,6},{8,9},{9,8},{10,11... | collective-permute-start | bytes 786440 | tf_op jit(solution)/shard_map/ppermute | solution.py:332
  42.1 10.2 %collective-permute-start.3 = (s16[528,128]{1,0:T(8,128)(2,1)S(1)}, s16[528,128]{1,0:T(8,128)(2,1)S(1)}, u32[]{:S(2)}, u32[]{:S(2)}) collective-permute-start(s16[528,128]{1,0:T(8,128)(2,1)S(1)} %get-tuple-element.24), channel_id=1, source_target_pairs={{0,64},{64,0},{128,192},{192,128},{1,65},{65,1},{129,193},{193,129... | collective-permute-start | bytes 405512 | tf_op jit(solution)/shard_map/ppermute | solution.py:332
  45.5 9.6 %collective-permute-start.6 = (s16[528,128]{1,0:T(8,128)(2,1)S(1)}, s16[528,128]{1,0:T(8,128)(2,1)S(1)}, u32[]{:S(2)}, u32[]{:S(2)}) collective-permute-start(s16[528,128]{1,0:T(8,128)(2,1)S(1)} %get-tuple-element.25), channel_id=1, source_target_pairs={{0,192},{64,128},{128,64},{192,0},{1,193},{65,129},{129,65},{193,1... | collective-permute-start | bytes 405512 | tf_op jit(solution)/shard_map/ppermute | solution.py:332
  52.5 14.5 %collective-permute-start.4 = (s16[528,128]{1,0:T(8,128)(2,1)S(1)}, s16[528,128]{1,0:T(8,128)(2,1)S(1)}, u32[]{:S(2)}, u32[]{:S(2)}) collective-permute-start(s16[528,128]{1,0:T(8,128)(2,1)S(1)} %shard_map.62.after_ref.own_ref), channel_id=1, source_target_pairs={{0,192},{64,128},{128,64},{192,0},{1,193},{65,129},{129,65},{193,1... | collective-permute-start | bytes 405512 | tf_op jit(solution)/shard_map/ppermute | solution.py:332
  55.2 13.4 %collective-permute-start.7 = (s16[528,128]{1,0:T(8,128)(2,1)S(1)}, s16[528,128]{1,0:T(8,128)(2,1)S(1)}, u32[]{:S(2)}, u32[]{:S(2)}) collective-permute-start(s16[528,128]{1,0:T(8,128)(2,1)S(1)} %shard_map.66.own_ref), channel_id=1, source_target_pairs={{0,64},{64,0},{128,192},{192,128},{1,65},{65,1},{129,193},{193,129... | collective-permute-start | bytes 405512 | tf_op jit(solution)/shard_map/ppermute | solution.py:332
  59.4 13.8 %all-to-all-start.2 = ((f32[16,32,128]{2,1,0:T(8,128)}), f32[16,32,128]{2,1,0:T(8,128)S(1)}, u32[]{:S(2)}, u32[]{:S(2)}) async-start(f32[16,32,128]{2,1,0:T(8,128)} %bitcast.11), calls=%async_computation.2 | async-start | bytes 524288 | tf_op jit(solution)/shard_map/all_to_all | solution.py:400
  67.1 6.9 %collective-permute-start.5 = (s16[528,128]{1,0:T(8,128)(2,1)S(1)}, s16[528,128]{1,0:T(8,128)(2,1)S(1)}, u32[]{:S(2)}, u32[]{:S(2)}) collective-permute-start(s16[528,128]{1,0:T(8,128)(2,1)S(1)} %shard_map.65.half0_ref), channel_id=1, source_target_pairs={{0,64},{64,0},{128,192},{192,128},{1,65},{65,1},{129,193},{193,129... | collective-permute-start | bytes 405512 | tf_op jit(solution)/shard_map/ppermute | solution.py:332
  68.7 8.2 %collective-permute-start.8 = (s16[528,128]{1,0:T(8,128)(2,1)S(1)}, s16[528,128]{1,0:T(8,128)(2,1)S(1)}, u32[]{:S(2)}, u32[]{:S(2)}) collective-permute-start(s16[528,128]{1,0:T(8,128)(2,1)S(1)} %shard_map.67.half1_ref), channel_id=1, source_target_pairs={{0,192},{64,128},{128,64},{192,0},{1,193},{65,129},{129,65},{193,1... | collective-permute-start | bytes 405512 | tf_op jit(solution)/shard_map/ppermute | solution.py:332
